TPU v7x, 32 devices: a whole 2x2x4 slice. The times are simulated.
32 devices in a mesh: dp: 8 (over z, core), mp: 4 (over y, x).
Axes of the slice: x: 2, y: 2, z: 4, core: 2. Of those that a mesh axis runs over, the one named last changes fastest.
Arguments:
- tokens: bfloat16 [20480, 1024], P('dp'), may hold values from -6 to 6
- lengths: int32 [8, 9], P('dp'), may hold values from 1 to 1024, 2560 in all within a row
- cotangent: bfloat16 [20480, 1024], P('dp'), may hold values from -6 to 6
- norm1_gain: float32 [1024], replicated, may hold values from 0.5 to 1.5
- norm1_bias: float32 [1024], replicated, may hold values from -3 to 3
- w_query: bfloat16 [1024, 1024], P(None, 'mp'), may hold values from -0.25 to 0.25
- w_key: bfloat16 [1024, 1024], P(None, 'mp'), may hold values from -0.25 to 0.25
- w_value: bfloat16 [1024, 1024], P(None, 'mp'), may hold values from -0.1875 to 0.1875
- w_output: bfloat16 [1024, 1024], P('mp'), may hold values from -0.75 to 0.75
- norm2_gain: float32 [1024], replicated, may hold values from 0.5 to 1.5
- norm2_bias: float32 [1024], replicated, may hold values from -3 to 3
- w_gate: bfloat16 [1024, 4096], P(None, 'mp'), may hold values from -0.1875 to 0.1875
- w_up: bfloat16 [1024, 4096], P(None, 'mp'), may hold values from -0.1875 to 0.1875
- w_down: bfloat16 [4096, 1024], P('mp'), may hold values from -0.1875 to 0.1875
Outputs:
- output: bfloat16 [20480, 1024], P(('dp', 'mp'))
- tokens_grad: bfloat16 [20480, 1024], P(('dp', 'mp'))
- query_grad: float32 [1024, 1024], P('dp', 'mp')
- key_grad: float32 [1024, 1024], P('dp', 'mp')
- value_grad: float32 [1024, 1024], P('dp', 'mp')
- output_proj_grad: float32 [1024, 1024], P('mp', 'dp')
- gate_grad: float32 [1024, 4096], P('dp', 'mp')
- up_grad: float32 [1024, 4096], P('dp', 'mp')
- down_grad: float32 [4096, 1024], P('mp', 'dp')
- norm1_gain_grad: float32 [1024], P('dp')
- norm1_bias_grad: float32 [1024], P('dp')
- norm2_gain_grad: float32 [1024], P('dp')
- norm2_bias_grad: float32 [1024], P('dp')
Inputs may be any that keep to these rules, and one draw needn't show every extreme that they name: Row i lists the lengths of 8 windows packed in order from the first row of pack i, then the number of padding rows at its end; each row sums to 2560 and its largest entry is exactly 1024.
All inputs are finite; a program needn't handle non-finite values.
Results may differ from a plain program's by a relative error of at most 0.025.
Values may be sent and summed in bfloat16 or wider, within the bound.
A program may use at most 256 MiB of HBM per device.

v0:
```python
import jax
import jax.numpy as jnp
from jax import lax
from jax.sharding import PartitionSpec as P

HD = 64


epsilon = 1e-05
rotary_base = 10000.0


def window_tables(lengths_row, rows_total, head_size):
    window_ends = jnp.cumsum(lengths_row)
    position = jnp.arange(rows_total, dtype=jnp.int32)
    passed = (position[:, None] >= window_ends[None, :]).astype(jnp.int32)
    segment = jnp.sum(passed, axis=1)
    window_start = jnp.sum(passed * lengths_row[None, :], axis=1)
    offset = (position - window_start).astype(jnp.float32)
    half_size = head_size // 2
    frequency = rotary_base ** (-2.0 * jnp.arange(half_size, dtype=jnp.float32) / head_size)
    angles = offset[:, None] * frequency[None, :]
    angles = jnp.concatenate([angles, angles], axis=1)
    return (segment, jnp.cos(angles), jnp.sin(angles))


def layer_stats(row_values, gain_vec, bias_vec):
    row_mean = jnp.mean(row_values, axis=-1, keepdims=True)
    centred = row_values - row_mean
    row_scale = lax.rsqrt(jnp.mean(centred * centred, axis=-1, keepdims=True) + epsilon)
    normed = centred * row_scale
    return (normed * gain_vec + bias_vec, normed, row_scale)


def layer_back(gradient, normed, row_scale, gain_vec):
    inner_grad = gradient * gain_vec
    centred_grad = inner_grad - jnp.mean(inner_grad, axis=-1, keepdims=True)
    return row_scale * (
        centred_grad - normed * jnp.mean(inner_grad * normed, axis=-1, keepdims=True)
    )


def rotate(field, cosine, sine_table, direction):
    row_count = field.shape[0]
    head_size = cosine.shape[1]
    pieces = field.reshape(row_count, field.shape[1] // head_size, head_size)
    half_size = head_size // 2
    turned = jnp.concatenate([-pieces[..., half_size:], pieces[..., :half_size]], axis=-1)
    result = pieces * cosine[:, None, :] + direction * turned * sine_table[:, None, :]
    return result.reshape(row_count, field.shape[1])


def block_scores(query_block, keys_split, segment_block, segment):
    scores = jnp.einsum(
        "qhd,khd->hqk", query_block, keys_split, preferred_element_type=jnp.float32
    ) * HD ** (-0.5)
    same_window = (segment_block[:, None] == segment[None, :])[None]
    return jnp.where(same_window, scores, -1e30)


def attend_forward(queries_rot, keys_rot, values, segment):
    row_count, feature_width = queries_rot.shape
    head_count = feature_width // HD
    block_rows = min(512, row_count)
    block_count = row_count // block_rows
    keys_split = keys_rot.reshape(row_count, head_count, HD)
    values_split = values.reshape(row_count, head_count, HD)

    def one_block(block_items):
        query_block, segment_block = block_items
        scores = block_scores(query_block, keys_split, segment_block, segment)
        row_top = jnp.max(scores, axis=-1, keepdims=True)
        exp_scores = jnp.exp(scores - row_top)
        row_total = jnp.sum(exp_scores, axis=-1, keepdims=True)
        attn_prob = (exp_scores / row_total).astype(jnp.bfloat16)
        mixed_block = jnp.einsum(
            "hqk,khd->qhd", attn_prob, values_split, preferred_element_type=jnp.float32
        )
        return (
            mixed_block.reshape(block_rows, feature_width),
            (row_top + jnp.log(row_total))[..., 0],
        )

    mixed_heads, log_totals = lax.map(
        one_block,
        (
            queries_rot.reshape(block_count, block_rows, head_count, HD),
            segment.reshape(block_count, block_rows),
        ),
    )
    return (mixed_heads.reshape(row_count, feature_width), log_totals)


def attend_backward(queries_rot, keys_rot, values, segment, log_totals, mixed_grad):
    row_count, feature_width = queries_rot.shape
    head_count = feature_width // HD
    block_rows = min(512, row_count)
    block_count = row_count // block_rows
    keys_split = keys_rot.reshape(row_count, head_count, HD)
    values_split = values.reshape(row_count, head_count, HD)
    scale_factor = HD ** (-0.5)

    def one_block(carried, block_items):
        keys_acc, values_acc = carried
        query_block, segment_block, log_block, grad_block = block_items
        scores = block_scores(query_block, keys_split, segment_block, segment)
        attn_prob = jnp.exp(scores - log_block[..., None])
        prob_grad = jnp.einsum(
            "qhd,khd->hqk", grad_block, values_split, preferred_element_type=jnp.float32
        )
        row_delta = jnp.sum(attn_prob * prob_grad, axis=-1, keepdims=True)
        score_grad = (attn_prob * (prob_grad - row_delta)).astype(jnp.bfloat16)
        values_acc = values_acc + jnp.einsum(
            "hqk,qhd->khd",
            attn_prob.astype(jnp.bfloat16),
            grad_block,
            preferred_element_type=jnp.float32,
        )
        keys_acc = (
            keys_acc
            + jnp.einsum(
                "hqk,qhd->khd", score_grad, query_block, preferred_element_type=jnp.float32
            )
            * scale_factor
        )
        query_grad = (
            jnp.einsum("hqk,khd->qhd", score_grad, keys_split, preferred_element_type=jnp.float32)
            * scale_factor
        )
        return ((keys_acc, values_acc), query_grad.reshape(block_rows, feature_width))

    zeros_acc = jnp.zeros((row_count, head_count, HD), jnp.float32)
    block_items = (
        queries_rot.reshape(block_count, block_rows, head_count, HD),
        segment.reshape(block_count, block_rows),
        log_totals,
        mixed_grad.reshape(block_count, block_rows, head_count, HD),
    )
    (keys_acc, values_acc), query_grads = lax.scan(one_block, (zeros_acc, zeros_acc), block_items)
    return (
        query_grads.reshape(row_count, feature_width),
        keys_acc.reshape(row_count, feature_width),
        values_acc.reshape(row_count, feature_width),
    )


def local(
    tokens,
    lengths,
    cotangent,
    norm1_gain,
    norm1_bias,
    w_query,
    w_key,
    w_value,
    w_output,
    norm2_gain,
    norm2_bias,
    w_gate,
    w_up,
    w_down,
):
    row_count = tokens.shape[0]
    segment, cosine, sine_table = window_tables(lengths[0], row_count, HD)
    live_rows = (segment < lengths.shape[1] - 1).astype(jnp.float32)
    share_rows = row_count // lax.axis_size("mp")
    own_start = lax.axis_index("mp") * share_rows
    tokens_f = tokens.astype(jnp.float32)
    out_grad = cotangent.astype(jnp.float32) * live_rows[:, None]
    normed_first, hat_first, scale_first = layer_stats(tokens_f, norm1_gain, norm1_bias)
    inputs_first = normed_first.astype(jnp.bfloat16)
    queries = jnp.dot(inputs_first, w_query, preferred_element_type=jnp.float32)
    keys_pre = jnp.dot(inputs_first, w_key, preferred_element_type=jnp.float32)
    values = jnp.dot(inputs_first, w_value, preferred_element_type=jnp.float32).astype(jnp.bfloat16)
    queries_rot = rotate(queries, cosine, sine_table, 1.0).astype(jnp.bfloat16)
    keys_rot = rotate(keys_pre, cosine, sine_table, 1.0).astype(jnp.bfloat16)
    mixed_heads, log_totals = attend_forward(queries_rot, keys_rot, values, segment)
    mixed_low = mixed_heads.astype(jnp.bfloat16)
    attn_partial = jnp.dot(mixed_low, w_output, preferred_element_type=jnp.float32)
    attn_rows = lax.psum_scatter(
        attn_partial.astype(jnp.bfloat16), "mp", scatter_dimension=0, tiled=True
    ).astype(jnp.float32)
    residual = lax.dynamic_slice_in_dim(tokens_f, own_start, share_rows, 0) + attn_rows
    normed_second, hat_second, scale_second = layer_stats(residual, norm2_gain, norm2_bias)
    inputs_second = lax.all_gather(normed_second.astype(jnp.bfloat16), "mp", axis=0, tiled=True)
    gate_pre = jnp.dot(inputs_second, w_gate, preferred_element_type=jnp.float32)
    up_proj = jnp.dot(inputs_second, w_up, preferred_element_type=jnp.float32)
    gate_sig = jax.nn.sigmoid(gate_pre)
    gate_act = gate_pre * gate_sig
    hidden = (gate_act * up_proj).astype(jnp.bfloat16)
    down_partial = jnp.dot(hidden, w_down, preferred_element_type=jnp.float32)
    output_own = residual + lax.psum_scatter(
        down_partial.astype(jnp.bfloat16), "mp", scatter_dimension=0, tiled=True
    ).astype(jnp.float32)
    down_in_grad = out_grad.astype(jnp.bfloat16)
    down_w_grad = jnp.dot(hidden.T, down_in_grad, preferred_element_type=jnp.float32)
    hidden_grad = jnp.dot(down_in_grad, w_down.T, preferred_element_type=jnp.float32)
    gate_in_grad = (hidden_grad * up_proj * gate_sig * (1.0 + gate_pre * (1.0 - gate_sig))).astype(
        jnp.bfloat16
    )
    up_in_grad = (hidden_grad * gate_act).astype(jnp.bfloat16)
    gate_w_grad = jnp.dot(inputs_second.T, gate_in_grad, preferred_element_type=jnp.float32)
    up_w_grad = jnp.dot(inputs_second.T, up_in_grad, preferred_element_type=jnp.float32)
    ffn_sums = (
        lax.psum_scatter(
            gate_w_grad.astype(jnp.bfloat16), "dp", scatter_dimension=0, tiled=True
        ).astype(jnp.float32),
        lax.psum_scatter(
            up_w_grad.astype(jnp.bfloat16), "dp", scatter_dimension=0, tiled=True
        ).astype(jnp.float32),
        lax.psum_scatter(
            down_w_grad.astype(jnp.bfloat16), "dp", scatter_dimension=1, tiled=True
        ).astype(jnp.float32),
    )
    second_partial = jnp.dot(gate_in_grad, w_gate.T, preferred_element_type=jnp.float32) + jnp.dot(
        up_in_grad, w_up.T, preferred_element_type=jnp.float32
    )
    second_grad = lax.psum_scatter(
        second_partial.astype(jnp.bfloat16), "mp", scatter_dimension=0, tiled=True
    ).astype(jnp.float32)
    own_out_grad = lax.dynamic_slice_in_dim(out_grad, own_start, share_rows, 0)
    residual_grad = own_out_grad + layer_back(second_grad, hat_second, scale_second, norm2_gain)
    attn_grad = lax.all_gather(residual_grad.astype(jnp.bfloat16), "mp", axis=0, tiled=True)
    gain_second_grad = jnp.sum(second_grad * hat_second, axis=0)
    bias_second_grad = jnp.sum(second_grad, axis=0)
    output_w_grad = jnp.dot(mixed_low.T, attn_grad, preferred_element_type=jnp.float32)
    mixed_grad = jnp.dot(attn_grad, w_output.T, preferred_element_type=jnp.float32).astype(
        jnp.bfloat16
    )
    query_rot_grad, key_rot_grad, value_acc_grad = attend_backward(
        queries_rot, keys_rot, values, segment, log_totals, mixed_grad
    )
    query_in_grad = rotate(query_rot_grad, cosine, sine_table, -1.0).astype(jnp.bfloat16)
    key_in_grad = rotate(key_rot_grad, cosine, sine_table, -1.0).astype(jnp.bfloat16)
    value_in_grad = value_acc_grad.astype(jnp.bfloat16)
    query_w_grad = jnp.dot(inputs_first.T, query_in_grad, preferred_element_type=jnp.float32)
    key_w_grad = jnp.dot(inputs_first.T, key_in_grad, preferred_element_type=jnp.float32)
    value_w_grad = jnp.dot(inputs_first.T, value_in_grad, preferred_element_type=jnp.float32)
    first_partial = jnp.dot(query_in_grad, w_query.T, preferred_element_type=jnp.float32)
    first_partial = first_partial + jnp.dot(
        key_in_grad, w_key.T, preferred_element_type=jnp.float32
    )
    first_partial = first_partial + jnp.dot(
        value_in_grad, w_value.T, preferred_element_type=jnp.float32
    )
    first_grad = lax.psum_scatter(
        first_partial.astype(jnp.bfloat16), "mp", scatter_dimension=0, tiled=True
    ).astype(jnp.float32)
    hat_own = lax.dynamic_slice_in_dim(hat_first, own_start, share_rows, 0)
    scale_own = lax.dynamic_slice_in_dim(scale_first, own_start, share_rows, 0)
    tokens_grad = (residual_grad + layer_back(first_grad, hat_own, scale_own, norm1_gain)).astype(
        jnp.bfloat16
    )
    gain_parts = lax.psum(
        (
            jnp.sum(first_grad * hat_own, axis=0),
            jnp.sum(first_grad, axis=0),
            gain_second_grad,
            bias_second_grad,
        ),
        "mp",
    )
    attn_sums = (
        lax.psum_scatter(
            query_w_grad.astype(jnp.bfloat16), "dp", scatter_dimension=0, tiled=True
        ).astype(jnp.float32),
        lax.psum_scatter(
            key_w_grad.astype(jnp.bfloat16), "dp", scatter_dimension=0, tiled=True
        ).astype(jnp.float32),
        lax.psum_scatter(
            value_w_grad.astype(jnp.bfloat16), "dp", scatter_dimension=0, tiled=True
        ).astype(jnp.float32),
        lax.psum_scatter(
            output_w_grad.astype(jnp.bfloat16), "dp", scatter_dimension=1, tiled=True
        ).astype(jnp.float32),
        lax.psum_scatter(
            gain_parts[0].astype(jnp.bfloat16), "dp", scatter_dimension=0, tiled=True
        ).astype(jnp.float32),
        lax.psum_scatter(
            gain_parts[1].astype(jnp.bfloat16), "dp", scatter_dimension=0, tiled=True
        ).astype(jnp.float32),
        lax.psum_scatter(
            gain_parts[2].astype(jnp.bfloat16), "dp", scatter_dimension=0, tiled=True
        ).astype(jnp.float32),
        lax.psum_scatter(
            gain_parts[3].astype(jnp.bfloat16), "dp", scatter_dimension=0, tiled=True
        ).astype(jnp.float32),
    )
    return (
        output_own.astype(jnp.bfloat16),
        tokens_grad,
        attn_sums[0],
        attn_sums[1],
        attn_sums[2],
        attn_sums[3],
        ffn_sums[0],
        ffn_sums[1],
        ffn_sums[2],
        attn_sums[4],
        attn_sums[5],
        attn_sums[6],
        attn_sums[7],
    )


def solution(mesh):
    return jax.shard_map(
        local,
        mesh=mesh,
        in_specs=(
            P("dp", None),
            P("dp", None),
            P("dp", None),
            P(),
            P(),
            P(None, "mp"),
            P(None, "mp"),
            P(None, "mp"),
            P("mp", None),
            P(),
            P(),
            P(None, "mp"),
            P(None, "mp"),
            P("mp", None),
        ),
        out_specs=(
            P(("dp", "mp"), None),
            P(("dp", "mp"), None),
            P("dp", "mp"),
            P("dp", "mp"),
            P("dp", "mp"),
            P("mp", "dp"),
            P("dp", "mp"),
            P("dp", "mp"),
            P("mp", "dp"),
            P("dp"),
            P("dp"),
            P("dp"),
            P("dp"),
        ),
        check_vma=False,
    )
```

profile of v0, /device:TPU:0, one launch (start us, length us, event | category | flops | bytes accessed | tf_op | source)
XLA Modules:
  0.0 1178.9 jit_solution(10888891391274027031)
XLA Ops:
  40.1 154.4 %while.27 = (s32[]{:T(128)}, bf16[5,512,256]{2,1,0:T(8,128)(2,1)}, f32[5,4,512]{2,1,0:T(4,128)}, s32[5,512]{1,0:T(8,128)S(1)}, s32[2560]{0:T(1024)S(1)}, /*index...) while((s32[]{:T(128)}, bf16[5,512,256]{2,1,0:T(8,128)(2,1)}, ...), condition=%wide.region_8.9_spmd, body=%wide.region_5.8_spmd.sunk | while | flops 1406400512 | bytes 156319888 | solution.py:84
  207.6 56.5 %reduce-scatter.16.cloned.1.call-done = bf16[640,1024]{1,0:T(8,128)(2,1)} async-done(((bf16[2560,1024]{1,0:T(8,128)(2,1)}), bf16[640,1024]{1,0:T(8,128)(2,1)}) %reduce-scatter.16.cloned.1.call-update) | async-done | bytes 1310736 | tf_op jit(solution)/shard_map/reduce_scatter | solution.py:180
  269.7 61.5 %all-gather.3.cloned.1.call-done = bf16[2560,1024]{1,0:T(8,128)(2,1)} async-done(((bf16[640,1024]{1,0:T(8,128)(2,1)}), bf16[2560,1024]{1,0:T(8,128)(2,1)}) %all-gather.3.cloned.1.call-update) | async-done | bytes 5242896 | tf_op jit(solution)/shard_map/all_gather | solution.py:185
  331.2 11.3 fusion.78
  350.8 19.2 %multiply_convert_fusion.1 = (bf16[2560,1024]{1,0:T(8,128)(2,1)}, bf16[2560,1024]{1,0:T(8,128)(2,1)}, bf16[2560,1024]{1,0:T(8,128)(2,1)}) fusion(f32[2560,1024]{1,0:T(8,128)} %fusion.77, f32[2560,1024]{1,0:T(8,128)} %fusion.78, bf16[1024,1024]{1,0:T(8,128)(2,1)S(1)} %copy-done, f32[2560]{0:T(1024)S(1)} %compare_convert_fusion, bf16[2560,1024]{1,0:T(8,128)(2,1)} %param.20), kind=kOutput, calls=%fused_computation.50 | convolution fusion | flops 5415895040 | bytes 44050432 | tf_op jit(solution)/shard_map/dot_general | solution.py:197
  403.3 44.4 %reduce-scatter.20.cloned.1.call-done = bf16[640,1024]{1,0:T(8,128)(2,1)} async-done(((bf16[2560,1024]{1,0:T(8,128)(2,1)}), bf16[640,1024]{1,0:T(8,128)(2,1)}) %reduce-scatter.20.cloned.1.call-update) | async-done | bytes 1310736 | tf_op jit(solution)/shard_map/reduce_scatter | solution.py:218
  451.7 60.3 %reduce-scatter.18.cloned.1.call-done = bf16[640,1024]{1,0:T(8,128)(2,1)} async-done(((bf16[2560,1024]{1,0:T(8,128)(2,1)}), bf16[640,1024]{1,0:T(8,128)(2,1)}) %reduce-scatter.18.cloned.1.call-update) | async-done | bytes 1310736 | tf_op jit(solution)/shard_map/reduce_scatter | solution.py:192
  549.9 28.7 %all-gather.5.cloned.1.call-done = bf16[2560,1024]{1,0:T(8,128)(2,1)} async-done(((bf16[640,1024]{1,0:T(8,128)(2,1)}), bf16[2560,1024]{1,0:T(8,128)(2,1)}) %all-gather.5.cloned.1.call-update) | async-done | bytes 5242896 | tf_op jit(solution)/shard_map/all_gather | solution.py:223
  589.6 335.2 %while.28 = (s32[]{:T(128)}, f32[2560,4,64]{0,2,1:T(8,128)}, f32[2560,4,64]{0,2,1:T(8,128)}, f32[5,512,256]{1,2,0:T(8,128)}, bf16[5,512,4,64]{1,3,2,0:T(8,128)(2...) while((s32[]{:T(128)}, f32[2560,4,64]{0,2,1:T(8,128)}, ...), condition=%wide.region_18.19_spmd.clone, body=%wide.region_16.18_spmd.clone.sunk | while | flops 3438802944 | bytes 179642544 | solution.py:139
  592.0 11.5 fusion.160
  614.7 15.5 %multiply_reduce_fusion.4 = (f32[4,512]{1,0:T(4,128)S(1)}, f32[4,512,2560]{2,1,0:T(8,128)}) fusion(f32[4,512,2560]{2,1,0:T(8,128)} %fusion.160, f32[4,512]{1,0:T(4,128)S(1)} %dynamic-slice_bitcast_fusion.2, pred[512,2560]{1,0:T(8,128)(4,1)S(1)} %broadcast_compare_fusion.5, bf16[2560,4,64]{0,2,1:T(8,128)(2,1)} %get-tuple-element.508, ...), kind=kOutput, calls=%fused_computation.17.clone.1 | convolution fusion | flops 697300992 | bytes 44843012 | tf_op jit(solution)/shard_map/while/body/eval_jaxpr/qhd,khd->hqk/dot_general | solution.py:108
  630.2 16.0 %multiply_convert_fusion.5 = bf16[4,512,2560]{2,1,0:T(8,128)(2,1)S(1)} fusion(f32[4,512,2560]{2,1,0:T(8,128)} %get-tuple-element.443, f32[4,512,2560]{2,1,0:T(8,128)} %fusion.160, f32[4,512]{1,0:T(4,128)S(1)} %get-tuple-element.444, f32[4,512]{1,0:T(4,128)S(1)} %dynamic-slice_bitcast_fusion.2, pred[512,2560]{1,0:T(8,128)(4,1)S(1)} %broadcast_compare_fusion.5), kind=kLoop, calls=%fused_computation.16.clone.1 | loop fusion | flops 31457280 | bytes 53755904 | tf_op jit(solution)/shard_map/while/body/eval_jaxpr/convert_element_type | solution.py:112
  658.2 11.4 fusion.160
  669.6 11.9 %fusion.162 = f32[2560,4,64]{0,2,1:T(8,128)} fusion(f32[4,512,2560]{2,1,0:T(8,128)} %fusion.160, f32[4,512]{1,0:T(4,128)S(1)} %dynamic-slice_bitcast_fusion.2, pred[512,2560]{1,0:T(8,128)(4,1)S(1)} %broadcast_compare_fusion.5, f32[2560,4,64]{0,2,1:T(8,128)} %get-tuple-element.487, pred[]{:T(512)S(6)} %compare.3, ...), kind=kOutput, calls=%fused_computation.26.clone.1 | convolution fusion | flops 693370880 | bytes 27795460 | tf_op jit(solution)/shard_map/while/body/eval_jaxpr/hqk,qhd->khd/dot_general | solution.py:113
  681.5 15.6 %multiply_reduce_fusion.4 = (f32[4,512]{1,0:T(4,128)S(1)}, f32[4,512,2560]{2,1,0:T(8,128)}) fusion(f32[4,512,2560]{2,1,0:T(8,128)} %fusion.160, f32[4,512]{1,0:T(4,128)S(1)} %dynamic-slice_bitcast_fusion.2, pred[512,2560]{1,0:T(8,128)(4,1)S(1)} %broadcast_compare_fusion.5, bf16[2560,4,64]{0,2,1:T(8,128)(2,1)} %get-tuple-element.508, ...), kind=kOutput, calls=%fused_computation.17.clone.1 | convolution fusion | flops 697300992 | bytes 44843012 | tf_op jit(solution)/shard_map/while/body/eval_jaxpr/qhd,khd->hqk/dot_general | solution.py:108
  697.1 15.7 %multiply_convert_fusion.5 = bf16[4,512,2560]{2,1,0:T(8,128)(2,1)S(1)} fusion(f32[4,512,2560]{2,1,0:T(8,128)} %get-tuple-element.443, f32[4,512,2560]{2,1,0:T(8,128)} %fusion.160, f32[4,512]{1,0:T(4,128)S(1)} %get-tuple-element.444, f32[4,512]{1,0:T(4,128)S(1)} %dynamic-slice_bitcast_fusion.2, pred[512,2560]{1,0:T(8,128)(4,1)S(1)} %broadcast_compare_fusion.5), kind=kLoop, calls=%fused_computation.16.clone.1 | loop fusion | flops 31457280 | bytes 53755904 | tf_op jit(solution)/shard_map/while/body/eval_jaxpr/convert_element_type | solution.py:112
  725.7 11.3 fusion.160
  737.0 11.7 fusion.162
  748.7 15.5 %multiply_reduce_fusion.4 = (f32[4,512]{1,0:T(4,128)S(1)}, f32[4,512,2560]{2,1,0:T(8,128)}) fusion(f32[4,512,2560]{2,1,0:T(8,128)} %fusion.160, f32[4,512]{1,0:T(4,128)S(1)} %dynamic-slice_bitcast_fusion.2, pred[512,2560]{1,0:T(8,128)(4,1)S(1)} %broadcast_compare_fusion.5, bf16[2560,4,64]{0,2,1:T(8,128)(2,1)} %get-tuple-element.508, ...), kind=kOutput, calls=%fused_computation.17.clone.1 | convolution fusion | flops 697300992 | bytes 44843012 | tf_op jit(solution)/shard_map/while/body/eval_jaxpr/qhd,khd->hqk/dot_general | solution.py:108
  764.2 15.7 %multiply_convert_fusion.5 = bf16[4,512,2560]{2,1,0:T(8,128)(2,1)S(1)} fusion(f32[4,512,2560]{2,1,0:T(8,128)} %get-tuple-element.443, f32[4,512,2560]{2,1,0:T(8,128)} %fusion.160, f32[4,512]{1,0:T(4,128)S(1)} %get-tuple-element.444, f32[4,512]{1,0:T(4,128)S(1)} %dynamic-slice_bitcast_fusion.2, pred[512,2560]{1,0:T(8,128)(4,1)S(1)} %broadcast_compare_fusion.5), kind=kLoop, calls=%fused_computation.16.clone.1 | loop fusion | flops 31457280 | bytes 53755904 | tf_op jit(solution)/shard_map/while/body/eval_jaxpr/convert_element_type | solution.py:112
  804.0 11.7 fusion.162
  815.8 15.5 %multiply_reduce_fusion.4 = (f32[4,512]{1,0:T(4,128)S(1)}, f32[4,512,2560]{2,1,0:T(8,128)}) fusion(f32[4,512,2560]{2,1,0:T(8,128)} %fusion.160, f32[4,512]{1,0:T(4,128)S(1)} %dynamic-slice_bitcast_fusion.2, pred[512,2560]{1,0:T(8,128)(4,1)S(1)} %broadcast_compare_fusion.5, bf16[2560,4,64]{0,2,1:T(8,128)(2,1)} %get-tuple-element.508, ...), kind=kOutput, calls=%fused_computation.17.clone.1 | convolution fusion | flops 697300992 | bytes 44843012 | tf_op jit(solution)/shard_map/while/body/eval_jaxpr/qhd,khd->hqk/dot_general | solution.py:108
  831.2 15.7 %multiply_convert_fusion.5 = bf16[4,512,2560]{2,1,0:T(8,128)(2,1)S(1)} fusion(f32[4,512,2560]{2,1,0:T(8,128)} %get-tuple-element.443, f32[4,512,2560]{2,1,0:T(8,128)} %fusion.160, f32[4,512]{1,0:T(4,128)S(1)} %get-tuple-element.444, f32[4,512]{1,0:T(4,128)S(1)} %dynamic-slice_bitcast_fusion.2, pred[512,2560]{1,0:T(8,128)(4,1)S(1)} %broadcast_compare_fusion.5), kind=kLoop, calls=%fused_computation.16.clone.1 | loop fusion | flops 31457280 | bytes 53755904 | tf_op jit(solution)/shard_map/while/body/eval_jaxpr/convert_element_type | solution.py:112
  859.8 11.3 fusion.160
  871.1 11.7 fusion.162
  882.8 15.5 %multiply_reduce_fusion.4 = (f32[4,512]{1,0:T(4,128)S(1)}, f32[4,512,2560]{2,1,0:T(8,128)}) fusion(f32[4,512,2560]{2,1,0:T(8,128)} %fusion.160, f32[4,512]{1,0:T(4,128)S(1)} %dynamic-slice_bitcast_fusion.2, pred[512,2560]{1,0:T(8,128)(4,1)S(1)} %broadcast_compare_fusion.5, bf16[2560,4,64]{0,2,1:T(8,128)(2,1)} %get-tuple-element.508, ...), kind=kOutput, calls=%fused_computation.17.clone.1 | convolution fusion | flops 697300992 | bytes 44843012 | tf_op jit(solution)/shard_map/while/body/eval_jaxpr/qhd,khd->hqk/dot_general | solution.py:108
  898.3 15.7 %multiply_convert_fusion.5 = bf16[4,512,2560]{2,1,0:T(8,128)(2,1)S(1)} fusion(f32[4,512,2560]{2,1,0:T(8,128)} %get-tuple-element.443, f32[4,512,2560]{2,1,0:T(8,128)} %fusion.160, f32[4,512]{1,0:T(4,128)S(1)} %get-tuple-element.444, f32[4,512]{1,0:T(4,128)S(1)} %dynamic-slice_bitcast_fusion.2, pred[512,2560]{1,0:T(8,128)(4,1)S(1)} %broadcast_compare_fusion.5), kind=kLoop, calls=%fused_computation.16.clone.1 | loop fusion | flops 31457280 | bytes 53755904 | tf_op jit(solution)/shard_map/while/body/eval_jaxpr/convert_element_type | solution.py:112
  1008.6 29.9 %reduce-scatter.26.cloned.1.call-done = bf16[128,256]{1,0:T(8,128)(2,1)} async-done(((bf16[1024,256]{1,0:T(8,128)(2,1)}), bf16[128,256]{1,0:T(8,128)(2,1)}) %reduce-scatter.26.cloned.1.call-update) | async-done | bytes 65552 | tf_op jit(solution)/shard_map/reduce_scatter | solution.py:267
  1040.0 30.4 %reduce-scatter.24.cloned.1.call-done = bf16[128,256]{1,0:T(8,128)(2,1)} async-done(((bf16[1024,256]{1,0:T(8,128)(2,1)}), bf16[128,256]{1,0:T(8,128)(2,1)}) %reduce-scatter.24.cloned.1.call-update) | async-done | bytes 65552 | tf_op jit(solution)/shard_map/reduce_scatter | solution.py:264
  1071.9 61.2 %reduce-scatter.22.cloned.1.call-done = bf16[640,1024]{1,0:T(8,128)(2,1)} async-done(((bf16[2560,1024]{1,0:T(8,128)(2,1)}), bf16[640,1024]{1,0:T(8,128)(2,1)}) %reduce-scatter.22.cloned.1.call-update) | async-done | bytes 1310736 | tf_op jit(solution)/shard_map/reduce_scatter | solution.py:246
  1136.3 15.0 %all-reduce.4 = (bf16[1024]{0:T(1024)(128)(2,1)S(1)}, bf16[1024]{0:T(1024)(128)(2,1)S(1)}, bf16[1024]{0:T(1024)(128)(2,1)S(1)}, bf16[1024]{0:T(1024)(128)(2,1)S(1)}) all-reduce(f32[1024]{0:T(1024)S(1)} %get-tuple-element.232, f32[1024]{0:T(1024)S(1)} %get-tuple-element.239, ...), channel_id=1, replica_groups=mesh['dp'=8,'mp'=4] {'mp'}, use_global_device_ids=true, to_apply=%region_30.31 | all-reduce | flops 4096 | bytes 24576 | tf_op jit(solution)/shard_map/psum | solution.py:254
  1151.3 13.8 %all-reduce.5 = (bf16[1024]{0:T(1024)(128)(2,1)S(1)}, bf16[1024]{0:T(1024)(128)(2,1)S(1)}, bf16[1024]{0:T(1024)(128)(2,1)S(1)}, bf16[1024]{0:T(1024)(128)(2,1)S(1)}) all-reduce(bf16[1024]{0:T(1024)(128)(2,1)S(1)} %get-tuple-element.280, bf16[1024]{0:T(1024)(128)(2,1)S(1)} %get-tuple-element.281, ...), channel_id=13, replica_groups=mesh['dp'=8,'mp'=4] {'dp'}, use_global_device_ids=true, to_apply=%region_31.32.clone | all-reduce | flops 4096 | bytes 16384
  (268 shorter events, 481.1 us)
Async XLA Ops:
  7.2 343.6 %copy-start = (bf16[1024,1024]{1,0:T(8,128)(2,1)S(1)}, bf16[1024,1024]{1,0:T(8,128)(2,1)}, u32[]{:S(2)}) copy-start(bf16[1024,1024]{1,0:T(8,128)(2,1)} %param.31) | copy-start | bytes 6291460
  7.2 256.9 %reduce-scatter.16.cloned.1.call-start = ((), (), s32[]{:S(2)}) async-start(), calls=%async_computation.11 | async-start | bytes 6553600 | tf_op jit(solution)/shard_map/reduce_scatter | solution.py:180
  13.8 11.3 copy-start.22
  17.3 14.9 %copy-start.6 = (f32[2560,64]{0,1:T(8,128)}, f32[2560,64]{0,1:T(8,128)S(1)}, u32[]{:S(2)}) copy-start(f32[2560,64]{0,1:T(8,128)S(1)} %get-tuple-element.318) | copy-start | bytes 1966084
  17.3 7.9 copy-start.20
  40.1 154.4 %copy-start.14 = (bf16[256,1024]{1,0:T(8,128)(2,1)S(1)}, bf16[256,1024]{1,0:T(8,128)(2,1)}, u32[]{:S(2)}) copy-start(bf16[256,1024]{1,0:T(8,128)(2,1)} %param.26) | copy-start | bytes 1572868
  47.0 7.0 copy-start.2
  77.8 7.0 copy-start.2
  139.4 7.0 copy-start.2
  199.8 131.4 %all-gather.3.cloned.1.call-start = ((), (), s32[]{:S(2)}) async-start(), calls=%async_computation.12 | async-start | bytes 6553600 | tf_op jit(solution)/shard_map/all_gather | solution.py:185
  269.6 178.1 %reduce-scatter.20.cloned.1.call-start = ((), (), s32[]{:S(2)}) async-start(), calls=%async_computation.14 | async-start | bytes 6553600 | tf_op jit(solution)/shard_map/reduce_scatter | solution.py:218
  331.2 11.3 copy-start.31
  331.2 11.3 copy-start.32
  370.0 8.6 copy-start.33
  370.0 8.6 copy-start.35
  386.1 125.9 %reduce-scatter.18.cloned.1.call-start = ((), (), s32[]{:S(2)}) async-start(), calls=%async_computation.13 | async-start | bytes 6553600 | tf_op jit(solution)/shard_map/reduce_scatter | solution.py:192
  396.1 182.5 %all-gather.5.cloned.1.call-start = ((), (), s32[]{:S(2)}) async-start(), calls=%async_computation.15 | async-start | bytes 6553600 | tf_op jit(solution)/shard_map/all_gather | solution.py:223
  447.7 64.3 %copy-start.10 = (bf16[640,1024]{1,0:T(8,128)(2,1)S(1)}, bf16[640,1024]{1,0:T(8,128)(2,1)}, u32[]{:S(2)}) copy-start(bf16[640,1024]{1,0:T(8,128)(2,1)} %reduce-scatter.20.cloned.1.call-done) | copy-start | bytes 3932164
  517.0 481.6 %reduce-scatter.36.cloned.1.call-start = ((), (), s32[]{:S(2)}) async-start(), calls=%async_computation.23 | async-start | bytes 2359296
  529.4 471.3 %reduce-scatter.32.cloned.1.call-start = ((), (), s32[]{:S(2)}) async-start(), calls=%async_computation.21 | async-start | bytes 2359296 | tf_op jit(solution)/shard_map/reduce_scatter | solution.py:208
  539.6 462.8 %reduce-scatter.30.cloned.1.call-start = ((), (), s32[]{:S(2)}) async-start(), calls=%async_computation.20 | async-start | bytes 2359296 | tf_op jit(solution)/shard_map/reduce_scatter | solution.py:205
  539.7 38.9 %copy-start.15 = (bf16[256,1024]{1,0:T(8,128)(2,1)S(1)}, bf16[256,1024]{1,0:T(8,128)(2,1)}, u32[]{:S(2)}) copy-start(bf16[256,1024]{1,0:T(8,128)(2,1)} %param.26) | copy-start | bytes 1572868
  549.9 454.3 %reduce-scatter.34.cloned.1.call-start = ((), (), s32[]{:S(2)}) async-start(), calls=%async_computation.22 | async-start | bytes 589824
  932.4 12.2 %copy-start.12 = (bf16[2560,4,64]{0,2,1:T(8,128)(2,1)}, bf16[2560,4,64]{0,2,1:T(8,128)(2,1)S(1)}, u32[]{:S(2)}) copy-start(bf16[2560,4,64]{0,2,1:T(8,128)(2,1)S(1)} %convert_element_type.210) | copy-start | bytes 3932164
  944.5 62.5 %reduce-scatter.28.cloned.1.call-start = ((), (), s32[]{:S(2)}) async-start(), calls=%async_computation.19 | async-start | bytes 589824 | tf_op jit(solution)/shard_map/reduce_scatter | solution.py:270
  959.5 79.0 %reduce-scatter.26.cloned.1.call-start = ((), (), s32[]{:S(2)}) async-start(), calls=%async_computation.18 | async-start | bytes 589824 | tf_op jit(solution)/shard_map/reduce_scatter | solution.py:267
  974.8 95.6 %reduce-scatter.24.cloned.1.call-start = ((), (), s32[]{:S(2)}) async-start(), calls=%async_computation.17 | async-start | bytes 589824 | tf_op jit(solution)/shard_map/reduce_scatter | solution.py:264
  985.4 147.7 %reduce-scatter.22.cloned.1.call-start = ((), (), s32[]{:S(2)}) async-start(), calls=%async_computation.16 | async-start | bytes 6553600 | tf_op jit(solution)/shard_map/reduce_scatter | solution.py:246
  996.6 136.6 %copy-start.24 = (f32[1024]{0:T(1024)S(1)}, f32[1024]{0:T(1024)}, u32[]{:S(2)}) copy-start(f32[1024]{0:T(1024)} %param.21) | copy-start | bytes 12292
  1004.2 132.0 %copy-start.26 = (f32[1024]{0:T(1024)S(1)}, f32[1024]{0:T(1024)}, u32[]{:S(2)}) copy-start(f32[1024]{0:T(1024)} %get-tuple-element.234) | copy-start | bytes 12292
  1004.2 132.1 %copy-start.27 = (f32[1024]{0:T(1024)S(1)}, f32[1024]{0:T(1024)}, u32[]{:S(2)}) copy-start(f32[1024]{0:T(1024)} %get-tuple-element.238) | copy-start | bytes 12292
  1133.2 34.3 %copy-start.11 = (bf16[640,1024]{1,0:T(8,128)(2,1)S(1)}, bf16[640,1024]{1,0:T(8,128)(2,1)}, u32[]{:S(2)}) copy-start(bf16[640,1024]{1,0:T(8,128)(2,1)} %reduce-scatter.22.cloned.1.call-done) | copy-start | bytes 3932164
  (21 other events, 76.1 us)
Sparse Core Ops, SparseCore 0:
  199.9 64.1 reduce-scatter.15
  269.8 61.4 all-gather.2
  386.3 61.4 reduce-scatter.19
  450.6 61.4 reduce-scatter.17
  517.1 61.4 all-gather.4
  580.7 35.7 reduce-scatter.35
  618.9 34.3 reduce-scatter.31
  655.6 34.3 reduce-scatter.29
  944.7 31.0 reduce-scatter.33
  977.9 29.0 reduce-scatter.27
  1009.3 29.1 reduce-scatter.25
  1041.3 29.0 reduce-scatter.23
  1073.4 59.6 reduce-scatter.21
where the time goes:
time: 1190 us; the launch traced here: 1180 us
  matrix products  471 us (40%)
  waiting for transfers between devices  374 us (31%)
  other arithmetic  200 us (17%)
  local copies, waits for them, and re-layouts  87.4 us (7%)
  blocking collectives  28.9 us (2%)
  between operations  15.5 us (1%)
    dot_general x10, matrix products, block_scores(): jnp.einsum('qhd,khd->hqk', query_block, keys_split, preferred_element_typ...  84.6 us
    convert_element_type x5, other arithmetic, one_block(): score_grad = (attn_prob * (prob_grad - row_delta)).astype(jnp.bfloat16)  78.8 us
    dot_general x5, matrix products, one_block(): jnp.einsum('qhd,khd->hqk', grad_block, values_split, preferred_element_ty...  77.5 us
    all_gather x1, waiting for transfers between devices, local(): lax.all_gather(normed_second.astype(jnp.bfloat16), 'mp', axis=0, tiled=True)  61.5 us
    reduce_scatter x1, waiting for transfers between devices, local(): lax.psum_scatter(first_partial.astype(jnp.bfloat16), 'mp', scatter_dimens...  61.2 us
    reduce_scatter x1, waiting for transfers between devices, local(): lax.psum_scatter(down_partial.astype(jnp.bfloat16), 'mp', scatter_dimensi...  60.3 us
    dot_general x5, matrix products, one_block(): jnp.einsum('hqk,qhd->khd', attn_prob.astype(jnp.bfloat16), grad_block, pr...  58.2 us
    reduce_scatter x1, waiting for transfers between devices, local(): lax.psum_scatter(attn_partial.astype(jnp.bfloat16), 'mp', scatter_dimensi...  56.5 us
  transfers between devices with their start and end apart: 13, of which 9 were waited for; matrix products, arithmetic and copies ran while one was open for 42% of the time, Pallas kernels for 0%

commit v1 on v0

v1 whole, which is shorter than its diff:
```python
import functools
import math

import jax
import jax.numpy as jnp
import numpy as np
from jax import lax
from jax.experimental import pallas as pl
from jax.experimental.pallas import tpu as pltpu
from jax.sharding import PartitionSpec as P

HD = 64
HALF = HD // 2
PAIR = 2 * HD
QB = 128
KB = 256
EPS = 1e-05
BASE = 10000.0
NEG = -1e30
MOST = 1024
SCALE = HD**-0.5
VMEM = pl.BlockSpec(memory_space=pltpu.VMEM)
SMEM = pl.BlockSpec(memory_space=pltpu.SMEM)
ANY = pl.BlockSpec(memory_space=pl.ANY)
MESH = pl.DeviceIdType.MESH
STEPS = 5
EARLY = 2
PIECES = 4
DIRECT = 1
VMEM_CAP = 62 << 20
F32 = jnp.float32
BF16 = jnp.bfloat16


def mm(a, b):
    return jnp.dot(a, b, preferred_element_type=F32)


def mm_nt(a, b):
    return lax.dot_general(a, b, (((1,), (1,)), ((), ())), preferred_element_type=F32)


def mm_tn(a, b):
    return lax.dot_general(a, b, (((0,), (0,)), ((), ())), preferred_element_type=F32)


def window_bounds(len_ref, position):
    entries = len_ref.shape[1]
    start = jnp.zeros_like(position)
    end = jnp.zeros_like(position)
    edge = jnp.int32(0)
    for entry in range(entries):
        size = len_ref[0, entry]
        inside = position >= edge
        start = jnp.where(inside, edge, start)
        edge = edge + size
        end = jnp.where(inside, edge, end)
    return start, end


def norm_rows(rows):
    mean = jnp.mean(rows, axis=-1, keepdims=True)
    centred = rows - mean
    scale = lax.rsqrt(jnp.mean(centred * centred, axis=-1, keepdims=True) + EPS)
    return centred * scale, scale


def rotate_t(field, cosine, sine, direction):
    parts = []
    for head in range(field.shape[0] // HD):
        first = field[head * HD : head * HD + HALF]
        second = field[head * HD + HALF : (head + 1) * HD]
        parts.append(first * cosine - direction * (second * sine))
        parts.append(second * cosine + direction * (first * sine))
    return jnp.concatenate(parts, axis=0)


def qkv_kernel(
    len_ref, tok_ref, gain_ref, bias_ref, freq_ref, wq_ref, wk_ref, wv_ref,
    a1_ref, k_ref, v_ref, qt_ref, kt_ref, vt_ref, cos_ref, sin_ref,
):
    rows = tok_ref.shape[0]
    position = lax.broadcasted_iota(jnp.int32, (1, rows), 1) + pl.program_id(0) * rows
    start, _ = window_bounds(len_ref, position)
    offset = (position - start).astype(F32)
    theta = freq_ref[...] * offset
    cosine, sine = jnp.cos(theta), jnp.sin(theta)
    cos_ref[...] = cosine
    sin_ref[...] = sine
    hat, _ = norm_rows(tok_ref[...].astype(F32))
    a1 = (hat * gain_ref[...] + bias_ref[...]).astype(BF16)
    a1_ref[...] = a1
    for w_ref, out_ref, out_t_ref, scale in (
        (wq_ref, None, qt_ref, SCALE),
        (wk_ref, k_ref, kt_ref, None),
    ):
        field = rotate_t(mm(a1, w_ref[...]).T, cosine, sine, 1.0).astype(BF16)
        if scale is not None:
            field = field * jnp.asarray(scale, BF16)
        out_t_ref[...] = field
        if out_ref is not None:
            out_ref[...] = field.T
    values = mm(a1, wv_ref[...]).astype(BF16)
    v_ref[...] = values
    vt_ref[...] = values.T


def project(lengths, tokens, gain, bias, wq, wk, wv):
    rows, width = tokens.shape
    feats = wq.shape[1]
    block = min(512, rows)
    freq = np.float32(BASE) ** (np.float32(-2.0 / HD) * np.arange(HALF, dtype=np.float32))
    freq = jnp.asarray(freq[:, None], F32)
    whole = lambda a: pl.BlockSpec(a.shape, lambda i: (0, 0))
    by_row = lambda cols: pl.BlockSpec((block, cols), lambda i: (i, 0))
    by_col = lambda size: pl.BlockSpec((size, block), lambda i: (0, i))
    nat = jax.ShapeDtypeStruct((rows, feats), BF16)
    trans = jax.ShapeDtypeStruct((feats, rows), BF16)
    table = jax.ShapeDtypeStruct((HALF, rows), F32)
    return pl.pallas_call(
        qkv_kernel,
        grid=(rows // block,),
        in_specs=[SMEM, by_row(width)] + [whole(a) for a in (gain, bias, freq, wq, wk, wv)],
        out_specs=[by_row(width)] + [by_row(feats)] * 2 + [by_col(feats)] * 3 + [by_col(HALF)] * 2,
        out_shape=[jax.ShapeDtypeStruct((rows, width), BF16)] + [nat] * 2 + [trans] * 3 + [table] * 2,
        compiler_params=pltpu.CompilerParams(vmem_limit_bytes=VMEM_CAP),
        cost_estimate=pl.CostEstimate(
            flops=6 * rows * width * feats, bytes_accessed=rows * width * 8, transcendentals=0
        ),
        name="qkv",
    )(lengths, tokens, gain, bias, freq, wq, wk, wv)


def block_diagonal_t(pair):
    head = lax.broadcasted_iota(jnp.int32, pair.shape, 0) < HD
    zero = jnp.zeros_like(pair)
    return jnp.concatenate([jnp.where(head, pair, zero), jnp.where(head, zero, pair)], axis=1)


def diagonal_blocks(product):
    return jnp.concatenate([product[:HD, :QB], product[HD:, QB:]], axis=1)


def key_range(len_ref, first):
    low, _ = window_bounds(len_ref, first)
    _, high = window_bounds(len_ref, first + (QB - 1))
    base = low // QB * QB
    return base, (high - base + (KB - 1)) // KB


def key_rows(at, rows):
    return pl.ds(pl.multiple_of(jnp.clip(at, 0, rows - KB), QB), KB)


def inside_window(start, end, at, rows):
    shift = jnp.minimum(at, rows - KB)
    key = lax.broadcasted_iota(jnp.int32, (KB, QB), 0)
    inside = (key >= jnp.maximum(start, at) - shift) & (key < end - shift)
    return jnp.concatenate([inside, inside], axis=1)


def fill_schedule(len_ref, sched, blocks, index_of, rows):
    def nothing(n):
        sched[0, n] = 0
        sched[1, n] = rows

    def one_query(turn, n):
        base, count = key_range(len_ref, index_of(turn) * QB)

        def one_key(kb, _):
            sched[0, n + kb] = turn
            sched[1, n + kb] = base + kb * KB
            return 0

        lax.fori_loop(0, count, one_key, 0)
        return n + count

    nothing(0)
    n = lax.fori_loop(0, blocks, one_query, jnp.int32(1))
    for extra in range(3):
        nothing(n + extra)
    return n - 1


def store_window(len_ref, window, turn, first):
    position = lax.broadcasted_iota(jnp.int32, (1, QB), 1) + first
    window[turn, 0:1], window[turn, 1:2] = window_bounds(len_ref, position)


def run_pipeline(count, scores, soften, mix):
    def two_pairs(turn, _):
        n = 1 + 2 * turn
        mix(n - 1, 1)
        scores(n + 1, 1)
        soften(n, 0)
        mix(n, 0)
        scores(n + 2, 0)
        soften(n + 1, 1)
        return 0

    turns = (count + 1) // 2
    scores(1, 0)
    lax.fori_loop(0, turns, two_pairs, 0)
    mix(2 * turns, 1)


def attend_kernel(begin, steps, len_ref, qt_ref, k_ref, vt_ref, *rest):
    if begin > 0:
        ot_before, lse_before, *rest = rest
    o_ref, ot_ref, lse_ref, sched, window, diag, stat, acc, keep_buf, score_buf, prob_buf = rest
    if begin > 0:
        ot_ref[...] = ot_before[...]
        lse_ref[...] = lse_before[...]
    owners, taken = o_ref.shape[:2]
    feats, rows = qt_ref.shape
    pairs = range(feats // PAIR)
    feat = [pl.ds(p * PAIR, PAIR) for p in pairs]

    def index_of(turn):
        return turn // taken * steps + begin + lax.rem(turn, taken)

    def prepare(turn, _):
        first = index_of(turn) * QB
        cols = pl.ds(pl.multiple_of(first, QB), QB)
        store_window(len_ref, window, turn, first)
        for p in pairs:
            diag[turn, p] = block_diagonal_t(qt_ref[feat[p], cols])
            stat[turn, p : p + 1] = jnp.full((1, 2 * QB), NEG, F32)
            stat[turn, 4 + p : 5 + p] = jnp.zeros((1, 2 * QB), F32)
            acc[turn, p] = jnp.zeros((HD, 2 * QB), F32)
        return 0

    lax.fori_loop(0, owners * taken, prepare, 0)
    count = fill_schedule(len_ref, sched, owners * taken, index_of, rows)

    def scores(n, buf):
        turn, keys = sched[0, n], key_rows(sched[1, n], rows)
        for p in pairs:
            score_buf[buf, p] = mm(k_ref[keys, feat[p]], diag[turn, p])

    def soften(n, buf):
        turn = sched[0, n]
        inside = inside_window(window[turn, 0:1], window[turn, 1:2], sched[1, n], rows)
        for p in pairs:
            top, total = stat[turn, p : p + 1], stat[turn, 4 + p : 5 + p]
            values = jnp.where(inside, score_buf[buf, p], NEG)
            new_top = jnp.maximum(top, jnp.max(values, axis=0, keepdims=True))
            prob = jnp.exp(values - new_top)
            keep = jnp.exp(top - new_top)
            stat[turn, p : p + 1] = new_top
            stat[turn, 4 + p : 5 + p] = keep * total + jnp.sum(prob, axis=0, keepdims=True)
            keep_buf[buf, p : p + 1] = keep
            prob_buf[buf, p] = prob.astype(BF16)

    def mix(n, buf):
        turn, keys = sched[0, n], key_rows(sched[1, n], rows)
        for p in pairs:
            mixed = diagonal_blocks(mm(vt_ref[feat[p], keys], prob_buf[buf, p]))
            acc[turn, p] = acc[turn, p] * keep_buf[buf, p : p + 1] + mixed

    prob_buf[1] = jnp.zeros_like(prob_buf[1])
    keep_buf[1] = jnp.ones_like(keep_buf[1])
    run_pipeline(count, scores, soften, mix)

    def finish(turn, _):
        index = index_of(turn)
        cols = pl.ds(pl.multiple_of(index * QB, QB), QB)
        for p in pairs:
            top, total = stat[turn, p : p + 1], stat[turn, 4 + p : 5 + p]
            mixed = acc[turn, p] / total
            mixed = jnp.concatenate([mixed[:, :QB], mixed[:, QB:]], axis=0).astype(BF16)
            lse_ref[index, p : p + 1] = top + jnp.log(total)
            ot_ref[feat[p], cols] = mixed
            o_ref[turn // taken, lax.rem(turn, taken), :, feat[p]] = mixed.T
        return 0

    lax.fori_loop(0, owners * taken, finish, 0)


def schedule_size(blocks):
    return blocks * ((2 * MOST + 2 * QB) // KB + 1) + 4


def attend(lengths, qt, k, vt, begin, end, steps, before=()):
    feats, rows = qt.shape
    pairs = feats // PAIR
    owners = rows // (steps * QB)
    share = (end - begin) / steps
    blocks = owners * (end - begin)
    return pl.pallas_call(
        functools.partial(attend_kernel, begin, steps),
        in_specs=[SMEM] + [VMEM] * (3 + len(before)),
        out_specs=[VMEM, VMEM, VMEM],
        out_shape=[
            jax.ShapeDtypeStruct((owners, end - begin, QB, feats), BF16),
            jax.ShapeDtypeStruct((feats, rows), BF16),
            jax.ShapeDtypeStruct((rows // QB, pairs, 2 * QB), F32),
        ],
        scratch_shapes=[
            pltpu.SMEM((2, schedule_size(blocks)), jnp.int32),
            pltpu.VMEM((blocks, 8, QB), jnp.int32),
            pltpu.VMEM((blocks, pairs, PAIR, 2 * QB), BF16),
            pltpu.VMEM((blocks, 8, 2 * QB), F32),
            pltpu.VMEM((blocks, pairs, HD, 2 * QB), F32),
            pltpu.VMEM((2, 8, 2 * QB), F32),
            pltpu.VMEM((2, pairs, KB, 2 * QB), F32),
            pltpu.VMEM((2, pairs, KB, 2 * QB), BF16),
        ],
        compiler_params=pltpu.CompilerParams(vmem_limit_bytes=VMEM_CAP),
        cost_estimate=pl.CostEstimate(
            flops=int(8 * share * rows * rows * feats),
            bytes_accessed=rows * feats * 10,
            transcendentals=int(share * rows * rows),
        ),
        name="attend",
    )(lengths, qt, k, vt, *before)


def attend_back_kernel(
    len_ref, qt_ref, k_ref, kt_ref, v_ref, do_ref, ot_ref, lse_ref, cos_ref, sin_ref,
    grad_ref, grad_t_ref, sched, window, q_diag, do_diag, stat, dq_acc, dk_acc, dv_acc,
    score_buf, prob_grad_buf, prob_buf, score_grad_buf,
):
    feats, rows = qt_ref.shape
    pairs = range(feats // PAIR)
    feat = [pl.ds(p * PAIR, PAIR) for p in pairs]
    dk_acc[...] = jnp.zeros_like(dk_acc)
    dv_acc[...] = jnp.zeros_like(dv_acc)
    dq_acc[...] = jnp.zeros_like(dq_acc)

    def prepare(turn, _):
        cols = pl.ds(pl.multiple_of(turn * QB, QB), QB)
        store_window(len_ref, window, turn, turn * QB)
        for p in pairs:
            do_t = do_ref[cols, feat[p]].T
            delta = do_t.astype(F32) * ot_ref[feat[p], cols].astype(F32)
            delta = [jnp.sum(part, axis=0, keepdims=True) for part in (delta[:HD], delta[HD:])]
            q_diag[turn, p] = block_diagonal_t(qt_ref[feat[p], cols])
            do_diag[turn, p] = block_diagonal_t(do_t)
            stat[turn, p : p + 1] = lse_ref[turn, p : p + 1]
            stat[turn, 4 + p : 5 + p] = jnp.concatenate(delta, axis=1)
        return 0

    lax.fori_loop(0, rows // QB, prepare, 0)
    count = fill_schedule(len_ref, sched, rows // QB, lambda turn: turn, rows)

    def scores(n, buf):
        turn, keys = sched[0, n], key_rows(sched[1, n], rows)
        for p in pairs:
            score_buf[buf, p] = mm(k_ref[keys, feat[p]], q_diag[turn, p])
            prob_grad_buf[buf, p] = mm(v_ref[keys, feat[p]], do_diag[turn, p])

    def soften(n, buf):
        turn = sched[0, n]
        inside = inside_window(window[turn, 0:1], window[turn, 1:2], sched[1, n], rows)
        for p in pairs:
            lse, delta = stat[turn, p : p + 1], stat[turn, 4 + p : 5 + p]
            prob = jnp.where(inside, jnp.exp(score_buf[buf, p] - lse), 0.0)
            prob_buf[buf, p] = prob.astype(BF16)
            score_grad_buf[buf, p] = (prob * (prob_grad_buf[buf, p] - delta)).astype(BF16)

    def mix(n, buf):
        turn, keys = sched[0, n], key_rows(sched[1, n], rows)
        for p in pairs:
            dv_acc[feat[p], keys] += mm_nt(do_diag[turn, p], prob_buf[buf, p])
            dk_acc[feat[p], keys] += mm_nt(q_diag[turn, p], score_grad_buf[buf, p])
            dq_acc[turn, p] += diagonal_blocks(mm(kt_ref[feat[p], keys], score_grad_buf[buf, p]))

    prob_buf[1] = jnp.zeros_like(prob_buf[1])
    score_grad_buf[1] = jnp.zeros_like(score_grad_buf[1])
    run_pipeline(count, scores, soften, mix)

    def finish(turn, _):
        cols = pl.ds(pl.multiple_of(turn * QB, QB), QB)
        cosine, sine = cos_ref[:, cols], sin_ref[:, cols]
        for p in pairs:
            dq = jnp.concatenate([dq_acc[turn, p, :, :QB], dq_acc[turn, p, :, QB:]], axis=0) * SCALE
            fields = (
                rotate_t(dq, cosine, sine, -1.0),
                rotate_t(dk_acc[feat[p], cols], cosine, sine, -1.0),
                dv_acc[feat[p], cols],
            )
            for kind, field in enumerate(fields):
                place = pl.ds(kind * feats + p * PAIR, PAIR)
                field = field.astype(BF16)
                grad_t_ref[place, cols] = field
                grad_ref[cols, place] = field.T
        return 0

    lax.fori_loop(0, rows // QB, finish, 0)


def attend_back(lengths, qt, k, kt, v, do, ot, lse, cosine, sine):
    feats, rows = qt.shape
    blocks = rows // QB
    return pl.pallas_call(
        attend_back_kernel,
        in_specs=[SMEM] + [VMEM] * 9,
        out_specs=[VMEM, VMEM],
        out_shape=[
            jax.ShapeDtypeStruct((rows, 3 * feats), BF16),
            jax.ShapeDtypeStruct((3 * feats, rows), BF16),
        ],
        scratch_shapes=[
            pltpu.SMEM((2, schedule_size(blocks)), jnp.int32),
            pltpu.VMEM((blocks, 8, QB), jnp.int32),
            pltpu.VMEM((blocks, feats // PAIR, PAIR, 2 * QB), BF16),
            pltpu.VMEM((blocks, feats // PAIR, PAIR, 2 * QB), BF16),
            pltpu.VMEM((blocks, 8, 2 * QB), F32),
            pltpu.VMEM((blocks, feats // PAIR, HD, 2 * QB), F32),
            pltpu.VMEM((feats, rows), F32),
            pltpu.VMEM((feats, rows), F32),
        ]
        + [pltpu.VMEM((2, feats // PAIR, KB, 2 * QB), kind) for kind in (F32, F32, BF16, BF16)],
        compiler_params=pltpu.CompilerParams(vmem_limit_bytes=VMEM_CAP),
        cost_estimate=pl.CostEstimate(
            flops=10 * rows * rows * feats, bytes_accessed=rows * feats * 28, transcendentals=rows * rows
        ),
        name="attend_back",
    )(lengths, qt, k, kt, v, do, ot, lse, cosine, sine)


def neighbours():
    me = lax.axis_index("mp")
    one = lax.rem(me, 2)
    across = me + 1 - 2 * one
    along = lax.rem(me + 2, 4)
    return me, across, along, lax.rem(across + 2, 4)


def remote(src, dst, sems, kind, step, device):
    send, recv = sems
    return pltpu.make_async_remote_copy(
        src_ref=src,
        dst_ref=dst,
        send_sem=send.at[kind, step],
        recv_sem=recv.at[kind, step],
        device_id={"mp": device},
        device_id_type=MESH,
    )


def pack_neighbours(packs):
    index = lax.axis_index("dp")
    core, chip = lax.rem(index, 2), index // 2
    chips = packs // 2
    return core, chip, index + 1 - 2 * core, [
        lax.rem(index + 2 * shift, packs) for shift in range(1, chips)
    ]


def chip_across(chip, bits):
    low, high = lax.rem(chip, 2), chip // 2
    low = 1 - low if bits % 2 else low
    high = 1 - high if bits // 2 else high
    return low + 2 * high


def remote_pack(src, dst, send, recv, device):
    return pltpu.make_async_remote_copy(
        src_ref=src, dst_ref=dst, send_sem=send, recv_sem=recv,
        device_id={"dp": device}, device_id_type=MESH,
    )


CHIPS = 4
PILES = (((0, 2), 0), ((1, 3), 0), ((0, 1), 2), ((2, 3), 2))
PARTNERS = (1, 2)


def group_barrier(devices, packs=()):
    barrier = pltpu.get_barrier_semaphore()
    for device in devices:
        pl.semaphore_signal(barrier, inc=1, device_id={"mp": device}, device_id_type=MESH)
    for device in packs:
        pl.semaphore_signal(barrier, inc=1, device_id={"dp": device}, device_id_type=MESH)
    pl.semaphore_wait(barrier, len(devices) + len(packs))


def scatter_first(part, slot, from_x, from_y, sems, kind, step):
    me, x, y, d = neighbours()
    return [
        remote(part.at[slot, x, 0], from_x.at[step, 0], sems, kind, step, x),
        remote(part.at[slot, y, 1], from_y.at[step, 0], sems, kind + 1, step, y),
        remote(part.at[slot, d, 0], from_x.at[step, 1], sems, kind + 2, step, x),
        remote(part.at[slot, d, 1], from_y.at[step, 1], sems, kind + 3, step, y),
    ]


def scatter_second(from_x, from_y, last_x, last_y, sems, kind, step):
    me, x, y, d = neighbours()
    return [
        remote(from_x.at[step, 1], last_y.at[step], sems, kind + 4, step, y),
        remote(from_y.at[step, 1], last_x.at[step], sems, kind + 5, step, x),
    ]


def scatter_middle(part, slot, from_x, from_y, last_x, last_y, sems, kind, step):
    me, x, y, d = neighbours()
    first = scatter_first(part, slot, from_x, from_y, sems, kind, step)
    second = scatter_second(from_x, from_y, last_x, last_y, sems, kind, step)
    first[2].wait_recv()
    total = from_x[step, 1].astype(F32) + part[slot, y, 0].astype(F32)
    from_x[step, 1] = total.astype(BF16)
    second[0].start()
    first[3].wait_recv()
    total = from_y[step, 1].astype(F32) + part[slot, x, 1].astype(F32)
    from_y[step, 1] = total.astype(BF16)
    second[1].start()


def scatter_last(part, slot, from_x, from_y, last_x, last_y, sems, kind, step):
    me, x, y, d = neighbours()
    first = scatter_first(part, slot, from_x, from_y, sems, kind, step)
    second = scatter_second(from_x, from_y, last_x, last_y, sems, kind, step)
    first[0].wait_recv()
    first[1].wait_recv()
    second[0].wait_recv()
    second[1].wait_recv()
    upper = part[slot, me, 0].astype(F32) + from_x[step, 0].astype(F32) + last_y[step].astype(F32)
    lower = part[slot, me, 1].astype(F32) + from_y[step, 0].astype(F32) + last_x[step].astype(F32)
    for copy in first + second:
        copy.wait_send()
    return jnp.concatenate([upper, lower], axis=0)


def ffn_kernel(
    packs,
    len_ref, early0, early1, early2, early3, o_hbm, tok_hbm, cot_hbm, wo0, wo1, wo2, wo3, wg_hbm, wu_hbm, wd_hbm, gain_ref, bias_ref,
    h1_ref, dh1_ref, sums_ref, do_hbm, land_hbm, down0_hbm, down1_hbm, down2_hbm, down3_hbm, rows_hbm, *rest,
):
    chips = packs // 2
    piles = rest[: len(PILES)]
    (
        wo, wg, wu, wd, o_all, tok, cot, h1_all, hid, dgate, dup, part, from_x, from_y, last_x, last_y,
        a2_all, acc, stage, do_own, db_own, load_sem, tok_sem, cot_sem, own_sem, early_sem, stage_sem, put_sem, pile_sem,
        core_send, core_recv, send_sem, recv_sem,
    ) = rest[len(PILES) :]
    core, chip, other_core, _ = pack_neighbours(packs)
    steps, owners, block, width = o_all.shape
    share = width // packs
    feats = o_hbm.shape[-1]
    size = owners * block
    cut = dgate.shape[-1] // PIECES
    early = early0.shape[1]
    some = owners // 2
    sems = (send_sem, recv_sem)
    me, x, y, d = neighbours()
    row_total = owners * steps * block
    live_end = row_total - len_ref[0, len_ref.shape[1] - 1]

    loads = [(wg_hbm, wg), (wu_hbm, wu), (wd_hbm, wd)]
    for source, group in ((wo0, me), (wo1, x), (wo2, y), (wo3, d)):
        loads.append((source, wo.at[pl.ds(pl.multiple_of(group * feats, feats), feats)]))
    loads = [pltpu.make_async_copy(a, b, load_sem.at[i]) for i, (a, b) in enumerate(loads)]

    def fetch(step):
        slot = lax.rem(step, 2)
        return (
            pltpu.make_async_copy(tok_hbm.at[:, step], tok.at[slot], tok_sem.at[slot]),
            pltpu.make_async_copy(cot_hbm.at[:, step], cot.at[slot], cot_sem.at[slot]),
        )

    def lanes(group):
        return pl.ds(pl.multiple_of(group * feats, feats), feats)

    def early_copies(step):
        return [
            pltpu.make_async_copy(
                source.at[:, step], o_all.at[step, :, :, lanes(group)], early_sem.at[step, i]
            )
            for i, (source, group) in enumerate(
                ((early0, me), (early1, x), (early2, y), (early3, d))
            )
        ]

    def own_copy(step):
        return pltpu.make_async_copy(
            o_hbm.at[:, step - early], o_all.at[step, :, :, lanes(me)], own_sem.at[step]
        )

    def gather_own(step):
        source, target = o_hbm.at[:, step - early], o_all.at[step, :, :, lanes(me)]
        return [
            remote(source, target, sems, 0, step, x),
            remote(source, target, sems, 1, step, y),
        ]

    halfway = owners // 2

    def gather_relay(step):
        upper = o_all.at[step, pl.ds(0, halfway), :, lanes(x)]
        lower = o_all.at[step, pl.ds(halfway, halfway), :, lanes(y)]
        return [
            remote(upper, upper, sems, 2, step, y),
            remote(lower, lower, sems, 3, step, x),
        ]

    def relay(step):
        for copy, passed in zip(gather_own(step), gather_relay(step)):
            copy.wait_recv()
            passed.start()

    outgoing = (hid, dgate, dup)

    def to_core(kind):
        source = outgoing[kind] if kind < 3 else stage.at[0].reshape(size, width)
        return remote_pack(
            source, land_hbm.at[kind], core_send.at[kind], core_recv.at[kind], other_core
        )

    def landed(kind):
        return pltpu.make_async_copy(
            land_hbm.at[kind], tok.at[kind % 2].reshape(size, width), tok_sem.at[kind % 2]
        )

    def pile_copies(kind):
        summed = cot.at[kind % 2].reshape(size, width)
        return [
            pltpu.make_async_copy(
                summed.at[pl.ds(pl.multiple_of(chip_across(chip, bits) * share, share), share)],
                pile.at[i, kind - first],
                pile_sem.at[kind % 2, bits],
            )
            for pile, (places, first) in zip(piles, PILES)
            for i, bits in enumerate(places)
            if first <= kind < first + 2
        ]

    def sum_kind(kind):
        landed(kind).wait()
        if kind >= 2:
            for copy in pile_copies(kind - 2):
                copy.wait()
        theirs = tok[kind % 2].reshape(size, width)
        if kind < 3:
            mine = [
                acc[kind, pl.ds(pl.multiple_of((2 * z + core) * share, share), share), :]
                for z in range(chips)
            ]
            mine = jnp.concatenate(mine, axis=0)
        else:
            mine = h1_all[...].reshape(size, width)
        total = (mine + theirs.astype(F32)).astype(BF16)
        cot[kind % 2] = total.reshape(owners, block, width)
        for copy in pile_copies(kind):
            copy.start()

    def put_rows(step):
        return [
            remote(
                stage.at[lax.rem(step, 2), target], rows_hbm.at[i, step], sems, 13 + i, step, target
            )
            for i, target in enumerate((x, y, d))
        ]

    def put_do(step):
        return [
            remote(do_own.at[step, target], do_hbm.at[me, step], sems, 10 + i, step, target)
            for i, target in enumerate((x, y, d))
        ]

    def keep_do(step):
        return pltpu.make_async_copy(do_own.at[step, me], do_hbm.at[me, step], put_sem.at[step])

    for copy in fetch(0):
        copy.start()
    for copy in loads:
        copy.start()
    for step in range(early):
        for copy in early_copies(step):
            copy.start()
    group_barrier((x, y, d), (other_core,))

    def begin(step, _):
        for copy in gather_own(step):
            copy.start()
        own_copy(step).start()
        return 0

    lax.fori_loop(early, steps, begin, 0)
    acc[...] = jnp.zeros_like(acc)
    sums_ref[...] = jnp.zeros_like(sums_ref)
    for copy in loads:
        copy.wait()

    def step_body(step, _):
        slot = lax.rem(step, 2)
        now, before, older = [lax.rem(step + lag, 3) for lag in (0, 2, 1)]

        @pl.when(step + 1 < steps)
        def _():
            for copy in fetch(step + 1):
                copy.start()

        @pl.when((step + 1 < steps) & (step + 1 >= early))
        def _():
            relay(step + 1)

        @pl.when(step < early)
        def _():
            for copy in early_copies(step):
                copy.wait()

        @pl.when((step < steps) & (step >= early))
        def _():
            for copy in gather_relay(step):
                copy.wait_recv()
            own_copy(step).wait()

        @pl.when(step < steps)
        def _():
            for copy in fetch(step):
                copy.wait()
            def some_rows(turn, _):
                who, rows = pl.ds(turn * some, some), pl.ds(turn * some * block, some * block)
                position = lax.broadcasted_iota(jnp.int32, (some, block, 1), 1) + step * block
                position = position + (steps * block) * (
                    lax.broadcasted_iota(jnp.int32, (some, block, 1), 0) + turn * some
                )
                eb = jnp.where(position < live_end, cot[slot, who].astype(F32), 0.0).astype(BF16)
                cot[slot, who] = eb
                eb = eb.reshape(some * block, width)
                mixed = mm(o_all[step, who].reshape(some * block, width), wo[...])
                h1 = tok[slot, who].reshape(some * block, width).astype(F32) + mixed
                h1_all[who] = h1.reshape(some, block, width)
                hat, _ = norm_rows(h1)
                a2 = (hat * gain_ref[...] + bias_ref[...]).astype(BF16)
                a2_all[rows] = a2
                for piece in range(PIECES):
                    cols = pl.ds(piece * cut, cut)
                    gate = mm(a2, wg[:, cols])
                    up = mm(a2, wu[:, cols])
                    back = mm_nt(eb, wd[cols, :])
                    sig = 0.5 * jnp.tanh(0.5 * gate) + 0.5
                    act = gate * sig
                    hid[rows, cols] = (act * up).astype(BF16)
                    dgate[rows, cols] = (back * up * (sig + act * (1.0 - sig))).astype(BF16)
                    dup[rows, cols] = (back * act).astype(BF16)
                dc = mm_nt(dgate[rows, :], wg[...]) + mm_nt(dup[rows, :], wu[...])
                part[now, who] = dc.astype(BF16).reshape(some, 2, block // 2, width)
                return 0

            lax.fori_loop(0, owners // some, some_rows, 0)
            h1_ref[step] = h1_all[me]
            dh1_ref[step] = cot[slot, me].astype(F32)
            for copy in scatter_first(part, now, from_x, from_y, sems, 4, step):
                copy.start()

        @pl.when(step == steps)
        def _():
            for kind in range(3):
                for z in range(chips):
                    rows = pl.ds(pl.multiple_of((2 * z + 1 - core) * share, share), share)
                    outgoing[kind][z * share : (z + 1) * share, :] = acc[kind, rows, :].astype(BF16)
                to_core(kind).start()

        @pl.when((step >= 1) & (step <= steps))
        def _():
            scatter_middle(
                part, before, from_x, from_y, last_x, last_y, sems, 4, step - 1
            )

        @pl.when(step == steps)
        def _():
            for kind in range(2):
                to_core(kind).wait_recv()
                landed(kind).start()
            sum_kind(0)
            to_core(2).wait_recv()
            landed(2).start()
            sum_kind(1)
            sum_kind(2)

        def stage_copies(at, direct):
            slot = lax.rem(at, 2)
            places = [(me, down0_hbm.at[at])]
            if not direct:
                places += [(x, down1_hbm), (y, down2_hbm), (d, down3_hbm)]
                places[1:] = [(who, out.at[at - DIRECT]) for who, out in places[1:]]
            return [
                pltpu.make_async_copy(stage.at[slot, who], out, stage_sem.at[i, slot])
                for i, (who, out) in enumerate(places)
            ]

        @pl.when(step < steps)
        def _():
            @pl.when((step >= 2) & (step - 2 < DIRECT))
            def _():
                for copy in stage_copies(step - 2, True):
                    copy.wait()
                for copy in put_rows(step - 2):
                    copy.wait_send()

            @pl.when((step >= 2) & (step - 2 >= DIRECT))
            def _():
                for copy in stage_copies(step - 2, False):
                    copy.wait()

            stage[slot] = mm(hid[...], wd[...]).astype(BF16).reshape(owners, block, width)

            @pl.when(step < DIRECT)
            def _():
                for copy in stage_copies(step, True) + put_rows(step):
                    copy.start()

            @pl.when(step >= DIRECT)
            def _():
                for copy in stage_copies(step, False):
                    copy.start()

            a2_t = a2_all[...].T
            eb_t = cot[slot].reshape(size, width).T
            acc[0] += mm(a2_t, dgate[...])
            acc[1] += mm(a2_t, dup[...])
            acc[2] += mm(eb_t, hid[...])

        @pl.when(step == steps)
        def _():
            for copy in stage_copies(steps - 2, False) + stage_copies(steps - 1, False):
                copy.wait()

        @pl.when(step >= 2)
        def _():
            prev = step - 2
            dc = scatter_last(part, older, from_x, from_y, last_x, last_y, sems, 4, prev)
            hat, scale = norm_rows(h1_ref[prev])
            sums_ref[0:1] += jnp.sum(dc * hat, axis=0, keepdims=True)
            sums_ref[1:2] += jnp.sum(dc, axis=0, keepdims=True)
            inner = dc * gain_ref[...]
            inner = inner - jnp.mean(inner, axis=-1, keepdims=True) - hat * jnp.mean(
                inner * hat, axis=-1, keepdims=True
            )
            dh1 = dh1_ref[prev] + scale * inner
            dh1_ref[prev] = dh1
            db = dh1.astype(BF16)
            db_own[prev] = db
            back = mm_nt(db, wo[...]).astype(BF16)
            for group in range(owners):
                do_own[prev, group] = back[:, group * feats : (group + 1) * feats]
            for copy in put_do(prev):
                copy.start()
            keep_do(prev).start()

        return 0

    lax.fori_loop(0, steps + 2, step_body, 0)

    o_mine = jnp.concatenate([o_all[step, me] for step in range(steps)], axis=0)
    for turn, which in enumerate((1 - core, core)):
        columns = [
            db_own[:, :, pl.ds(pl.multiple_of((2 * z + which) * share, share), share)].reshape(
                steps * block, share
            )
            for z in range(chips)
        ]
        values = mm_tn(jnp.concatenate(columns, axis=1), o_mine)
        if turn == 0:
            stage[0] = values.astype(BF16).reshape(owners, block, width)
            to_core(3).start()
        else:
            h1_all[...] = values.reshape(owners, block, width)

    to_core(3).wait_recv()
    landed(3).start()
    sum_kind(3)
    for kind in range(4):
        to_core(kind).wait_send()
    for copy in pile_copies(2) + pile_copies(3):
        copy.wait()

    def sent(step, _):
        for copy in gather_own(step) + gather_relay(step):
            copy.wait_send()
        return 0

    lax.fori_loop(early, steps, sent, 0)

    for step in range(DIRECT):
        for copy in put_rows(step):
            copy.wait_recv()

    def finish(step, _):
        for copy in put_do(step):
            copy.wait()
        keep_do(step).wait()
        return 0

    lax.fori_loop(0, steps, finish, 0)


def ffn(lengths, early, o, tokens, cotangent, wo, wg, wu, wd, gain, bias, steps, packs):
    rows, width = tokens.shape
    feats = o.shape[-1]
    owners = width // feats
    block = rows // (owners * steps)
    hidden = wg.shape[1]
    size = owners * block
    chips = packs // 2
    by_owner = lambda a: a.reshape(owners, steps, block, a.shape[1])
    own = jax.ShapeDtypeStruct((steps, block, width), F32)
    half = (steps, 2, block // 2, width)
    dma = pltpu.SemaphoreType.DMA
    flops = 2 * rows * width * (width + 9 * hidden)
    h1, dh1, sums, do, _, *rest = pl.pallas_call(
        functools.partial(ffn_kernel, packs),
        in_specs=[SMEM] + [ANY] * 14 + [VMEM, VMEM],
        out_specs=[VMEM, VMEM, VMEM] + [ANY] * (7 + len(PILES)),
        out_shape=[
            own,
            own,
            jax.ShapeDtypeStruct((2, width), F32),
            jax.ShapeDtypeStruct((owners, steps, block, feats), BF16),
            jax.ShapeDtypeStruct((4, size, width), BF16),
        ]
        + [jax.ShapeDtypeStruct((steps, block, width), BF16)]
        + [jax.ShapeDtypeStruct((steps - DIRECT, block, width), BF16)] * 3
        + [jax.ShapeDtypeStruct((3, DIRECT, block, width), BF16)]
        + [jax.ShapeDtypeStruct((2, 2, width // packs, width), BF16)] * len(PILES),
        scratch_shapes=[
            pltpu.VMEM((width, width), BF16),
            pltpu.VMEM((width, hidden), BF16),
            pltpu.VMEM((width, hidden), BF16),
            pltpu.VMEM((hidden, width), BF16),
            pltpu.VMEM((steps, owners, block, width), BF16),
            pltpu.VMEM((2, owners, block, width), BF16),
            pltpu.VMEM((2, owners, block, width), BF16),
            pltpu.VMEM((owners, block, width), F32),
            pltpu.VMEM((size, hidden), BF16),
            pltpu.VMEM((size, hidden), BF16),
            pltpu.VMEM((size, hidden), BF16),
            pltpu.VMEM((3, owners, 2, block // 2, width), BF16),
            pltpu.VMEM(half, BF16),
            pltpu.VMEM(half, BF16),
            pltpu.VMEM((steps, block // 2, width), BF16),
            pltpu.VMEM((steps, block // 2, width), BF16),
            pltpu.VMEM((size, width), BF16),
            pltpu.VMEM((3, width, hidden), F32),
            pltpu.VMEM((2, owners, block, width), BF16),
            pltpu.VMEM((steps, owners, block, feats), BF16),
            pltpu.VMEM((steps, block, width), BF16),
            dma((7,)),
            dma((2,)),
            dma((2,)),
            dma((steps,)),
            dma((early[0].shape[1], 4)),
            dma((4, 2)),
            dma((steps,)),
            dma((2, chips)),
            dma((4,)),
            dma((4,)),
            dma((16, steps)),
            dma((16, steps)),
        ],
        compiler_params=pltpu.CompilerParams(
            collective_id=0, has_side_effects=True, vmem_limit_bytes=VMEM_CAP
        ),
        cost_estimate=pl.CostEstimate(flops=flops, bytes_accessed=rows * width * 14, transcendentals=0),
        name="ffn",
    )(lengths, *early, o, by_owner(tokens), by_owner(cotangent), *wo, wg, wu, wd, gain, bias)
    return h1, dh1, sums, do.reshape(rows, feats), rest[:5], rest[5:]


def last_kernel(
    packs,
    grad_hbm, grad_t_hbm, a1_hbm, tok_hbm, dh1_ref, h1_hbm, wq_ref, wk_ref, wv_ref, gain_ref, sums2_ref, *rest,
):
    chips = packs // 2
    downs, rest = rest[:5], rest[5:]
    piles, rest = rest[: len(PILES)], rest[len(PILES) :]
    (
        out_ref, tg_ref, gq_ref, gk_ref, gv_ref, gate_ref, up_ref, down_ref, proj_ref, norm_ref,
        grad, grad_t, a1, tok, part, from_x, from_y, last_x, last_y, h1, down, pile, pile_out, pile_in, sums1,
        full, core_out, core_in, chip_out, chip_in, proj_out, proj_in, norm_out, norm_in,
        grad_sem, tok_sem, load_sem, core_send, core_recv, chip_send, chip_recv, pile_send, pile_recv,
        small_send, small_recv, send_sem, recv_sem,
    ) = rest
    steps, owners, _, half, width = part.shape
    feats = wq_ref.shape[1]
    size = owners * 2 * half
    share = width // packs
    tall = 3 * feats
    sems = (send_sem, recv_sem)
    me, x, y, d = neighbours()
    core, chip, other_core, next_chips = pack_neighbours(packs)

    def fetch(step):
        return [
            pltpu.make_async_copy(grad_hbm.at[:, step], grad.at[step], grad_sem.at[step]),
            pltpu.make_async_copy(tok_hbm.at[:, step], tok.at[step], tok_sem.at[step]),
        ]

    later = [(grad_t_hbm, grad_t), (a1_hbm, a1)]
    later += [(piles[i], pile.at[i]) for i in range(len(PILES))]
    later += [(h1_hbm, h1), (downs[0], down.at[0])]
    later += [(downs[i], down.at[i, pl.ds(DIRECT, steps - DIRECT)]) for i in range(1, 4)]
    later += [(downs[4], down.at[pl.ds(1, 3), pl.ds(0, DIRECT)])]
    later = [pltpu.make_async_copy(a, b, load_sem.at[i]) for i, (a, b) in enumerate(later)]

    def to_core():
        return remote_pack(core_out, core_in, core_send, core_recv, other_core)

    def to_chips():
        return [
            remote_pack(
                chip_out.at[lax.rem(chip + i + 1, chips)], chip_in.at[i],
                chip_send.at[i], chip_recv.at[i], device,
            )
            for i, device in enumerate(next_chips)
        ]

    def pile_copies():
        index = lax.axis_index("dp")
        return [
            remote_pack(
                pile_out.at[i], pile_in.at[i], pile_send.at[i], pile_recv.at[i],
                index + 2 * (chip_across(chip, bits) - chip),
            )
            for i, bits in enumerate(reversed(PARTNERS))
        ]

    def small(kind, source, target):
        return [
            remote(source(device), target.at[i], (small_send, small_recv), kind, i, device)
            for i, device in enumerate((x, y, d))
        ]

    def proj_copies():
        return small(0, lambda device: proj_out.at[device], proj_in)

    def norm_copies():
        return small(1, lambda device: norm_out, norm_in)

    def begin(step, _):
        for copy in fetch(step):
            copy.start()
        return 0

    lax.fori_loop(0, steps, begin, 0)
    for copy in later:
        copy.start()
    group_barrier((x, y, d), [other_core] + next_chips)
    sums1[...] = jnp.zeros_like(sums1)

    def first(step, _):
        for copy in fetch(step):
            copy.wait()
        rows = grad[step].reshape(size, tall)
        da = mm_nt(rows[:, :feats], wq_ref[...])
        da = da + mm_nt(rows[:, feats : 2 * feats], wk_ref[...])
        da = da + mm_nt(rows[:, 2 * feats :], wv_ref[...])
        part[step] = da.astype(BF16).reshape(owners, 2, half, width)
        for copy in scatter_first(part, step, from_x, from_y, sems, 0, step):
            copy.start()

        @pl.when(step == 0)
        def _():
            for copy in later[2 : 2 + len(PILES)]:
                copy.wait()
            for i in range(2):
                total = pile[2 * i, 1].astype(F32) + pile[2 * i + 1, 1].astype(F32)
                pile_out[i] = total.astype(BF16)
            for copy in pile_copies():
                copy.start()

        hat, _ = norm_rows(tok[step].reshape(size, width).astype(F32))
        sums1[0:1] += jnp.sum(da * hat, axis=0, keepdims=True)
        sums1[1:2] += jnp.sum(da, axis=0, keepdims=True)
        return 0

    lax.fori_loop(0, steps, first, 0)
    later[0].wait()
    later[1].wait()
    for kind in range(3):
        rows = pl.ds(kind * feats, feats)
        full[rows, :] = mm(grad_t[rows, :], a1[...])
    full[pl.ds(tall, 16), :] = jnp.concatenate(
        [sums1[...], sums2_ref[...], jnp.zeros((12, width), F32)], axis=0
    )
    for z in range(chips):
        columns = pl.ds(pl.multiple_of((2 * z + 1 - core) * share, share), share)
        core_out[z] = full[:, columns].astype(BF16)
    to_core().start()

    to_core().wait_recv()
    for z in range(chips):
        columns = pl.ds(pl.multiple_of((2 * z + core) * share, share), share)
        chip_out[z] = (full[:, columns] + core_in[z].astype(F32)).astype(BF16)
    for copy in to_chips():
        copy.start()
    for copy in later[2 + len(PILES) :]:
        copy.wait()

    def sum_piles():
        for copy in pile_copies():
            copy.wait_recv()
        for kind in range(4):
            half, at = kind // 2, kind % 2
            total = pile[2 * half, 0, at].astype(F32) + pile[2 * half + 1, 0, at].astype(F32)
            total = total + pile_in[half, at].astype(F32)
            if kind < 2:
                (gate_ref, up_ref)[kind][...] = total
            elif kind == 2:
                down_ref[...] = total.T
            else:
                for group in range(owners):
                    proj_out[group] = total[:, group * feats : (group + 1) * feats].astype(BF16)
                for copy in proj_copies():
                    copy.start()

    def finish(step):
        da = scatter_last(part, step, from_x, from_y, last_x, last_y, sems, 0, step)
        hat, scale = norm_rows(tok[step, me].astype(F32))
        inner = da * gain_ref[...]
        inner = inner - jnp.mean(inner, axis=-1, keepdims=True) - hat * jnp.mean(
            inner * hat, axis=-1, keepdims=True
        )
        tg_ref[step] = (dh1_ref[step] + scale * inner).astype(BF16)

    def second(step, _):
        scatter_middle(part, step, from_x, from_y, last_x, last_y, sems, 0, step)
        total = h1[step]
        for i in range(4):
            total = total + down[i, step].astype(F32)
        out_ref[step] = total.astype(BF16)
        return 0

    def third(step, _):
        finish(step)
        return 0

    lax.fori_loop(0, steps, second, 0)
    sum_piles()
    lax.fori_loop(0, steps - 2, third, 0)
    total = chip_out[chip].astype(F32)
    for i, copy in enumerate(to_chips()):
        copy.wait_recv()
        total = total + chip_in[i].astype(F32)
    norm_out[...] = total[tall : tall + 8]
    for copy in norm_copies():
        copy.start()
    finish(steps - 2)
    for kind, ref in enumerate((gq_ref, gk_ref, gv_ref)):
        ref[...] = total[kind * feats : (kind + 1) * feats].T
    total = proj_out[me].astype(F32)
    for i, copy in enumerate(proj_copies()):
        copy.wait_recv()
        total = total + proj_in[i].astype(F32)
    proj_ref[...] = total.T
    finish(steps - 1)
    total = norm_out[...]
    for i, copy in enumerate(norm_copies()):
        copy.wait_recv()
        total = total + norm_in[i]
    norm_ref[...] = total
    for copy in [to_core()] + to_chips() + pile_copies() + proj_copies() + norm_copies():
        copy.wait_send()


def last(grads, grads_t, a1, tokens, dh1, h1, wq, wk, wv, gain, sums2, downs, piles, packs):
    rows, width = tokens.shape
    steps, block, _ = dh1.shape
    owners = rows // (steps * block)
    feats = wq.shape[1]
    hidden = piles[0].shape[-1]
    chips = packs // 2
    share = width // packs
    tall = 3 * feats + 16
    by_owner = lambda a: a.reshape(owners, steps, block, a.shape[1])
    half = (steps, 2, block // 2, width)
    dma = pltpu.SemaphoreType.DMA
    own = jax.ShapeDtypeStruct((steps, block, width), BF16)
    f32 = lambda *shape: jax.ShapeDtypeStruct(shape, F32)
    return pl.pallas_call(
        functools.partial(last_kernel, packs),
        in_specs=[ANY] * 4 + [VMEM, ANY] + [VMEM] * 5 + [ANY] * (5 + len(piles)),
        out_specs=[VMEM] * 10,
        out_shape=[own, own]
        + [f32(share, feats)] * 3
        + [f32(share, hidden), f32(share, hidden), f32(hidden, share), f32(feats, share), f32(8, share)],
        scratch_shapes=[
            pltpu.VMEM((steps, owners, block, 3 * feats), BF16),
            pltpu.VMEM((3 * feats, rows), BF16),
            pltpu.VMEM((rows, width), BF16),
            pltpu.VMEM((steps, owners, block, width), BF16),
            pltpu.VMEM((steps, owners, 2, block // 2, width), BF16),
            pltpu.VMEM(half, BF16),
            pltpu.VMEM(half, BF16),
            pltpu.VMEM((steps, block // 2, width), BF16),
            pltpu.VMEM((steps, block // 2, width), BF16),
            pltpu.VMEM((steps, block, width), F32),
            pltpu.VMEM((4, steps, block, width), BF16),
            pltpu.VMEM((len(PILES), 2, 2, share, hidden), BF16),
            pltpu.VMEM((2, 2, share, hidden), BF16),
            pltpu.VMEM((2, 2, share, hidden), BF16),
            pltpu.VMEM((2, width), F32),
            pltpu.VMEM((tall, width), F32),
            pltpu.VMEM((chips, tall, share), BF16),
            pltpu.VMEM((chips, tall, share), BF16),
            pltpu.VMEM((chips, tall, share), BF16),
            pltpu.VMEM((chips - 1, tall, share), BF16),
            pltpu.VMEM((owners, share, feats), BF16),
            pltpu.VMEM((owners - 1, share, feats), BF16),
            pltpu.VMEM((8, share), F32),
            pltpu.VMEM((owners - 1, 8, share), F32),
            dma((steps,)),
            dma((steps,)),
            dma((8 + len(piles),)),
            dma,
            dma,
            dma((chips - 1,)),
            dma((chips - 1,)),
            dma((2,)),
            dma((2,)),
            dma((2, owners - 1)),
            dma((2, owners - 1)),
            dma((6, steps)),
            dma((6, steps)),
        ],
        compiler_params=pltpu.CompilerParams(
            collective_id=1, has_side_effects=True, vmem_limit_bytes=VMEM_CAP
        ),
        cost_estimate=pl.CostEstimate(
            flops=12 * rows * width * feats, bytes_accessed=rows * width * 20, transcendentals=0
        ),
        name="last",
    )(
        by_owner(grads), grads_t, a1, by_owner(tokens), dh1, h1, wq, wk, wv, gain, sums2, *downs, *piles
    )


def hand_out_kernel(count, *refs):
    sources, outs, held = refs[:count], refs[count : 2 * count], refs[2 * count : 3 * count]
    in_sem, out_sem = refs[3 * count :]
    loads = [pltpu.make_async_copy(sources[i], held[i], in_sem.at[i]) for i in range(count)]
    stores = [pltpu.make_async_copy(held[i], outs[i], out_sem.at[i]) for i in range(count)]
    for copy in loads:
        copy.start()
    for load, store in zip(loads, stores):
        load.wait()
        store.start()
    for store in stores:
        store.wait()


def hand_out(arrays):
    count = len(arrays)
    return pl.pallas_call(
        functools.partial(hand_out_kernel, count),
        in_specs=[ANY] * count,
        out_specs=[ANY] * count,
        out_shape=[jax.ShapeDtypeStruct(a.shape, a.dtype) for a in arrays],
        scratch_shapes=[pltpu.VMEM(a.shape, a.dtype) for a in arrays]
        + [pltpu.SemaphoreType.DMA((count,))] * 2,
        compiler_params=pltpu.CompilerParams(vmem_limit_bytes=VMEM_CAP),
        name="hand_out",
    )(*arrays)


def local_square(
    tokens, lengths, cotangent, norm1_gain, norm1_bias, w_query, w_key, w_value, w_output,
    norm2_gain, norm2_bias, w_gate, w_up, w_down,
):
    rows, width = tokens.shape
    groups = lax.axis_size("mp")
    packs = lax.axis_size("dp")
    gain1, bias1 = norm1_gain[None, :], norm1_bias[None, :]
    exchange = lambda a, shift: lax.ppermute(a, "mp", [(i, i ^ shift) for i in range(groups)])
    w_outputs = [w_output] + [exchange(w_output, shift) for shift in range(1, groups)]
    a1, k, v, qt, kt, vt, cosine, sine = project(
        lengths, tokens, gain1, bias1, w_query, w_key, w_value
    )
    early, mixed_t, lse = attend(lengths, qt, k, vt, 0, EARLY, STEPS)
    early = [early] + [exchange(early, shift) for shift in range(1, groups)]
    mixed, mixed_t, lse = attend(lengths, qt, k, vt, EARLY, STEPS, STEPS, (mixed_t, lse))
    h1, dh1, sums2, mixed_grad, downs, piles = ffn(
        lengths, early, mixed, tokens, cotangent, w_outputs, w_gate, w_up, w_down,
        norm2_gain[None, :], norm2_bias[None, :], STEPS, packs,
    )
    downs[1:4] = [exchange(downs[shift], shift) for shift in range(1, groups)]
    for i, bits in enumerate(PARTNERS):
        perm = [(j, j ^ (2 * bits)) for j in range(packs)]
        piles[2 * i + 1] = lax.ppermute(piles[2 * i + 1], "dp", perm)
    grads, grads_t = attend_back(
        lengths, qt, k, kt, v, mixed_grad, mixed_t, lse, cosine, sine
    )
    *results, norms = last(
        grads, grads_t, a1, tokens, dh1, h1, w_query, w_key, w_value, gain1, sums2, downs, piles, packs
    )
    output, tokens_grad, grad_q, grad_k, grad_v, gate, up, down, proj = hand_out(results)
    own_rows = (rows // groups, width)
    return (
        output.reshape(own_rows),
        tokens_grad.reshape(own_rows),
        grad_q,
        grad_k,
        grad_v,
        proj,
        gate,
        up,
        down,
        norms[0],
        norms[1],
        norms[2],
        norms[3],
    )


def layer_stats(row_values, gain_vec, bias_vec):
    normed, row_scale = norm_rows(row_values)
    return (normed * gain_vec + bias_vec, normed, row_scale)


def layer_back(gradient, normed, row_scale, gain_vec):
    inner_grad = gradient * gain_vec
    centred_grad = inner_grad - jnp.mean(inner_grad, axis=-1, keepdims=True)
    return row_scale * (
        centred_grad - normed * jnp.mean(inner_grad * normed, axis=-1, keepdims=True)
    )


def scatter_rows(partial, axis, dim=0):
    return lax.psum_scatter(
        partial.astype(BF16), axis, scatter_dimension=dim, tiled=True
    ).astype(F32)


def local(
    tokens, lengths, cotangent, norm1_gain, norm1_bias, w_query, w_key, w_value, w_output,
    norm2_gain, norm2_bias, w_gate, w_up, w_down,
):
    row_count, width = tokens.shape
    feats = w_query.shape[1]
    gain1, bias1 = norm1_gain[None, :], norm1_bias[None, :]
    a1, k, v, qt, kt, vt, cosine, sine = project(
        lengths, tokens, gain1, bias1, w_query, w_key, w_value
    )
    mixed, mixed_t, lse = attend(lengths, qt, k, vt, 0, 1, 1)
    mixed = mixed.reshape(row_count, feats)

    share_rows = row_count // lax.axis_size("mp")
    own_start = lax.axis_index("mp") * share_rows
    own = lambda a: lax.dynamic_slice_in_dim(a, own_start, share_rows, 0)
    live_end = row_count - lengths[0, lengths.shape[1] - 1]
    live = jnp.arange(row_count, dtype=jnp.int32)[:, None] < live_end
    out_grad = jnp.where(live, cotangent, jnp.zeros_like(cotangent))

    attn_rows = scatter_rows(mm(mixed, w_output), "mp")
    residual = own(tokens).astype(F32) + attn_rows
    normed_second, hat_second, scale_second = layer_stats(residual, norm2_gain, norm2_bias)
    inputs_second = lax.all_gather(normed_second.astype(BF16), "mp", axis=0, tiled=True)
    gate_pre = mm(inputs_second, w_gate)
    up_proj = mm(inputs_second, w_up)
    gate_sig = jax.nn.sigmoid(gate_pre)
    gate_act = gate_pre * gate_sig
    hidden = (gate_act * up_proj).astype(BF16)
    output_own = residual + scatter_rows(mm(hidden, w_down), "mp")
    down_w_grad = mm_tn(hidden, out_grad)
    hidden_grad = mm_nt(out_grad, w_down)
    gate_in_grad = (hidden_grad * up_proj * gate_sig * (1.0 + gate_pre * (1.0 - gate_sig))).astype(BF16)
    up_in_grad = (hidden_grad * gate_act).astype(BF16)
    gate_w_grad = mm_tn(inputs_second, gate_in_grad)
    up_w_grad = mm_tn(inputs_second, up_in_grad)
    ffn_sums = (
        scatter_rows(gate_w_grad, "dp"),
        scatter_rows(up_w_grad, "dp"),
        scatter_rows(down_w_grad, "dp", 1),
    )
    second_grad = scatter_rows(mm_nt(gate_in_grad, w_gate) + mm_nt(up_in_grad, w_up), "mp")
    residual_grad = own(out_grad).astype(F32) + layer_back(
        second_grad, hat_second, scale_second, norm2_gain
    )
    attn_grad = lax.all_gather(residual_grad.astype(BF16), "mp", axis=0, tiled=True)
    gain_second_grad = jnp.sum(second_grad * hat_second, axis=0)
    bias_second_grad = jnp.sum(second_grad, axis=0)
    output_w_grad = mm_tn(mixed, attn_grad)
    mixed_grad = mm_nt(attn_grad, w_output).astype(BF16)

    grads, grads_t = attend_back(
        lengths, qt, k, kt, v, mixed_grad, mixed_t, lse, cosine, sine
    )
    w_qkv = jnp.concatenate([w_query, w_key, w_value], axis=1)
    qkv_w_grad = mm(grads_t, a1)
    first_grad = scatter_rows(mm_nt(grads, w_qkv), "mp")
    hat_own, scale_own = norm_rows(own(tokens).astype(F32))
    tokens_grad = (residual_grad + layer_back(first_grad, hat_own, scale_own, norm1_gain)).astype(BF16)
    gain_parts = jnp.stack(
        [
            jnp.sum(first_grad * hat_own, axis=0),
            jnp.sum(first_grad, axis=0),
            gain_second_grad,
            bias_second_grad,
        ]
    )
    gain_parts = scatter_rows(lax.psum(gain_parts, "mp"), "dp", 1)
    attn_sums = scatter_rows(jnp.concatenate([qkv_w_grad, output_w_grad], axis=0), "dp", 1)
    return (
        output_own.astype(BF16),
        tokens_grad,
        attn_sums[:feats].T,
        attn_sums[feats : 2 * feats].T,
        attn_sums[2 * feats : 3 * feats].T,
        attn_sums[3 * feats :],
        ffn_sums[0],
        ffn_sums[1],
        ffn_sums[2],
        gain_parts[0],
        gain_parts[1],
        gain_parts[2],
        gain_parts[3],
    )


def solution(mesh):
    square = mesh.shape["mp"] == 4 and mesh.shape["dp"] == 2 * CHIPS
    rows, weight_in, weight_out = P("dp", None), P(None, "mp"), P("mp", None)
    row_out = P(("dp", "mp"), None)
    return jax.shard_map(
        local_square if square else local,
        mesh=mesh,
        in_specs=(rows, rows, rows, P(), P(), weight_in, weight_in, weight_in, weight_out)
        + (P(), P(), weight_in, weight_in, weight_out),
        out_specs=(row_out, row_out)
        + (P("dp", "mp"),) * 3
        + (P("mp", "dp"), P("dp", "mp"), P("dp", "mp"), P("mp", "dp"))
        + (P("dp"),) * 4,
        check_vma=False,
    )
```

time: 1190 us -> 275 us (0.23)
  matrix products: 471 us -> 0 us
  waiting for transfers between devices: 374 us -> 5.96 us
  Pallas kernels: 0 us -> 252 us
  other arithmetic: 200 us -> 0 us
  local copies, waits for them, and re-layouts: 87.4 us -> 1.37 us
  blocking collectives: 28.9 us -> 0 us
  between operations: 15.5 us -> 0.92 us
  starting transfers between devices: 0.79 us -> 14.3 us
    dot_general x56 -> x0, matrix products: 471 us -> none  [the longest x10 84.6 us: block_scores(): jnp.einsum('qhd,khd->hqk', query_block, keys_split, preferred_element_typ...]
    reduce_scatter x9 -> x0, waiting for transfers between devices: 284 us -> none  [the longest x1 61.2 us: local(): lax.psum_scatter(first_partial.astype(jnp.bfloat16), 'mp', scatter_dimens...]
    pallas_call x0 -> x7, Pallas kernels: none -> 252 us  [the longest x1 105 us: ffn(): pl.pallas_call(functools.partial(ffn_kernel, packs), in_specs=[SMEM] + [A...]
    convert_element_type x26 -> x0, other arithmetic: 119 us -> none  [the longest x5 78.8 us: one_block(): score_grad = (attn_prob * (prob_grad - row_delta)).astype(jnp.bfloat16)]
    all_gather x2 -> x0, waiting for transfers between devices: 90.2 us -> none  [the longest x1 61.5 us: local(): lax.all_gather(normed_second.astype(jnp.bfloat16), 'mp', axis=0, tiled=True)]
    while x13 -> x0, local copies, waits for them, and re-layouts: 44.7 us -> none
    reduce_sum x12 -> x0, other arithmetic: 43.7 us -> none  [the longest x5 28.8 us: one_block(): row_total = jnp.sum(exp_scores, axis=-1, keepdims=True)]
    mul x5 -> x0, other arithmetic: 18.8 us -> none  [the longest x1 7.84 us: layer_stats(): normed = centred * row_scale]
  transfers between devices with their start and end apart: 13 -> 11, of which waited for: 9 -> 3; matrix products, arithmetic and copies ran while one was open for 42% -> 0% of each run, Pallas kernels for 0% -> 32%
where the time goes in v1:
time: 275 us
  Pallas kernels  252 us (92%)
  starting transfers between devices  14.3 us (5%)
  waiting for transfers between devices  5.96 us (2%)
    pallas_call x1, Pallas kernels, ffn(): pl.pallas_call(functools.partial(ffn_kernel, packs), in_specs=[SMEM] + [A...  105 us
    pallas_call x1, Pallas kernels, last(): pl.pallas_call(functools.partial(last_kernel, packs), in_specs=[ANY] * 4...  56.6 us
    pallas_call x1, Pallas kernels, attend_back(): pl.pallas_call(attend_back_kernel, in_specs=[SMEM] + [VMEM] * 9, out_spec...  44.8 us
    pallas_call x2, Pallas kernels, attend(): pl.pallas_call(functools.partial(attend_kernel, begin, steps), in_specs=[...  30 us
    pallas_call x1, Pallas kernels, project(): pl.pallas_call(qkv_kernel, grid=(rows // block,), in_specs=[SMEM, by_row(...  12.4 us
    ppermute x9, starting transfers between devices, local_square(): lax.ppermute(a, 'mp', [(i, i ^ shift) for i in range(groups)])  11.6 us
  transfers between devices with their start and end apart: 11, of which 3 were waited for; matrix products, arithmetic and copies ran while one was open for 0% of the time, Pallas kernels for 32%

profile of v1, /device:TPU:0, one launch (start us, length us, event | category | flops | bytes accessed | tf_op | source)
XLA Modules:
  0.0 274.9 jit_solution(8207961186699902983)
XLA Ops:
  0.6 3.0 %collective-permute-start.4 = (bf16[256,1024]{1,0:T(8,128)(2,1)}, bf16[256,1024]{1,0:T(8,128)(2,1)S(1)}, u32[]{:S(2)}, u32[]{:S(2)}) collective-permute-start(bf16[256,1024]{1,0:T(8,128)(2,1)} %wo0.1), channel_id=1, source_target_pairs={{0,2},{1,3},{2,0},{3,1},{4,6},{5,7},{6,4},{7,5},{8,10},{9,11},{10,... | collective-permute-start | bytes 1572872 | tf_op jit(solution)/shard_map/ppermute | solution.py:1268
  3.7 1.5 collective-permute-start.3
  5.2 0.1 collective-permute-start.5
  5.2 12.4 %qkv.1 = (bf16[2560,1024]{1,0:T(8,128)(2,1)}, bf16[2560,256]{1,0:T(8,128)(2,1)}, bf16[2560,256]{1,0:T(8,128)(2,1)}, bf16[256,2560]{1,0:T(8,128)(2,1)}, bf16[256,...) custom-call(s32[1,9]{1,0:T(1,128)} %len_ref.9, ...), custom_call_target="tpu_custom_call" | custom-call | flops 4026531840 | bytes 20971520 | tf_op jit(solution)/shard_map/qkv/pallas_call | solution.py:120
  17.6 11.6 %attend.2 = (bf16[4,2,128,256]{3,2,1,0:T(8,128)(2,1)}, bf16[256,2560]{1,0:T(8,128)(2,1)}, f32[20,2,256]{2,1,0:T(2,128)}) custom-call(s32[1,9]{1,0:T(1,128)} %len_ref.9, bf16[256,2560]{1,0:T(8,128)(2,1)} %get-tuple-element.61.qt_ref, bf16[2560,256]{1,0:T(8,128)(2,1)} %get-tuple-element.62.k_ref, bf16[256,2560]{1,0:T(8,128)(2,1)} %get-tuple-element.65.vt_ref), custom_call_target="tpu_custom_call" | custom-call | flops 5368709120 | bytes 6553600 | tf_op jit(solution)/shard_map/attend/pallas_call | solution.py:290
  29.3 2.9 %collective-permute-start.2 = (bf16[4,2,128,256]{3,2,1,0:T(8,128)(2,1)}, bf16[4,2,128,256]{3,2,1,0:T(8,128)(2,1)}, u32[]{:S(2)}, u32[]{:S(2)}) collective-permute-start(bf16[4,2,128,256]{3,2,1,0:T(8,128)(2,1)} %get-tuple-element.66.early0), channel_id=1, source_target_pairs={{0,3},{1,2},{2,1},{3,0},{4,7},{5,6},{6,5},{7,4},{8,11},{9,10},{10,... | collective-permute-start | bytes 1572872 | tf_op jit(solution)/shard_map/ppermute | solution.py:1268
  32.1 0.5 collective-permute-start.1
  32.7 0.0 collective-permute-done.4.wo2
  32.7 0.1 collective-permute-start
  32.8 18.3 %attend.3 = (bf16[4,3,128,256]{3,2,1,0:T(8,128)(2,1)}, bf16[256,2560]{1,0:T(8,128)(2,1)}, f32[20,2,256]{2,1,0:T(2,128)}) custom-call(s32[1,9]{1,0:T(1,128)} %len_ref.9, bf16[256,2560]{1,0:T(8,128)(2,1)} %get-tuple-element.61.qt_ref, bf16[2560,256]{1,0:T(8,128)(2,1)} %get-tuple-element.62.k_ref, bf16[256,2560]{1,0:T(8,128)(2,1)} %get-tuple-element.65.vt_ref, ...), custom_call_target="tpu_custom_call" | custom-call | flops 8053063680 | bytes 6553600 | tf_op jit(solution)/shard_map/attend/pallas_call | solution.py:290
  51.1 0.0 copy-done.1
  51.1 0.0 collective-permute-done.3.wo1
  51.1 0.0 copy-start.2
  51.1 0.0 collective-permute-done.5.wo3
  51.1 0.0 collective-permute-done.2.early3
  51.2 4.2 %collective-permute-done.1.early2 = bf16[4,2,128,256]{3,2,1,0:T(8,128)(2,1)} collective-permute-done((bf16[4,2,128,256]{3,2,1,0:T(8,128)(2,1)}, bf16[4,2,128,256]{3,2,1,0:T(8,128)(2,1)}, u32[]{:S(2)}, u32[]{:S(2)}) %collective-permute-start.1) | collective-permute-done | bytes 524320 | tf_op jit(solution)/shard_map/ppermute | solution.py:1268
  55.3 0.2 collective-permute-done.early1
  55.6 104.9 %ffn.1 = (f32[5,128,1024]{2,1,0:T(8,128)}, f32[5,128,1024]{2,1,0:T(8,128)}, f32[2,1024]{1,0:T(2,128)}, bf16[4,5,128,256]{3,2,1,0:T(8,128)(2,1)}, bf16[4,512,1024...) custom-call(s32[1,9]{1,0:T(1,128)} %len_ref.9, ...), custom_call_target="tpu_custom_call" | custom-call | flops 53687091200 | bytes 36700160 | tf_op jit(solution)/shard_map/ffn/pallas_call | solution.py:905
  160.5 0.7 collective-permute-start.6
  161.2 1.4 collective-permute-start.7
  162.6 1.5 collective-permute-start.8
  164.0 2.2 collective-permute-start.9
  166.2 0.5 collective-permute-start.10
  166.7 44.8 %attend_back.1 = (bf16[2560,768]{1,0:T(8,128)(2,1)}, bf16[768,2560]{1,0:T(8,128)(2,1)}) custom-call(s32[1,9]{1,0:T(1,128)} %len_ref.9, bf16[256,2560]{1,0:T(8,128)(2,1)} %get-tuple-element.61.qt_ref, bf16[2560,256]{1,0:T(8,128)(2,1)} %get-tuple-element.62.k_ref, bf16[256,2560]{1,0:T(8,128)(2,1)} %get-tuple-element.63.kt_ref, ...), custom_call_target="tpu_custom_call" | custom-call | flops 16777216000 | bytes 18350080 | tf_op jit(solution)/shard_map/attend_back/pallas_call | solution.py:396
  211.5 0.0 collective-permute-done.6.rest_1_
  211.6 0.0 collective-permute-done.7.rest_2_
  211.6 0.0 collective-permute-done.8.rest_3_
  211.6 0.0 collective-permute-done.9.rest_6_
  211.6 1.5 collective-permute-done.10.rest_8_
  213.1 56.6 %last.1 = (bf16[5,128,1024]{2,1,0:T(8,128)(2,1)}, bf16[5,128,1024]{2,1,0:T(8,128)(2,1)}, f32[128,256]{1,0:T(8,128)}, f32[128,256]{1,0:T(8,128)}, f32[128,256]{1,...) custom-call(bf16[4,5,128,768]{3,2,1,0:T(8,128)(2,1)} %bitcast.20, ...), custom_call_target="tpu_custom_call" | custom-call | flops 8053063680 | bytes 52428800 | tf_op jit(solution)/shard_map/last/pallas_call | solution.py:1174
  269.7 1.4 slice_bitcast_fusion
  271.1 3.6 %hand_out.1 = (bf16[5,128,1024]{2,1,0:T(8,128)(2,1)}, bf16[5,128,1024]{2,1,0:T(8,128)(2,1)}, f32[128,256]{1,0:T(8,128)}, f32[128,256]{1,0:T(8,128)}, f32[128,256...) custom-call(bf16[5,128,1024]{2,1,0:T(8,128)(2,1)} %get-tuple-element.90.re, ...), custom_call_target="tpu_custom_call" | custom-call | tf_op jit(solution)/shard_map/hand_out/pallas_call | solution.py:1248
  (6 shorter events, 0.0 us)
Async XLA Ops:
  0.6 32.0 %collective-permute-start.4 = (bf16[256,1024]{1,0:T(8,128)(2,1)}, bf16[256,1024]{1,0:T(8,128)(2,1)S(1)}, u32[]{:S(2)}, u32[]{:S(2)}) collective-permute-start(bf16[256,1024]{1,0:T(8,128)(2,1)} %wo0.1), channel_id=1, source_target_pairs={{0,2},{1,3},{2,0},{3,1},{4,6},{5,7},{6,4},{7,5},{8,10},{9,11},{10,... | collective-permute-start | bytes 1572872 | tf_op jit(solution)/shard_map/ppermute | solution.py:1268
  3.7 47.4 %collective-permute-start.3 = (bf16[256,1024]{1,0:T(8,128)(2,1)}, bf16[256,1024]{1,0:T(8,128)(2,1)S(1)}, u32[]{:S(2)}, u32[]{:S(2)}) collective-permute-start(bf16[256,1024]{1,0:T(8,128)(2,1)} %wo0.1), channel_id=1, source_target_pairs={{0,1},{1,0},{2,3},{3,2},{4,5},{5,4},{6,7},{7,6},{8,9},{9,8},{10,11... | collective-permute-start | bytes 1572872 | tf_op jit(solution)/shard_map/ppermute | solution.py:1268
  5.2 46.0 %collective-permute-start.5 = (bf16[256,1024]{1,0:T(8,128)(2,1)}, bf16[256,1024]{1,0:T(8,128)(2,1)S(1)}, u32[]{:S(2)}, u32[]{:S(2)}) collective-permute-start(bf16[256,1024]{1,0:T(8,128)(2,1)} %wo0.1), channel_id=1, source_target_pairs={{0,3},{1,2},{2,1},{3,0},{4,7},{5,6},{6,5},{7,4},{8,11},{9,10},{10,... | collective-permute-start | bytes 1572872 | tf_op jit(solution)/shard_map/ppermute | solution.py:1268
  29.3 21.9 %collective-permute-start.2 = (bf16[4,2,128,256]{3,2,1,0:T(8,128)(2,1)}, bf16[4,2,128,256]{3,2,1,0:T(8,128)(2,1)}, u32[]{:S(2)}, u32[]{:S(2)}) collective-permute-start(bf16[4,2,128,256]{3,2,1,0:T(8,128)(2,1)} %get-tuple-element.66.early0), channel_id=1, source_target_pairs={{0,3},{1,2},{2,1},{3,0},{4,7},{5,6},{6,5},{7,4},{8,11},{9,10},{10,... | collective-permute-start | bytes 1572872 | tf_op jit(solution)/shard_map/ppermute | solution.py:1268
  32.1 23.2 %collective-permute-start.1 = (bf16[4,2,128,256]{3,2,1,0:T(8,128)(2,1)}, bf16[4,2,128,256]{3,2,1,0:T(8,128)(2,1)}, u32[]{:S(2)}, u32[]{:S(2)}) collective-permute-start(bf16[4,2,128,256]{3,2,1,0:T(8,128)(2,1)} %get-tuple-element.66.early0), channel_id=1, source_target_pairs={{0,2},{1,3},{2,0},{3,1},{4,6},{5,7},{6,4},{7,5},{8,10},{9,11},{10,... | collective-permute-start | bytes 1572872 | tf_op jit(solution)/shard_map/ppermute | solution.py:1268
  32.7 18.4 %copy-start.1 = (bf16[256,1024]{1,0:T(8,128)(2,1)}, bf16[256,1024]{1,0:T(8,128)(2,1)S(1)}, u32[]{:S(2)}) copy-start(bf16[256,1024]{1,0:T(8,128)(2,1)S(1)} %collective-permute-done.4.wo2) | copy-start | bytes 1572868
  32.7 22.9 %collective-permute-start = (bf16[4,2,128,256]{3,2,1,0:T(8,128)(2,1)}, bf16[4,2,128,256]{3,2,1,0:T(8,128)(2,1)}, u32[]{:S(2)}, u32[]{:S(2)}) collective-permute-start(bf16[4,2,128,256]{3,2,1,0:T(8,128)(2,1)} %get-tuple-element.66.early0), channel_id=1, source_target_pairs={{0,1},{1,0},{2,3},{3,2},{4,5},{5,4},{6,7},{7,6},{8,9},{9,8},{10,11... | collective-permute-start | bytes 1572872 | tf_op jit(solution)/shard_map/ppermute | solution.py:1268
  51.1 4.5 %copy-start.2 = (bf16[256,1024]{1,0:T(8,128)(2,1)}, bf16[256,1024]{1,0:T(8,128)(2,1)S(1)}, u32[]{:S(2)}) copy-start(bf16[256,1024]{1,0:T(8,128)(2,1)S(1)} %collective-permute-done.3.wo1) | copy-start | bytes 1572868
  51.1 4.4 %copy-start.3 = (bf16[256,1024]{1,0:T(8,128)(2,1)}, bf16[256,1024]{1,0:T(8,128)(2,1)S(1)}, u32[]{:S(2)}) copy-start(bf16[256,1024]{1,0:T(8,128)(2,1)S(1)} %collective-permute-done.5.wo3) | copy-start | bytes 1572868
  160.5 51.1 %collective-permute-start.6 = (bf16[4,128,1024]{2,1,0:T(8,128)(2,1)}, bf16[4,128,1024]{2,1,0:T(8,128)(2,1)S(1)}, u32[]{:S(2)}, u32[]{:S(2)}) collective-permute-start(bf16[4,128,1024]{2,1,0:T(8,128)(2,1)} %get-tuple-element.82), channel_id=1, source_target_pairs={{0,1},{1,0},{2,3},{3,2},{4,5},{5,4},{6,7},{7,6},{8,9},{9,8},{10,11... | collective-permute-start | bytes 3145736 | tf_op jit(solution)/shard_map/ppermute | solution.py:1268
  161.2 50.3 %collective-permute-start.7 = (bf16[4,128,1024]{2,1,0:T(8,128)(2,1)}, bf16[4,128,1024]{2,1,0:T(8,128)(2,1)}, u32[]{:S(2)}, u32[]{:S(2)}) collective-permute-start(bf16[4,128,1024]{2,1,0:T(8,128)(2,1)} %get-tuple-element.83), channel_id=1, source_target_pairs={{0,2},{1,3},{2,0},{3,1},{4,6},{5,7},{6,4},{7,5},{8,10},{9,11},{10,... | collective-permute-start | bytes 3145736 | tf_op jit(solution)/shard_map/ppermute | solution.py:1268
  162.6 49.0 %collective-permute-start.8 = (bf16[4,128,1024]{2,1,0:T(8,128)(2,1)}, bf16[4,128,1024]{2,1,0:T(8,128)(2,1)}, u32[]{:S(2)}, u32[]{:S(2)}) collective-permute-start(bf16[4,128,1024]{2,1,0:T(8,128)(2,1)} %get-tuple-element.84), channel_id=1, source_target_pairs={{0,3},{1,2},{2,1},{3,0},{4,7},{5,6},{6,5},{7,4},{8,11},{9,10},{10,... | collective-permute-start | bytes 3145736 | tf_op jit(solution)/shard_map/ppermute | solution.py:1268
  164.0 47.6 %collective-permute-start.9 = (bf16[2,2,128,1024]{3,2,1,0:T(8,128)(2,1)}, bf16[2,2,128,1024]{3,2,1,0:T(8,128)(2,1)}, u32[]{:S(2)}, u32[]{:S(2)}) collective-permute-start(bf16[2,2,128,1024]{3,2,1,0:T(8,128)(2,1)} %get-tuple-element.87), channel_id=1, source_target_pairs={{0,8},{4,12},{8,0},{12,4},{16,24},{20,28},{24,16},{28,20},{1,9},{5... | collective-permute-start | bytes 3145736 | tf_op jit(solution)/shard_map/ppermute | solution.py:1283
  166.2 46.9 %collective-permute-start.10 = (bf16[2,2,128,1024]{3,2,1,0:T(8,128)(2,1)}, bf16[2,2,128,1024]{3,2,1,0:T(8,128)(2,1)}, u32[]{:S(2)}, u32[]{:S(2)}) collective-permute-start(bf16[2,2,128,1024]{3,2,1,0:T(8,128)(2,1)} %get-tuple-element.89), channel_id=1, source_target_pairs={{0,16},{4,20},{8,24},{12,28},{16,0},{20,4},{24,8},{28,12},{1,17},{... | collective-permute-start | bytes 3145736 | tf_op jit(solution)/shard_map/ppermute | solution.py:1283
  211.6 1.6 copy-start

commit v2 on v1

--- a/solution.py
+++ b/solution.py
@@ -25,8 +25,7 @@
 MESH = pl.DeviceIdType.MESH
 STEPS = 5
 EARLY = 2
-PIECES = 4
-DIRECT = 1
+TILE = 256
 VMEM_CAP = 62 << 20
 F32 = jnp.float32
 BF16 = jnp.bfloat16
@@ -207,7 +206,11 @@
 def attend_kernel(begin, steps, len_ref, qt_ref, k_ref, vt_ref, *rest):
     if begin > 0:
         ot_before, lse_before, *rest = rest
-    o_ref, ot_ref, lse_ref, sched, window, diag, stat, acc, keep_buf, score_buf, prob_buf = rest
+    o_ref, *rest = rest
+    first_ref = None
+    if begin == 0 and steps > 1:
+        first_ref, *rest = rest
+    ot_ref, lse_ref, sched, window, diag, stat, acc, keep_buf, score_buf, prob_buf = rest
     if begin > 0:
         ot_ref[...] = ot_before[...]
         lse_ref[...] = lse_before[...]
@@ -271,7 +274,14 @@
             mixed = jnp.concatenate([mixed[:, :QB], mixed[:, QB:]], axis=0).astype(BF16)
             lse_ref[index, p : p + 1] = top + jnp.log(total)
             ot_ref[feat[p], cols] = mixed
-            o_ref[turn // taken, lax.rem(turn, taken), :, feat[p]] = mixed.T
+            mixed = mixed.T
+            o_ref[turn // taken, lax.rem(turn, taken), :, feat[p]] = mixed
+            if first_ref is not None:
+
+                @pl.when(lax.rem(turn, taken) == 0)
+                def _():
+                    first_ref[turn // taken, 0, :, feat[p]] = mixed
+
         return 0
 
     lax.fori_loop(0, owners * taken, finish, 0)
@@ -287,12 +297,16 @@
     owners = rows // (steps * QB)
     share = (end - begin) / steps
     blocks = owners * (end - begin)
+    first = []
+    if begin == 0 and steps > 1:
+        first = [jax.ShapeDtypeStruct((owners, 1, QB, feats), BF16)]
     return pl.pallas_call(
         functools.partial(attend_kernel, begin, steps),
         in_specs=[SMEM] + [VMEM] * (3 + len(before)),
-        out_specs=[VMEM, VMEM, VMEM],
-        out_shape=[
-            jax.ShapeDtypeStruct((owners, end - begin, QB, feats), BF16),
+        out_specs=[VMEM] * (3 + len(first)),
+        out_shape=[jax.ShapeDtypeStruct((owners, end - begin, QB, feats), BF16)]
+        + first
+        + [
             jax.ShapeDtypeStruct((feats, rows), BF16),
             jax.ShapeDtypeStruct((rows // QB, pairs, 2 * QB), F32),
         ],
@@ -533,7 +547,7 @@
     piles = rest[: len(PILES)]
     (
         wo, wg, wu, wd, o_all, tok, cot, h1_all, hid, dgate, dup, part, from_x, from_y, last_x, last_y,
-        a2_all, acc, stage, do_own, db_own, load_sem, tok_sem, cot_sem, own_sem, early_sem, stage_sem, put_sem, pile_sem,
+        a2_t, eb_t, acc, stage, do_own, db_own, load_sem, tok_sem, cot_sem, own_sem, early_sem, stage_sem, put_sem, pile_sem,
         core_send, core_recv, send_sem, recv_sem,
     ) = rest[len(PILES) :]
     core, chip, other_core, _ = pack_neighbours(packs)
@@ -541,9 +555,9 @@
     share = width // packs
     feats = o_hbm.shape[-1]
     size = owners * block
-    cut = dgate.shape[-1] // PIECES
+    tiles = [pl.ds(at, TILE) for at in range(0, width, TILE)]
     early = early0.shape[1]
-    some = owners // 2
+    some = owners
     sems = (send_sem, recv_sem)
     me, x, y, d = neighbours()
     row_total = owners * steps * block
@@ -572,6 +586,7 @@
             for i, (source, group) in enumerate(
                 ((early0, me), (early1, x), (early2, y), (early3, d))
             )
+            if step < source.shape[1]
         ]
 
     def own_copy(step):
@@ -604,7 +619,7 @@
     outgoing = (hid, dgate, dup)
 
     def to_core(kind):
-        source = outgoing[kind] if kind < 3 else stage.at[0].reshape(size, width)
+        source = outgoing[kind] if kind < 3 else stage.at[steps % 2].reshape(size, width)
         return remote_pack(
             source, land_hbm.at[kind], core_send.at[kind], core_recv.at[kind], other_core
         )
@@ -646,12 +661,11 @@
         for copy in pile_copies(kind):
             copy.start()
 
-    def put_rows(step):
+    def put_rows():
+        slot = (steps - 1) % 2
         return [
-            remote(
-                stage.at[lax.rem(step, 2), target], rows_hbm.at[i, step], sems, 13 + i, step, target
-            )
-            for i, target in enumerate((x, y, d))
+            remote(stage.at[slot, target], rows_hbm.at[i], sems, 13 + i, 0, target)
+            for i, target in enumerate((x, y))
         ]
 
     def put_do(step):
@@ -697,10 +711,21 @@
         def _():
             relay(step + 1)
 
-        @pl.when(step < early)
-        def _():
-            for copy in early_copies(step):
-                copy.wait()
+        for which in range(early):
+
+            @pl.when(step == which)
+            def _():
+                if which == 0:
+                    for copy in early_copies(0):
+                        copy.wait()
+                    for after in range(1, early):
+                        for copy in early_copies(after):
+                            copy.wait()
+                        for copy in gather_relay(after):
+                            copy.start()
+                else:
+                    for copy in gather_relay(which):
+                        copy.wait_recv()
 
         @pl.when((step < steps) & (step >= early))
         def _():
@@ -713,32 +738,44 @@
             for copy in fetch(step):
                 copy.wait()
             def some_rows(turn, _):
-                who, rows = pl.ds(turn * some, some), pl.ds(turn * some * block, some * block)
+                count = some * block
+                who = pl.ds(turn * some, some)
+                rows = pl.ds(pl.multiple_of(turn * count, count), count)
                 position = lax.broadcasted_iota(jnp.int32, (some, block, 1), 1) + step * block
                 position = position + (steps * block) * (
                     lax.broadcasted_iota(jnp.int32, (some, block, 1), 0) + turn * some
                 )
                 eb = jnp.where(position < live_end, cot[slot, who].astype(F32), 0.0).astype(BF16)
                 cot[slot, who] = eb
-                eb = eb.reshape(some * block, width)
-                mixed = mm(o_all[step, who].reshape(some * block, width), wo[...])
-                h1 = tok[slot, who].reshape(some * block, width).astype(F32) + mixed
-                h1_all[who] = h1.reshape(some, block, width)
-                hat, _ = norm_rows(h1)
+                eb = eb.reshape(count, width)
+                mixed = o_all[step, who].reshape(count, width)
+                for cols in tiles:
+                    h1 = tok[slot, who, :, cols].reshape(count, TILE).astype(F32)
+                    h1 = h1 + mm(mixed, wo[:, cols])
+                    h1_all[who, :, cols] = h1.reshape(some, block, TILE)
+                hat, _ = norm_rows(h1_all[who].reshape(count, width))
                 a2 = (hat * gain_ref[...] + bias_ref[...]).astype(BF16)
-                a2_all[rows] = a2
-                for piece in range(PIECES):
-                    cols = pl.ds(piece * cut, cut)
-                    gate = mm(a2, wg[:, cols])
-                    up = mm(a2, wu[:, cols])
-                    back = mm_nt(eb, wd[cols, :])
+
+                def products(cols):
+                    return mm(a2, wg[:, cols]), mm(a2, wu[:, cols]), mm_nt(eb, wd[cols, :])
+
+                def hidden(cols, gate, up, back):
                     sig = 0.5 * jnp.tanh(0.5 * gate) + 0.5
                     act = gate * sig
                     hid[rows, cols] = (act * up).astype(BF16)
                     dgate[rows, cols] = (back * up * (sig + act * (1.0 - sig))).astype(BF16)
                     dup[rows, cols] = (back * act).astype(BF16)
-                dc = mm_nt(dgate[rows, :], wg[...]) + mm_nt(dup[rows, :], wu[...])
-                part[now, who] = dc.astype(BF16).reshape(some, 2, block // 2, width)
+
+                ready = products(tiles[0])
+                a2_t[:, rows] = a2.T
+                eb_t[:, rows] = eb.T
+                for cols, ahead in zip(tiles, tiles[1:] + [None]):
+                    coming = products(ahead) if ahead is not None else None
+                    hidden(cols, *ready)
+                    ready = coming
+                for cols in tiles:
+                    dc = mm_nt(dgate[rows, :], wg[cols, :]) + mm_nt(dup[rows, :], wu[cols, :])
+                    part[now, who, :, :, cols] = dc.astype(BF16).reshape(some, 2, block // 2, TILE)
                 return 0
 
             lax.fori_loop(0, owners // some, some_rows, 0)
@@ -772,52 +809,57 @@
             sum_kind(1)
             sum_kind(2)
 
-        def stage_copies(at, direct):
+        def stage_copies(at, final):
             slot = lax.rem(at, 2)
-            places = [(me, down0_hbm.at[at])]
-            if not direct:
-                places += [(x, down1_hbm), (y, down2_hbm), (d, down3_hbm)]
-                places[1:] = [(who, out.at[at - DIRECT]) for who, out in places[1:]]
+            places = [(me, down0_hbm), (d, down3_hbm)]
+            if not final:
+                places += [(x, down1_hbm), (y, down2_hbm)]
             return [
-                pltpu.make_async_copy(stage.at[slot, who], out, stage_sem.at[i, slot])
+                pltpu.make_async_copy(stage.at[slot, who], out.at[at], stage_sem.at[i, slot])
                 for i, (who, out) in enumerate(places)
             ]
 
         @pl.when(step < steps)
         def _():
-            @pl.when((step >= 2) & (step - 2 < DIRECT))
-            def _():
-                for copy in stage_copies(step - 2, True):
-                    copy.wait()
-                for copy in put_rows(step - 2):
-                    copy.wait_send()
-
-            @pl.when((step >= 2) & (step - 2 >= DIRECT))
+            @pl.when(step >= 2)
             def _():
                 for copy in stage_copies(step - 2, False):
                     copy.wait()
 
-            stage[slot] = mm(hid[...], wd[...]).astype(BF16).reshape(owners, block, width)
-
-            @pl.when(step < DIRECT)
-            def _():
-                for copy in stage_copies(step, True) + put_rows(step):
-                    copy.start()
-
-            @pl.when(step >= DIRECT)
+            def some_output(turn, _):
+                count = some * block
+                who = pl.ds(turn * some, some)
+                rows = pl.ds(pl.multiple_of(turn * count, count), count)
+                for cols in tiles:
+                    partial = mm(hid[rows, :], wd[:, cols]).astype(BF16)
+                    stage[slot, who, :, cols] = partial.reshape(some, block, TILE)
+                return 0
+
+            lax.fori_loop(0, owners // some, some_output, 0)
+
+            @pl.when(step < steps - 1)
             def _():
                 for copy in stage_copies(step, False):
                     copy.start()
 
-            a2_t = a2_all[...].T
-            eb_t = cot[slot].reshape(size, width).T
-            acc[0] += mm(a2_t, dgate[...])
-            acc[1] += mm(a2_t, dup[...])
-            acc[2] += mm(eb_t, hid[...])
+            @pl.when(step == steps - 1)
+            def _():
+                for copy in stage_copies(step, True):
+                    copy.start()
+
+            def some_grads(turn, _):
+                rows = pl.ds(pl.multiple_of(turn * size, size), size)
+                for cols in tiles:
+                    acc[0, rows, cols] += mm(a2_t[rows, :], dgate[:, cols])
+                    acc[1, rows, cols] += mm(a2_t[rows, :], dup[:, cols])
+                    acc[2, rows, cols] += mm(eb_t[rows, :], hid[:, cols])
+                return 0
+
+            lax.fori_loop(0, width // size, some_grads, 0)
 
         @pl.when(step == steps)
         def _():
-            for copy in stage_copies(steps - 2, False) + stage_copies(steps - 1, False):
+            for copy in stage_copies(steps - 2, False) + stage_copies(steps - 1, True):
                 copy.wait()
 
         @pl.when(step >= 2)
@@ -842,6 +884,11 @@
                 copy.start()
             keep_do(prev).start()
 
+        @pl.when(step == steps)
+        def _():
+            for copy in put_rows():
+                copy.start()
+
         return 0
 
     lax.fori_loop(0, steps + 2, step_body, 0)
@@ -856,7 +903,7 @@
         ]
         values = mm_tn(jnp.concatenate(columns, axis=1), o_mine)
         if turn == 0:
-            stage[0] = values.astype(BF16).reshape(owners, block, width)
+            stage[steps % 2] = values.astype(BF16).reshape(owners, block, width)
             to_core(3).start()
         else:
             h1_all[...] = values.reshape(owners, block, width)
@@ -869,6 +916,10 @@
     for copy in pile_copies(2) + pile_copies(3):
         copy.wait()
 
+    for step in range(1, early):
+        for copy in gather_relay(step):
+            copy.wait_send()
+
     def sent(step, _):
         for copy in gather_own(step) + gather_relay(step):
             copy.wait_send()
@@ -876,9 +927,8 @@
 
     lax.fori_loop(early, steps, sent, 0)
 
-    for step in range(DIRECT):
-        for copy in put_rows(step):
-            copy.wait_recv()
+    for copy in put_rows():
+        copy.wait()
 
     def finish(step, _):
         for copy in put_do(step):
@@ -913,9 +963,10 @@
             jax.ShapeDtypeStruct((owners, steps, block, feats), BF16),
             jax.ShapeDtypeStruct((4, size, width), BF16),
         ]
-        + [jax.ShapeDtypeStruct((steps, block, width), BF16)]
-        + [jax.ShapeDtypeStruct((steps - DIRECT, block, width), BF16)] * 3
-        + [jax.ShapeDtypeStruct((3, DIRECT, block, width), BF16)]
+        + [
+            jax.ShapeDtypeStruct((taken, block, width), BF16)
+            for taken in (steps, steps - 1, steps - 1, steps, 2)
+        ]
         + [jax.ShapeDtypeStruct((2, 2, width // packs, width), BF16)] * len(PILES),
         scratch_shapes=[
             pltpu.VMEM((width, width), BF16),
@@ -934,7 +985,8 @@
             pltpu.VMEM(half, BF16),
             pltpu.VMEM((steps, block // 2, width), BF16),
             pltpu.VMEM((steps, block // 2, width), BF16),
-            pltpu.VMEM((size, width), BF16),
+            pltpu.VMEM((width, size), BF16),
+            pltpu.VMEM((width, size), BF16),
             pltpu.VMEM((3, width, hidden), F32),
             pltpu.VMEM((2, owners, block, width), BF16),
             pltpu.VMEM((steps, owners, block, feats), BF16),
@@ -949,8 +1001,8 @@
             dma((2, chips)),
             dma((4,)),
             dma((4,)),
-            dma((16, steps)),
-            dma((16, steps)),
+            dma((15, steps)),
+            dma((15, steps)),
         ],
         compiler_params=pltpu.CompilerParams(
             collective_id=0, has_side_effects=True, vmem_limit_bytes=VMEM_CAP
@@ -969,7 +1021,8 @@
     downs, rest = rest[:5], rest[5:]
     piles, rest = rest[: len(PILES)], rest[len(PILES) :]
     (
-        out_ref, tg_ref, gq_ref, gk_ref, gv_ref, gate_ref, up_ref, down_ref, proj_ref, norm_ref,
+        out_hbm, tg_hbm, gq_hbm, gk_hbm, gv_hbm, gate_hbm, up_hbm, down_hbm, proj_hbm, norm_ref,
+        out_ref, tg_ref, gq_ref, gk_ref, gv_ref, gate_ref, up_ref, down_ref, proj_ref, row_sem, result_sem,
         grad, grad_t, a1, tok, part, from_x, from_y, last_x, last_y, h1, down, pile, pile_out, pile_in, sums1,
         full, core_out, core_in, chip_out, chip_in, proj_out, proj_in, norm_out, norm_in,
         grad_sem, tok_sem, load_sem, core_send, core_recv, chip_send, chip_recv, pile_send, pile_recv,
@@ -992,9 +1045,9 @@
 
     later = [(grad_t_hbm, grad_t), (a1_hbm, a1)]
     later += [(piles[i], pile.at[i]) for i in range(len(PILES))]
-    later += [(h1_hbm, h1), (downs[0], down.at[0])]
-    later += [(downs[i], down.at[i, pl.ds(DIRECT, steps - DIRECT)]) for i in range(1, 4)]
-    later += [(downs[4], down.at[pl.ds(1, 3), pl.ds(0, DIRECT)])]
+    later += [(h1_hbm, h1)]
+    later += [(downs[i], down.at[i, pl.ds(0, downs[i].shape[0])]) for i in range(4)]
+    later += [(downs[4], down.at[pl.ds(1, 2), steps - 1])]
     later = [pltpu.make_async_copy(a, b, load_sem.at[i]) for i, (a, b) in enumerate(later)]
 
     def to_core():
@@ -1108,6 +1161,21 @@
                 for copy in proj_copies():
                     copy.start()
 
+    def row_copies(step):
+        return [
+            pltpu.make_async_copy(source.at[step], out.at[step], row_sem.at[i, step])
+            for i, (source, out) in enumerate(((out_ref, out_hbm), (tg_ref, tg_hbm)))
+        ]
+
+    results = (
+        (gq_ref, gq_hbm), (gk_ref, gk_hbm), (gv_ref, gv_hbm), (gate_ref, gate_hbm),
+        (up_ref, up_hbm), (down_ref, down_hbm), (proj_ref, proj_hbm),
+    )
+    results = [
+        pltpu.make_async_copy(source, out, result_sem.at[i])
+        for i, (source, out) in enumerate(results)
+    ]
+
     def finish(step):
         da = scatter_last(part, step, from_x, from_y, last_x, last_y, sems, 0, step)
         hat, scale = norm_rows(tok[step, me].astype(F32))
@@ -1116,6 +1184,7 @@
             inner * hat, axis=-1, keepdims=True
         )
         tg_ref[step] = (dh1_ref[step] + scale * inner).astype(BF16)
+        row_copies(step)[1].start()
 
     def second(step, _):
         scatter_middle(part, step, from_x, from_y, last_x, last_y, sems, 0, step)
@@ -1123,6 +1192,7 @@
         for i in range(4):
             total = total + down[i, step].astype(F32)
         out_ref[step] = total.astype(BF16)
+        row_copies(step)[0].start()
         return 0
 
     def third(step, _):
@@ -1131,6 +1201,8 @@
 
     lax.fori_loop(0, steps, second, 0)
     sum_piles()
+    for copy in results[3:6]:
+        copy.start()
     lax.fori_loop(0, steps - 2, third, 0)
     total = chip_out[chip].astype(F32)
     for i, copy in enumerate(to_chips()):
@@ -1142,17 +1214,24 @@
     finish(steps - 2)
     for kind, ref in enumerate((gq_ref, gk_ref, gv_ref)):
         ref[...] = total[kind * feats : (kind + 1) * feats].T
+        results[kind].start()
     total = proj_out[me].astype(F32)
     for i, copy in enumerate(proj_copies()):
         copy.wait_recv()
         total = total + proj_in[i].astype(F32)
     proj_ref[...] = total.T
+    results[6].start()
     finish(steps - 1)
     total = norm_out[...]
     for i, copy in enumerate(norm_copies()):
         copy.wait_recv()
         total = total + norm_in[i]
     norm_ref[...] = total
+    for copy in results:
+        copy.wait()
+    for step in range(steps):
+        for copy in row_copies(step):
+            copy.wait()
     for copy in [to_core()] + to_chips() + pile_copies() + proj_copies() + norm_copies():
         copy.wait_send()
 
@@ -1171,14 +1250,17 @@
     dma = pltpu.SemaphoreType.DMA
     own = jax.ShapeDtypeStruct((steps, block, width), BF16)
     f32 = lambda *shape: jax.ShapeDtypeStruct(shape, F32)
+    out_shape = [own, own] + [f32(share, feats)] * 3
+    out_shape += [f32(share, hidden)] * 2 + [f32(hidden, share), f32(feats, share), f32(8, share)]
     return pl.pallas_call(
         functools.partial(last_kernel, packs),
         in_specs=[ANY] * 4 + [VMEM, ANY] + [VMEM] * 5 + [ANY] * (5 + len(piles)),
-        out_specs=[VMEM] * 10,
-        out_shape=[own, own]
-        + [f32(share, feats)] * 3
-        + [f32(share, hidden), f32(share, hidden), f32(hidden, share), f32(feats, share), f32(8, share)],
-        scratch_shapes=[
+        out_specs=[ANY] * 9 + [VMEM],
+        out_shape=out_shape,
+        scratch_shapes=[pltpu.VMEM(a.shape, a.dtype) for a in out_shape[:9]]
+        + [
+            dma((2, steps)),
+            dma((7,)),
             pltpu.VMEM((steps, owners, block, 3 * feats), BF16),
             pltpu.VMEM((3 * feats, rows), BF16),
             pltpu.VMEM((rows, width), BF16),
@@ -1230,12 +1312,15 @@
 
 
 def hand_out_kernel(count, *refs):
-    sources, outs, held = refs[:count], refs[count : 2 * count], refs[2 * count : 3 * count]
-    in_sem, out_sem = refs[3 * count :]
+    sources, norm_ref, refs = refs[:count], refs[count], refs[count + 1 :]
+    outs, norms, held = refs[:count], refs[count : count + 4], refs[count + 4 : 2 * count + 4]
+    in_sem, out_sem = refs[2 * count + 4 :]
     loads = [pltpu.make_async_copy(sources[i], held[i], in_sem.at[i]) for i in range(count)]
     stores = [pltpu.make_async_copy(held[i], outs[i], out_sem.at[i]) for i in range(count)]
     for copy in loads:
         copy.start()
+    for i, norm in enumerate(norms):
+        norm[...] = norm_ref[i]
     for load, store in zip(loads, stores):
         load.wait()
         store.start()
@@ -1243,18 +1328,19 @@
         store.wait()
 
 
-def hand_out(arrays):
+def hand_out(arrays, norms):
     count = len(arrays)
+    shape = lambda a: jax.ShapeDtypeStruct(a.shape, a.dtype)
     return pl.pallas_call(
         functools.partial(hand_out_kernel, count),
-        in_specs=[ANY] * count,
-        out_specs=[ANY] * count,
-        out_shape=[jax.ShapeDtypeStruct(a.shape, a.dtype) for a in arrays],
+        in_specs=[ANY] * count + [VMEM],
+        out_specs=[ANY] * count + [VMEM] * 4,
+        out_shape=[shape(a) for a in arrays] + [jax.ShapeDtypeStruct(norms.shape[1:], F32)] * 4,
         scratch_shapes=[pltpu.VMEM(a.shape, a.dtype) for a in arrays]
         + [pltpu.SemaphoreType.DMA((count,))] * 2,
         compiler_params=pltpu.CompilerParams(vmem_limit_bytes=VMEM_CAP),
         name="hand_out",
-    )(*arrays)
+    )(*arrays, norms)
 
 
 def local_square(
@@ -1270,9 +1356,10 @@
     a1, k, v, qt, kt, vt, cosine, sine = project(
         lengths, tokens, gain1, bias1, w_query, w_key, w_value
     )
-    early, mixed_t, lse = attend(lengths, qt, k, vt, 0, EARLY, STEPS)
-    early = [early] + [exchange(early, shift) for shift in range(1, groups)]
-    mixed, mixed_t, lse = attend(lengths, qt, k, vt, EARLY, STEPS, STEPS, (mixed_t, lse))
+    early, early_first, mixed_t, lse = attend(lengths, qt, k, vt, 0, EARLY, STEPS)
+    early = [early, exchange(early, 1), exchange(early, 2), exchange(early_first, 3)]
+    qt_late, *w_outputs = lax.optimization_barrier((qt, *w_outputs))
+    mixed, mixed_t, lse = attend(lengths, qt_late, k, vt, EARLY, STEPS, STEPS, (mixed_t, lse))
     h1, dh1, sums2, mixed_grad, downs, piles = ffn(
         lengths, early, mixed, tokens, cotangent, w_outputs, w_gate, w_up, w_down,
         norm2_gain[None, :], norm2_bias[None, :], STEPS, packs,
@@ -1287,7 +1374,9 @@
     *results, norms = last(
         grads, grads_t, a1, tokens, dh1, h1, w_query, w_key, w_value, gain1, sums2, downs, piles, packs
     )
-    output, tokens_grad, grad_q, grad_k, grad_v, gate, up, down, proj = hand_out(results)
+    output, tokens_grad, grad_q, grad_k, grad_v, gate, up, down, proj, *sums = hand_out(
+        results, norms
+    )
     own_rows = (rows // groups, width)
     return (
         output.reshape(own_rows),
@@ -1299,10 +1388,7 @@
         gate,
         up,
         down,
-        norms[0],
-        norms[1],
-        norms[2],
-        norms[3],
+        *sums,
     )
 
 

time: 275 us -> 275 us (level)
  waiting for transfers between devices: 5.96 us -> 1.49 us
  Pallas kernels: 252 us -> 255 us
    ppermute x9, waiting for transfers between devices: 4.43 us -> 1.48 us  [local_square(): lax.ppermute(a, 'mp', [(i, i ^ shift) for i in range(groups)])]
  transfers between devices with their start and end apart: 11 -> 11, of which waited for: 3 -> 1; matrix products, arithmetic and copies ran while one was open for 0% -> 0% of each run, Pallas kernels for 32% -> 32%
where the time goes in v2:
time: 275 us; the launch traced here: 274 us
  Pallas kernels  255 us (93%)
  starting transfers between devices  14.7 us (5%)
    pallas_call x1, Pallas kernels, ffn(): pl.pallas_call(functools.partial(ffn_kernel, packs), in_specs=[SMEM] + [A...  104 us
    pallas_call x1, Pallas kernels, last(): pl.pallas_call(functools.partial(last_kernel, packs), in_specs=[ANY] * 4...  57.7 us
    pallas_call x1, Pallas kernels, attend_back(): pl.pallas_call(attend_back_kernel, in_specs=[SMEM] + [VMEM] * 9, out_spec...  45.4 us
    pallas_call x2, Pallas kernels, attend(): pl.pallas_call(functools.partial(attend_kernel, begin, steps), in_specs=[...  31.2 us
    pallas_call x1, Pallas kernels, project(): pl.pallas_call(qkv_kernel, grid=(rows // block,), in_specs=[SMEM, by_row(...  12.4 us
    ppermute x9, starting transfers between devices, local_square(): lax.ppermute(a, 'mp', [(i, i ^ shift) for i in range(groups)])  11.6 us
  transfers between devices with their start and end apart: 11, of which 1 were waited for; matrix products, arithmetic and copies ran while one was open for 0% of the time, Pallas kernels for 32%

profile of v2, /device:TPU:0, one launch (start us, length us, event | category | flops | bytes accessed | tf_op | source)
XLA Modules:
  0.0 274.3 jit_solution(11271815796447509618)
XLA Ops:
  0.6 3.0 %collective-permute-start.4 = (bf16[256,1024]{1,0:T(8,128)(2,1)}, bf16[256,1024]{1,0:T(8,128)(2,1)S(1)}, u32[]{:S(2)}, u32[]{:S(2)}) collective-permute-start(bf16[256,1024]{1,0:T(8,128)(2,1)} %wo0), channel_id=1, source_target_pairs={{0,2},{1,3},{2,0},{3,1},{4,6},{5,7},{6,4},{7,5},{8,10},{9,11},{10,... | collective-permute-start | bytes 1572872 | tf_op jit(solution)/shard_map/ppermute | solution.py:1354
  3.7 1.5 collective-permute-start.3
  5.2 0.1 collective-permute-start.5
  5.2 12.4 %qkv.1 = (bf16[2560,1024]{1,0:T(8,128)(2,1)}, bf16[2560,256]{1,0:T(8,128)(2,1)}, bf16[2560,256]{1,0:T(8,128)(2,1)}, bf16[256,2560]{1,0:T(8,128)(2,1)}, bf16[256,...) custom-call(s32[1,9]{1,0:T(1,128)} %len_ref.9, ...), custom_call_target="tpu_custom_call" | custom-call | flops 4026531840 | bytes 20971520 | tf_op jit(solution)/shard_map/qkv/pallas_call | solution.py:119
  17.6 12.5 %attend.2 = (bf16[4,2,128,256]{3,2,1,0:T(8,128)(2,1)}, bf16[4,1,128,256]{3,2,1,0:T(8,128)(2,1)}, bf16[256,2560]{1,0:T(8,128)(2,1)}, f32[20,2,256]{2,1,0:T(2,128)}) custom-call(s32[1,9]{1,0:T(1,128)} %len_ref.9, bf16[256,2560]{1,0:T(8,128)(2,1)} %get-tuple-element.78.qt_ref, bf16[2560,256]{1,0:T(8,128)(2,1)} %get-tuple-element.72.k_ref, ...), custom_call_target="tpu_custom_call" | custom-call | flops 5368709120 | bytes 6553600 | tf_op jit(solution)/shard_map/attend/pallas_call | solution.py:303
  30.1 1.9 collective-permute-start.1
  32.1 1.5 collective-permute-start
  33.5 0.0 collective-permute-done.4.wo2
  33.6 0.1 collective-permute-start.2
  33.6 0.0 collective-permute-done.3.wo1
  33.6 0.0 collective-permute-done.5.wo3
  33.6 18.7 %attend.3 = (bf16[4,3,128,256]{3,2,1,0:T(8,128)(2,1)}, bf16[256,2560]{1,0:T(8,128)(2,1)}, f32[20,2,256]{2,1,0:T(2,128)}) custom-call(s32[1,9]{1,0:T(1,128)} %len_ref.9, bf16[256,2560]{1,0:T(8,128)(2,1)} %get-tuple-element.78.qt_ref, bf16[2560,256]{1,0:T(8,128)(2,1)} %get-tuple-element.72.k_ref, bf16[256,2560]{1,0:T(8,128)(2,1)} %get-tuple-element.75.vt_ref, ...), custom_call_target="tpu_custom_call" | custom-call | flops 8053063680 | bytes 6553600 | tf_op jit(solution)/shard_map/attend/pallas_call | solution.py:303
  52.3 0.0 copy-done.1
  52.3 0.0 collective-permute-done.2.early3
  52.4 0.0 collective-permute-done.1.early2
  52.4 0.0 collective-permute-done.early1
  52.4 0.7 copy-done.4
  53.0 103.9 %ffn.1 = (f32[5,128,1024]{2,1,0:T(8,128)}, f32[5,128,1024]{2,1,0:T(8,128)}, f32[2,1024]{1,0:T(2,128)}, bf16[4,5,128,256]{3,2,1,0:T(8,128)(2,1)}, bf16[4,512,1024...) custom-call(s32[1,9]{1,0:T(1,128)} %len_ref.9, ...), custom_call_target="tpu_custom_call" | custom-call | flops 53687091200 | bytes 36700160 | tf_op jit(solution)/shard_map/ffn/pallas_call | solution.py:955
  156.9 0.5 collective-permute-start.6
  157.4 1.5 collective-permute-start.7
  158.9 1.9 collective-permute-start.9
  160.7 1.3 collective-permute-start.10
  162.0 1.6 collective-permute-start.8
  163.6 45.4 %attend_back.1 = (bf16[2560,768]{1,0:T(8,128)(2,1)}, bf16[768,2560]{1,0:T(8,128)(2,1)}) custom-call(s32[1,9]{1,0:T(1,128)} %len_ref.9, bf16[256,2560]{1,0:T(8,128)(2,1)} %get-tuple-element.78.qt_ref, bf16[2560,256]{1,0:T(8,128)(2,1)} %get-tuple-element.72.k_ref, bf16[256,2560]{1,0:T(8,128)(2,1)} %get-tuple-element.73.kt_ref, ...), custom_call_target="tpu_custom_call" | custom-call | flops 16777216000 | bytes 18350080 | tf_op jit(solution)/shard_map/attend_back/pallas_call | solution.py:410
  209.0 0.0 collective-permute-done.6.rest_1_
  209.0 0.0 collective-permute-done.7.rest_2_
  209.0 0.0 collective-permute-done.9.rest_6_
  209.0 0.0 collective-permute-done.10.rest_8_
  209.0 1.5 collective-permute-done.8.rest_3_
  210.4 1.1 copy-done
  211.5 57.7 %last.1 = (bf16[5,128,1024]{2,1,0:T(8,128)(2,1)}, bf16[5,128,1024]{2,1,0:T(8,128)(2,1)}, f32[128,256]{1,0:T(8,128)}, f32[128,256]{1,0:T(8,128)}, f32[128,256]{1,...) custom-call(bf16[4,5,128,768]{3,2,1,0:T(8,128)(2,1)} %bitcast.12, ...), custom_call_target="tpu_custom_call" | custom-call | flops 8053063680 | bytes 52428800 | tf_op jit(solution)/shard_map/last/pallas_call | solution.py:1255
  269.3 4.9 %hand_out.1 = (bf16[5,128,1024]{2,1,0:T(8,128)(2,1)}, bf16[5,128,1024]{2,1,0:T(8,128)(2,1)}, f32[128,256]{1,0:T(8,128)}, f32[128,256]{1,0:T(8,128)}, f32[128,256...) custom-call(bf16[5,128,1024]{2,1,0:T(8,128)(2,1)} %get-tuple-element, ...), custom_call_target="tpu_custom_call" | custom-call | tf_op jit(solution)/shard_map/hand_out/pallas_call | solution.py:1334
  (7 shorter events, 0.0 us)
Async XLA Ops:
  0.6 32.9 %collective-permute-start.4 = (bf16[256,1024]{1,0:T(8,128)(2,1)}, bf16[256,1024]{1,0:T(8,128)(2,1)S(1)}, u32[]{:S(2)}, u32[]{:S(2)}) collective-permute-start(bf16[256,1024]{1,0:T(8,128)(2,1)} %wo0), channel_id=1, source_target_pairs={{0,2},{1,3},{2,0},{3,1},{4,6},{5,7},{6,4},{7,5},{8,10},{9,11},{10,... | collective-permute-start | bytes 1572872 | tf_op jit(solution)/shard_map/ppermute | solution.py:1354
  3.7 29.9 %collective-permute-start.3 = (bf16[256,1024]{1,0:T(8,128)(2,1)}, bf16[256,1024]{1,0:T(8,128)(2,1)S(1)}, u32[]{:S(2)}, u32[]{:S(2)}) collective-permute-start(bf16[256,1024]{1,0:T(8,128)(2,1)} %wo0), channel_id=1, source_target_pairs={{0,1},{1,0},{2,3},{3,2},{4,5},{5,4},{6,7},{7,6},{8,9},{9,8},{10,11... | collective-permute-start | bytes 1572872 | tf_op jit(solution)/shard_map/ppermute | solution.py:1354
  5.2 28.4 %collective-permute-start.5 = (bf16[256,1024]{1,0:T(8,128)(2,1)}, bf16[256,1024]{1,0:T(8,128)(2,1)S(1)}, u32[]{:S(2)}, u32[]{:S(2)}) collective-permute-start(bf16[256,1024]{1,0:T(8,128)(2,1)} %wo0), channel_id=1, source_target_pairs={{0,3},{1,2},{2,1},{3,0},{4,7},{5,6},{6,5},{7,4},{8,11},{9,10},{10,... | collective-permute-start | bytes 1572872 | tf_op jit(solution)/shard_map/ppermute | solution.py:1354
  30.1 22.3 %collective-permute-start.1 = (bf16[4,2,128,256]{3,2,1,0:T(8,128)(2,1)}, bf16[4,2,128,256]{3,2,1,0:T(8,128)(2,1)}, u32[]{:S(2)}, u32[]{:S(2)}) collective-permute-start(bf16[4,2,128,256]{3,2,1,0:T(8,128)(2,1)} %get-tuple-element.76.early0), channel_id=1, source_target_pairs={{0,2},{1,3},{2,0},{3,1},{4,6},{5,7},{6,4},{7,5},{8,10},{9,11},{10,... | collective-permute-start | bytes 1572872 | tf_op jit(solution)/shard_map/ppermute | solution.py:1354
  32.1 20.3 %collective-permute-start = (bf16[4,2,128,256]{3,2,1,0:T(8,128)(2,1)}, bf16[4,2,128,256]{3,2,1,0:T(8,128)(2,1)}, u32[]{:S(2)}, u32[]{:S(2)}) collective-permute-start(bf16[4,2,128,256]{3,2,1,0:T(8,128)(2,1)} %get-tuple-element.76.early0), channel_id=1, source_target_pairs={{0,1},{1,0},{2,3},{3,2},{4,5},{5,4},{6,7},{7,6},{8,9},{9,8},{10,11... | collective-permute-start | bytes 1572872 | tf_op jit(solution)/shard_map/ppermute | solution.py:1354
  33.6 18.8 %copy-start.1 = (bf16[256,1024]{1,0:T(8,128)(2,1)}, bf16[256,1024]{1,0:T(8,128)(2,1)S(1)}, u32[]{:S(2)}) copy-start(bf16[256,1024]{1,0:T(8,128)(2,1)S(1)} %collective-permute-done.4.wo2) | copy-start | bytes 1572868
  33.6 18.8 %collective-permute-start.2 = (bf16[4,1,128,256]{3,2,1,0:T(8,128)(2,1)}, bf16[4,1,128,256]{3,2,1,0:T(8,128)(2,1)S(1)}, u32[]{:S(2)}, u32[]{:S(2)}) collective-permute-start(bf16[4,1,128,256]{3,2,1,0:T(8,128)(2,1)} %get-tuple-element.77), channel_id=1, source_target_pairs={{0,3},{1,2},{2,1},{3,0},{4,7},{5,6},{6,5},{7,4},{8,11},{9,10},{10,... | collective-permute-start | bytes 786440 | tf_op jit(solution)/shard_map/ppermute | solution.py:1354
  33.6 18.7 %copy-start.2 = (bf16[256,1024]{1,0:T(8,128)(2,1)}, bf16[256,1024]{1,0:T(8,128)(2,1)S(1)}, u32[]{:S(2)}) copy-start(bf16[256,1024]{1,0:T(8,128)(2,1)S(1)} %collective-permute-done.3.wo1) | copy-start | bytes 1572868
  33.6 18.7 %copy-start.3 = (bf16[256,1024]{1,0:T(8,128)(2,1)}, bf16[256,1024]{1,0:T(8,128)(2,1)S(1)}, u32[]{:S(2)}) copy-start(bf16[256,1024]{1,0:T(8,128)(2,1)S(1)} %collective-permute-done.5.wo3) | copy-start | bytes 1572868
  52.4 0.7 copy-start.4
  156.9 52.0 %collective-permute-start.6 = (bf16[4,128,1024]{2,1,0:T(8,128)(2,1)}, bf16[4,128,1024]{2,1,0:T(8,128)(2,1)}, u32[]{:S(2)}, u32[]{:S(2)}) collective-permute-start(bf16[4,128,1024]{2,1,0:T(8,128)(2,1)} %get-tuple-element.98), channel_id=1, source_target_pairs={{0,1},{1,0},{2,3},{3,2},{4,5},{5,4},{6,7},{7,6},{8,9},{9,8},{10,11... | collective-permute-start | bytes 3145736 | tf_op jit(solution)/shard_map/ppermute | solution.py:1354
  157.4 51.6 %collective-permute-start.7 = (bf16[4,128,1024]{2,1,0:T(8,128)(2,1)}, bf16[4,128,1024]{2,1,0:T(8,128)(2,1)}, u32[]{:S(2)}, u32[]{:S(2)}) collective-permute-start(bf16[4,128,1024]{2,1,0:T(8,128)(2,1)} %get-tuple-element.99), channel_id=1, source_target_pairs={{0,2},{1,3},{2,0},{3,1},{4,6},{5,7},{6,4},{7,5},{8,10},{9,11},{10,... | collective-permute-start | bytes 3145736 | tf_op jit(solution)/shard_map/ppermute | solution.py:1354
  158.9 50.1 %collective-permute-start.9 = (bf16[2,2,128,1024]{3,2,1,0:T(8,128)(2,1)}, bf16[2,2,128,1024]{3,2,1,0:T(8,128)(2,1)}, u32[]{:S(2)}, u32[]{:S(2)}) collective-permute-start(bf16[2,2,128,1024]{3,2,1,0:T(8,128)(2,1)} %get-tuple-element.103), channel_id=1, source_target_pairs={{0,8},{4,12},{8,0},{12,4},{16,24},{20,28},{24,16},{28,20},{1,9},{5... | collective-permute-start | bytes 3145736 | tf_op jit(solution)/shard_map/ppermute | solution.py:1370
  160.7 48.2 %collective-permute-start.10 = (bf16[2,2,128,1024]{3,2,1,0:T(8,128)(2,1)}, bf16[2,2,128,1024]{3,2,1,0:T(8,128)(2,1)}, u32[]{:S(2)}, u32[]{:S(2)}) collective-permute-start(bf16[2,2,128,1024]{3,2,1,0:T(8,128)(2,1)} %get-tuple-element.105), channel_id=1, source_target_pairs={{0,16},{4,20},{8,24},{12,28},{16,0},{20,4},{24,8},{28,12},{1,17},{... | collective-permute-start | bytes 3145736 | tf_op jit(solution)/shard_map/ppermute | solution.py:1370
  162.0 48.4 %collective-permute-start.8 = (bf16[5,128,1024]{2,1,0:T(8,128)(2,1)}, bf16[5,128,1024]{2,1,0:T(8,128)(2,1)S(1)}, u32[]{:S(2)}, u32[]{:S(2)}) collective-permute-start(bf16[5,128,1024]{2,1,0:T(8,128)(2,1)} %get-tuple-element.100), channel_id=1, source_target_pairs={{0,3},{1,2},{2,1},{3,0},{4,7},{5,6},{6,5},{7,4},{8,11},{9,10},{10,... | collective-permute-start | bytes 3932168 | tf_op jit(solution)/shard_map/ppermute | solution.py:1354
  210.4 1.1 copy-start

commit v3 on v2

--- a/solution.py
+++ b/solution.py
@@ -203,14 +203,21 @@
     mix(2 * turns, 1)
 
 
-def attend_kernel(begin, steps, len_ref, qt_ref, k_ref, vt_ref, *rest):
+def attend_kernel(begin, steps, len_ref, qt_ref, k_hbm, vt_hbm, *rest):
     if begin > 0:
         ot_before, lse_before, *rest = rest
     o_ref, *rest = rest
     first_ref = None
     if begin == 0 and steps > 1:
         first_ref, *rest = rest
-    ot_ref, lse_ref, sched, window, diag, stat, acc, keep_buf, score_buf, prob_buf = rest
+    ot_ref, lse_ref, k_ref, vt_ref, load_sem, *rest = rest
+    sched, window, diag, stat, acc, keep_buf, score_buf, prob_buf = rest
+    loads = [
+        pltpu.make_async_copy(k_hbm, k_ref, load_sem.at[0]),
+        pltpu.make_async_copy(vt_hbm, vt_ref, load_sem.at[1]),
+    ]
+    for copy in loads:
+        copy.start()
     if begin > 0:
         ot_ref[...] = ot_before[...]
         lse_ref[...] = lse_before[...]
@@ -235,6 +242,8 @@
 
     lax.fori_loop(0, owners * taken, prepare, 0)
     count = fill_schedule(len_ref, sched, owners * taken, index_of, rows)
+    for copy in loads:
+        copy.wait()
 
     def scores(n, buf):
         turn, keys = sched[0, n], key_rows(sched[1, n], rows)
@@ -302,7 +311,7 @@
         first = [jax.ShapeDtypeStruct((owners, 1, QB, feats), BF16)]
     return pl.pallas_call(
         functools.partial(attend_kernel, begin, steps),
-        in_specs=[SMEM] + [VMEM] * (3 + len(before)),
+        in_specs=[SMEM, VMEM, ANY, ANY] + [VMEM] * len(before),
         out_specs=[VMEM] * (3 + len(first)),
         out_shape=[jax.ShapeDtypeStruct((owners, end - begin, QB, feats), BF16)]
         + first
@@ -311,6 +320,9 @@
             jax.ShapeDtypeStruct((rows // QB, pairs, 2 * QB), F32),
         ],
         scratch_shapes=[
+            pltpu.VMEM((rows, feats), BF16),
+            pltpu.VMEM((feats, rows), BF16),
+            pltpu.SemaphoreType.DMA((2,)),
             pltpu.SMEM((2, schedule_size(blocks)), jnp.int32),
             pltpu.VMEM((blocks, 8, QB), jnp.int32),
             pltpu.VMEM((blocks, pairs, PAIR, 2 * QB), BF16),
@@ -331,13 +343,29 @@
 
 
 def attend_back_kernel(
-    len_ref, qt_ref, k_ref, kt_ref, v_ref, do_ref, ot_ref, lse_ref, cos_ref, sin_ref,
-    grad_ref, grad_t_ref, sched, window, q_diag, do_diag, stat, dq_acc, dk_acc, dv_acc,
+    len_ref, qt_ref, k_hbm, kt_hbm, v_hbm, do_ref, ot_ref, lse_ref, cos_hbm, sin_hbm,
+    grad_hbm, grad_t_hbm, grad_ref, grad_t_ref, k_ref, kt_ref, v_ref, cos_ref, sin_ref, load_sem, out_sem, sched, window, q_diag, do_diag, stat, dq_acc, dk_acc, dv_acc,
     score_buf, prob_grad_buf, prob_buf, score_grad_buf,
 ):
     feats, rows = qt_ref.shape
     pairs = range(feats // PAIR)
     feat = [pl.ds(p * PAIR, PAIR) for p in pairs]
+    loads = (
+        (k_hbm, k_ref), (kt_hbm, kt_ref), (v_hbm, v_ref), (cos_hbm, cos_ref), (sin_hbm, sin_ref),
+    )
+    loads = [pltpu.make_async_copy(a, b, load_sem.at[i]) for i, (a, b) in enumerate(loads)]
+    for copy in loads:
+        copy.start()
+
+    def store(turn):
+        cols = pl.ds(pl.multiple_of(turn * QB, QB), QB)
+        return [
+            pltpu.make_async_copy(grad_ref.at[cols], grad_hbm.at[cols], out_sem.at[0, turn]),
+            pltpu.make_async_copy(
+                grad_t_ref.at[:, cols], grad_t_hbm.at[:, cols], out_sem.at[1, turn]
+            ),
+        ]
+
     dk_acc[...] = jnp.zeros_like(dk_acc)
     dv_acc[...] = jnp.zeros_like(dv_acc)
     dq_acc[...] = jnp.zeros_like(dq_acc)
@@ -357,6 +385,8 @@
 
     lax.fori_loop(0, rows // QB, prepare, 0)
     count = fill_schedule(len_ref, sched, rows // QB, lambda turn: turn, rows)
+    for copy in loads:
+        copy.wait()
 
     def scores(n, buf):
         turn, keys = sched[0, n], key_rows(sched[1, n], rows)
@@ -399,9 +429,18 @@
                 field = field.astype(BF16)
                 grad_t_ref[place, cols] = field
                 grad_ref[cols, place] = field.T
+        for copy in store(turn):
+            copy.start()
         return 0
 
     lax.fori_loop(0, rows // QB, finish, 0)
+
+    def stored(turn, _):
+        for copy in store(turn):
+            copy.wait()
+        return 0
+
+    lax.fori_loop(0, rows // QB, stored, 0)
 
 
 def attend_back(lengths, qt, k, kt, v, do, ot, lse, cosine, sine):
@@ -409,13 +448,22 @@
     blocks = rows // QB
     return pl.pallas_call(
         attend_back_kernel,
-        in_specs=[SMEM] + [VMEM] * 9,
-        out_specs=[VMEM, VMEM],
+        in_specs=[SMEM, VMEM] + [ANY] * 3 + [VMEM] * 3 + [ANY] * 2,
+        out_specs=[ANY, ANY],
         out_shape=[
             jax.ShapeDtypeStruct((rows, 3 * feats), BF16),
             jax.ShapeDtypeStruct((3 * feats, rows), BF16),
         ],
         scratch_shapes=[
+            pltpu.VMEM((rows, 3 * feats), BF16),
+            pltpu.VMEM((3 * feats, rows), BF16),
+            pltpu.VMEM((rows, feats), BF16),
+            pltpu.VMEM((feats, rows), BF16),
+            pltpu.VMEM((rows, feats), BF16),
+            pltpu.VMEM(cosine.shape, F32),
+            pltpu.VMEM(sine.shape, F32),
+            pltpu.SemaphoreType.DMA((5,)),
+            pltpu.SemaphoreType.DMA((2, blocks)),
             pltpu.SMEM((2, schedule_size(blocks)), jnp.int32),
             pltpu.VMEM((blocks, 8, QB), jnp.int32),
             pltpu.VMEM((blocks, feats // PAIR, PAIR, 2 * QB), BF16),
@@ -541,13 +589,13 @@
 def ffn_kernel(
     packs,
     len_ref, early0, early1, early2, early3, o_hbm, tok_hbm, cot_hbm, wo0, wo1, wo2, wo3, wg_hbm, wu_hbm, wd_hbm, gain_ref, bias_ref,
-    h1_ref, dh1_ref, sums_ref, do_hbm, land_hbm, down0_hbm, down1_hbm, down2_hbm, down3_hbm, rows_hbm, *rest,
+    h1_hbm, dh1_hbm, sums_ref, do_hbm, land_hbm, down0_hbm, down1_hbm, down2_hbm, down3_hbm, rows_hbm, *rest,
 ):
     chips = packs // 2
     piles = rest[: len(PILES)]
     (
         wo, wg, wu, wd, o_all, tok, cot, h1_all, hid, dgate, dup, part, from_x, from_y, last_x, last_y,
-        a2_t, eb_t, acc, stage, do_own, db_own, load_sem, tok_sem, cot_sem, own_sem, early_sem, stage_sem, put_sem, pile_sem,
+        a2_t, eb_t, acc, stage, do_own, db_own, h1_ref, dh1_ref, kept_sem, load_sem, tok_sem, cot_sem, own_sem, early_sem, stage_sem, put_sem, pile_sem,
         core_send, core_recv, send_sem, recv_sem,
     ) = rest[len(PILES) :]
     core, chip, other_core, _ = pack_neighbours(packs)
@@ -672,6 +720,12 @@
         return [
             remote(do_own.at[step, target], do_hbm.at[me, step], sems, 10 + i, step, target)
             for i, target in enumerate((x, y, d))
+        ]
+
+    def keep_rows(step):
+        return [
+            pltpu.make_async_copy(source.at[step], out.at[step], kept_sem.at[i, step])
+            for i, (source, out) in enumerate(((h1_ref, h1_hbm), (dh1_ref, dh1_hbm)))
         ]
 
     def keep_do(step):
@@ -875,6 +929,8 @@
             )
             dh1 = dh1_ref[prev] + scale * inner
             dh1_ref[prev] = dh1
+            for copy in keep_rows(prev):
+                copy.start()
             db = dh1.astype(BF16)
             db_own[prev] = db
             back = mm_nt(db, wo[...]).astype(BF16)
@@ -931,7 +987,7 @@
         copy.wait()
 
     def finish(step, _):
-        for copy in put_do(step):
+        for copy in put_do(step) + keep_rows(step):
             copy.wait()
         keep_do(step).wait()
         return 0
@@ -955,7 +1011,7 @@
     h1, dh1, sums, do, _, *rest = pl.pallas_call(
         functools.partial(ffn_kernel, packs),
         in_specs=[SMEM] + [ANY] * 14 + [VMEM, VMEM],
-        out_specs=[VMEM, VMEM, VMEM] + [ANY] * (7 + len(PILES)),
+        out_specs=[ANY, ANY, VMEM] + [ANY] * (7 + len(PILES)),
         out_shape=[
             own,
             own,
@@ -991,6 +1047,9 @@
             pltpu.VMEM((2, owners, block, width), BF16),
             pltpu.VMEM((steps, owners, block, feats), BF16),
             pltpu.VMEM((steps, block, width), BF16),
+            pltpu.VMEM(own.shape, F32),
+            pltpu.VMEM(own.shape, F32),
+            dma((2, steps)),
             dma((7,)),
             dma((2,)),
             dma((2,)),
@@ -1015,7 +1074,7 @@
 
 def last_kernel(
     packs,
-    grad_hbm, grad_t_hbm, a1_hbm, tok_hbm, dh1_ref, h1_hbm, wq_ref, wk_ref, wv_ref, gain_ref, sums2_ref, *rest,
+    grad_hbm, grad_t_hbm, a1_hbm, tok_hbm, dh1_hbm, h1_hbm, wq_hbm, wk_hbm, wv_hbm, gain_ref, sums2_ref, *rest,
 ):
     chips = packs // 2
     downs, rest = rest[:5], rest[5:]
@@ -1023,13 +1082,14 @@
     (
         out_hbm, tg_hbm, gq_hbm, gk_hbm, gv_hbm, gate_hbm, up_hbm, down_hbm, proj_hbm, norm_ref,
         out_ref, tg_ref, gq_ref, gk_ref, gv_ref, gate_ref, up_ref, down_ref, proj_ref, row_sem, result_sem,
+        dh1_ref, wq_ref, wk_ref, wv_ref, weight_sem,
         grad, grad_t, a1, tok, part, from_x, from_y, last_x, last_y, h1, down, pile, pile_out, pile_in, sums1,
         full, core_out, core_in, chip_out, chip_in, proj_out, proj_in, norm_out, norm_in,
         grad_sem, tok_sem, load_sem, core_send, core_recv, chip_send, chip_recv, pile_send, pile_recv,
         small_send, small_recv, send_sem, recv_sem,
     ) = rest
     steps, owners, _, half, width = part.shape
-    feats = wq_ref.shape[1]
+    feats = wq_hbm.shape[1]
     size = owners * 2 * half
     share = width // packs
     tall = 3 * feats
@@ -1089,11 +1149,18 @@
             copy.start()
         return 0
 
+    weights = ((wq_hbm, wq_ref), (wk_hbm, wk_ref), (wv_hbm, wv_ref), (dh1_hbm, dh1_ref))
+    weights = [pltpu.make_async_copy(a, b, weight_sem.at[i]) for i, (a, b) in enumerate(weights)]
+    for copy in weights[:3]:
+        copy.start()
     lax.fori_loop(0, steps, begin, 0)
-    for copy in later:
+    for copy in later + weights[3:]:
         copy.start()
     group_barrier((x, y, d), [other_core] + next_chips)
     sums1[...] = jnp.zeros_like(sums1)
+
+    for copy in weights[:3]:
+        copy.wait()
 
     def first(step, _):
         for copy in fetch(step):
@@ -1199,6 +1266,7 @@
         finish(step)
         return 0
 
+    weights[3].wait()
     lax.fori_loop(0, steps, second, 0)
     sum_piles()
     for copy in results[3:6]:
@@ -1254,13 +1322,18 @@
     out_shape += [f32(share, hidden)] * 2 + [f32(hidden, share), f32(feats, share), f32(8, share)]
     return pl.pallas_call(
         functools.partial(last_kernel, packs),
-        in_specs=[ANY] * 4 + [VMEM, ANY] + [VMEM] * 5 + [ANY] * (5 + len(piles)),
+        in_specs=[ANY] * 9 + [VMEM] * 2 + [ANY] * (5 + len(piles)),
         out_specs=[ANY] * 9 + [VMEM],
         out_shape=out_shape,
         scratch_shapes=[pltpu.VMEM(a.shape, a.dtype) for a in out_shape[:9]]
         + [
             dma((2, steps)),
             dma((7,)),
+            pltpu.VMEM((steps, block, width), F32),
+            pltpu.VMEM((width, feats), BF16),
+            pltpu.VMEM((width, feats), BF16),
+            pltpu.VMEM((width, feats), BF16),
+            dma((4,)),
             pltpu.VMEM((steps, owners, block, 3 * feats), BF16),
             pltpu.VMEM((3 * feats, rows), BF16),
             pltpu.VMEM((rows, width), BF16),
@@ -1312,16 +1385,21 @@
 
 
 def hand_out_kernel(count, *refs):
-    sources, norm_ref, refs = refs[:count], refs[count], refs[count + 1 :]
-    outs, norms, held = refs[:count], refs[count : count + 4], refs[count + 4 : 2 * count + 4]
-    in_sem, out_sem = refs[2 * count + 4 :]
-    loads = [pltpu.make_async_copy(sources[i], held[i], in_sem.at[i]) for i in range(count)]
-    stores = [pltpu.make_async_copy(held[i], outs[i], out_sem.at[i]) for i in range(count)]
-    for copy in loads:
+    sources, outs, held = refs[: count + 1], refs[count + 1 : 2 * count + 5], refs[2 * count + 5 : -2]
+    in_sem, out_sem = refs[-2:]
+    norm, vectors = held[count], held[count + 1 :]
+    loads = [pltpu.make_async_copy(sources[i], held[i], in_sem.at[i]) for i in range(count + 1)]
+    ready = list(held[:count]) + list(vectors)
+    stores = [
+        pltpu.make_async_copy(ready[i], outs[i], out_sem.at[i]) for i in range(count + 4)
+    ]
+    for copy in reversed(loads):
         copy.start()
-    for i, norm in enumerate(norms):
-        norm[...] = norm_ref[i]
-    for load, store in zip(loads, stores):
+    loads[count].wait()
+    for i, vector in enumerate(vectors):
+        vector[...] = norm[i]
+        stores[count + i].start()
+    for load, store in zip(loads[:count], stores):
         load.wait()
         store.start()
     for store in stores:
@@ -1331,13 +1409,15 @@
 def hand_out(arrays, norms):
     count = len(arrays)
     shape = lambda a: jax.ShapeDtypeStruct(a.shape, a.dtype)
+    vectors = [jax.ShapeDtypeStruct(norms.shape[1:], F32)] * 4
+    out_shape = [shape(a) for a in arrays] + vectors
     return pl.pallas_call(
         functools.partial(hand_out_kernel, count),
-        in_specs=[ANY] * count + [VMEM],
-        out_specs=[ANY] * count + [VMEM] * 4,
-        out_shape=[shape(a) for a in arrays] + [jax.ShapeDtypeStruct(norms.shape[1:], F32)] * 4,
-        scratch_shapes=[pltpu.VMEM(a.shape, a.dtype) for a in arrays]
-        + [pltpu.SemaphoreType.DMA((count,))] * 2,
+        in_specs=[ANY] * (count + 1),
+        out_specs=[ANY] * (count + 4),
+        out_shape=out_shape,
+        scratch_shapes=[pltpu.VMEM(a.shape, a.dtype) for a in list(arrays) + [norms] + vectors]
+        + [pltpu.SemaphoreType.DMA((count + 4,))] * 2,
         compiler_params=pltpu.CompilerParams(vmem_limit_bytes=VMEM_CAP),
         name="hand_out",
     )(*arrays, norms)

time: 275 us -> 273 us (level)
  Pallas kernels: 255 us -> 240 us
  waiting for transfers between devices: 1.49 us -> 12 us
  starting transfers between devices: 14.7 us -> 17.7 us
    pallas_call x2, Pallas kernels: 103 us -> 93.7 us  [the longest x1 57.8 us: last(): pl.pallas_call(functools.partial(last_kernel, packs), in_specs=[ANY] * 9...]
    ppermute x2, waiting for transfers between devices: 0.01 us -> 9.26 us  [local_square(): piles[2 * i + 1] = lax.ppermute(piles[2 * i + 1], 'dp', perm)]
    pallas_call x2, Pallas kernels: 31.2 us -> 27.5 us  [attend(): pl.pallas_call(functools.partial(attend_kernel, begin, steps), in_specs=[...]
    ppermute x2, starting transfers between devices: 3.12 us -> 6.22 us  [local_square(): piles[2 * i + 1] = lax.ppermute(piles[2 * i + 1], 'dp', perm)]
  transfers between devices with their start and end apart: 11 -> 11, of which waited for: 1 -> 3; matrix products, arithmetic and copies ran while one was open for 0% -> 0% of each run, Pallas kernels for 32% -> 28%
where the time goes in v3:
time: 273 us; the launch traced here: 272 us
  Pallas kernels  240 us (88%)
  starting transfers between devices  17.7 us (6%)
  waiting for transfers between devices  12 us (4%)
    pallas_call x1, Pallas kernels, ffn(): pl.pallas_call(functools.partial(ffn_kernel, packs), in_specs=[SMEM] + [A...  101 us
    pallas_call x1, Pallas kernels, last(): pl.pallas_call(functools.partial(last_kernel, packs), in_specs=[ANY] * 9...  57.8 us
    pallas_call x1, Pallas kernels, attend_back(): pl.pallas_call(attend_back_kernel, in_specs=[SMEM, VMEM] + [ANY] * 3 + [V...  36 us
    pallas_call x2, Pallas kernels, attend(): pl.pallas_call(functools.partial(attend_kernel, begin, steps), in_specs=[...  27.5 us
    pallas_call x1, Pallas kernels, project(): pl.pallas_call(qkv_kernel, grid=(rows // block,), in_specs=[SMEM, by_row(...  12.4 us
    ppermute x9, starting transfers between devices, local_square(): lax.ppermute(a, 'mp', [(i, i ^ shift) for i in range(groups)])  11.5 us
    ppermute x2, waiting for transfers between devices, local_square(): piles[2 * i + 1] = lax.ppermute(piles[2 * i + 1], 'dp', perm)  9.26 us
    ppermute x2, starting transfers between devices, local_square(): piles[2 * i + 1] = lax.ppermute(piles[2 * i + 1], 'dp', perm)  6.22 us
  transfers between devices with their start and end apart: 11, of which 3 were waited for; matrix products, arithmetic and copies ran while one was open for 0% of the time, Pallas kernels for 28%

profile of v3, /device:TPU:0, one launch (start us, length us, event | category | flops | bytes accessed | tf_op | source)
XLA Modules:
  0.0 272.0 jit_solution(15171411916706821054)
XLA Ops:
  0.6 3.0 %collective-permute-start.4 = (bf16[256,1024]{1,0:T(8,128)(2,1)}, bf16[256,1024]{1,0:T(8,128)(2,1)S(1)}, u32[]{:S(2)}, u32[]{:S(2)}) collective-permute-start(bf16[256,1024]{1,0:T(8,128)(2,1)} %wo0), channel_id=1, source_target_pairs={{0,2},{1,3},{2,0},{3,1},{4,6},{5,7},{6,4},{7,5},{8,10},{9,11},{10,... | collective-permute-start | bytes 1572872 | tf_op jit(solution)/shard_map/ppermute | solution.py:1434
  3.7 1.5 collective-permute-start.3
  5.2 0.1 collective-permute-start.5
  5.2 12.4 %qkv.1 = (bf16[2560,1024]{1,0:T(8,128)(2,1)}, bf16[2560,256]{1,0:T(8,128)(2,1)}, bf16[2560,256]{1,0:T(8,128)(2,1)}, bf16[256,2560]{1,0:T(8,128)(2,1)}, bf16[256,...) custom-call(s32[1,9]{1,0:T(1,128)} %len_ref.9, ...), custom_call_target="tpu_custom_call" | custom-call | flops 4026531840 | bytes 20971520 | tf_op jit(solution)/shard_map/qkv/pallas_call | solution.py:119
  17.6 12.7 %attend.2 = (bf16[4,2,128,256]{3,2,1,0:T(8,128)(2,1)}, bf16[4,1,128,256]{3,2,1,0:T(8,128)(2,1)}, bf16[256,2560]{1,0:T(8,128)(2,1)}, f32[20,2,256]{2,1,0:T(2,128)}) custom-call(s32[1,9]{1,0:T(1,128)} %len_ref.9, bf16[256,2560]{1,0:T(8,128)(2,1)} %get-tuple-element.78.qt_ref, bf16[2560,256]{1,0:T(8,128)(2,1)} %get-tuple-element.72.k_hbm, ...), custom_call_target="tpu_custom_call" | custom-call | flops 5368709120 | bytes 6553600 | tf_op jit(solution)/shard_map/attend/pallas_call | solution.py:312
  30.3 2.0 collective-permute-start.1
  32.3 1.5 collective-permute-start
  33.8 0.0 collective-permute-done.4.wo2
  33.8 0.1 collective-permute-start.2
  33.9 0.0 collective-permute-done.3.wo1
  33.9 0.0 collective-permute-done.5.wo3
  33.9 14.9 %attend.3 = (bf16[4,3,128,256]{3,2,1,0:T(8,128)(2,1)}, bf16[256,2560]{1,0:T(8,128)(2,1)}, f32[20,2,256]{2,1,0:T(2,128)}) custom-call(s32[1,9]{1,0:T(1,128)} %len_ref.9, bf16[256,2560]{1,0:T(8,128)(2,1)} %get-tuple-element.78.qt_ref, bf16[2560,256]{1,0:T(8,128)(2,1)} %get-tuple-element.72.k_hbm, bf16[256,2560]{1,0:T(8,128)(2,1)} %get-tuple-element.75.vt_hbm, ...), custom_call_target="tpu_custom_call" | custom-call | flops 8053063680 | bytes 6553600 | tf_op jit(solution)/shard_map/attend/pallas_call | solution.py:312
  48.8 0.0 copy-done.1
  48.8 2.7 collective-permute-done.2.early3
  51.5 0.0 collective-permute-done.1.early2
  51.5 0.0 collective-permute-done.early1
  51.5 0.7 copy-done.4
  52.2 101.2 %ffn.1 = (f32[5,128,1024]{2,1,0:T(8,128)}, f32[5,128,1024]{2,1,0:T(8,128)}, f32[2,1024]{1,0:T(2,128)}, bf16[4,5,128,256]{3,2,1,0:T(8,128)(2,1)}, bf16[4,512,1024...) custom-call(s32[1,9]{1,0:T(1,128)} %len_ref.9, ...), custom_call_target="tpu_custom_call" | custom-call | flops 53687091200 | bytes 36700160 | tf_op jit(solution)/shard_map/ffn/pallas_call | solution.py:1011
  153.4 1.3 collective-permute-start.6
  154.7 0.6 collective-permute-start.7
  155.3 3.2 %collective-permute-start.9 = (bf16[2,2,128,1024]{3,2,1,0:T(8,128)(2,1)}, bf16[2,2,128,1024]{3,2,1,0:T(8,128)(2,1)}, u32[]{:S(2)}, u32[]{:S(2)}) collective-permute-start(bf16[2,2,128,1024]{3,2,1,0:T(8,128)(2,1)} %get-tuple-element.103), channel_id=1, source_target_pairs={{0,8},{4,12},{8,0},{12,4},{16,24},{20,28},{24,16},{28,20},{1,9},{5... | collective-permute-start | bytes 3145736 | tf_op jit(solution)/shard_map/ppermute | solution.py:1450
  158.5 3.0 %collective-permute-start.10 = (bf16[2,2,128,1024]{3,2,1,0:T(8,128)(2,1)}, bf16[2,2,128,1024]{3,2,1,0:T(8,128)(2,1)}, u32[]{:S(2)}, u32[]{:S(2)}) collective-permute-start(bf16[2,2,128,1024]{3,2,1,0:T(8,128)(2,1)} %get-tuple-element.105), channel_id=1, source_target_pairs={{0,16},{4,20},{8,24},{12,28},{16,0},{20,4},{24,8},{28,12},{1,17},{... | collective-permute-start | bytes 3145736 | tf_op jit(solution)/shard_map/ppermute | solution.py:1450
  161.6 1.4 collective-permute-start.8
  162.9 36.0 %attend_back.1 = (bf16[2560,768]{1,0:T(8,128)(2,1)}, bf16[768,2560]{1,0:T(8,128)(2,1)}) custom-call(s32[1,9]{1,0:T(1,128)} %len_ref.9, bf16[256,2560]{1,0:T(8,128)(2,1)} %get-tuple-element.78.qt_ref, bf16[2560,256]{1,0:T(8,128)(2,1)} %get-tuple-element.72.k_hbm, bf16[256,2560]{1,0:T(8,128)(2,1)} %get-tuple-element.73.kt_hbm, ...), custom_call_target="tpu_custom_call" | custom-call | flops 16777216000 | bytes 18350080 | tf_op jit(solution)/shard_map/attend_back/pallas_call | solution.py:449
  198.9 0.0 collective-permute-done.6.rest_1_
  198.9 0.0 collective-permute-done.7.rest_2_
  199.0 6.0 %collective-permute-done.9.rest_6_ = bf16[2,2,128,1024]{3,2,1,0:T(8,128)(2,1)} collective-permute-done((bf16[2,2,128,1024]{3,2,1,0:T(8,128)(2,1)}, bf16[2,2,128,1024]{3,2,1,0:T(8,128)(2,1)}, u32[]{:S(2)}, u32[]{:S(2)}) %collective-permute-start.9) | collective-permute-done | bytes 1048608 | tf_op jit(solution)/shard_map/ppermute | solution.py:1450
  204.9 3.3 %collective-permute-done.10.rest_8_ = bf16[2,2,128,1024]{3,2,1,0:T(8,128)(2,1)} collective-permute-done((bf16[2,2,128,1024]{3,2,1,0:T(8,128)(2,1)}, bf16[2,2,128,1024]{3,2,1,0:T(8,128)(2,1)}, u32[]{:S(2)}, u32[]{:S(2)}) %collective-permute-start.10) | collective-permute-done | bytes 1048608 | tf_op jit(solution)/shard_map/ppermute | solution.py:1450
  208.2 0.0 collective-permute-done.8.rest_3_
  208.2 1.1 copy-done
  209.3 57.8 %last.1 = (bf16[5,128,1024]{2,1,0:T(8,128)(2,1)}, bf16[5,128,1024]{2,1,0:T(8,128)(2,1)}, f32[128,256]{1,0:T(8,128)}, f32[128,256]{1,0:T(8,128)}, f32[128,256]{1,...) custom-call(bf16[4,5,128,768]{3,2,1,0:T(8,128)(2,1)} %bitcast.12, ...), custom_call_target="tpu_custom_call" | custom-call | flops 8053063680 | bytes 52428800 | tf_op jit(solution)/shard_map/last/pallas_call | solution.py:1323
  267.1 4.8 %hand_out.1 = (bf16[5,128,1024]{2,1,0:T(8,128)(2,1)}, bf16[5,128,1024]{2,1,0:T(8,128)(2,1)}, f32[128,256]{1,0:T(8,128)}, f32[128,256]{1,0:T(8,128)}, f32[128,256...) custom-call(bf16[5,128,1024]{2,1,0:T(8,128)(2,1)} %get-tuple-element, ...), custom_call_target="tpu_custom_call" | custom-call | tf_op jit(solution)/shard_map/hand_out/pallas_call | solution.py:1414
  (7 shorter events, 0.0 us)
Async XLA Ops:
  0.6 33.2 %collective-permute-start.4 = (bf16[256,1024]{1,0:T(8,128)(2,1)}, bf16[256,1024]{1,0:T(8,128)(2,1)S(1)}, u32[]{:S(2)}, u32[]{:S(2)}) collective-permute-start(bf16[256,1024]{1,0:T(8,128)(2,1)} %wo0), channel_id=1, source_target_pairs={{0,2},{1,3},{2,0},{3,1},{4,6},{5,7},{6,4},{7,5},{8,10},{9,11},{10,... | collective-permute-start | bytes 1572872 | tf_op jit(solution)/shard_map/ppermute | solution.py:1434
  3.7 30.2 %collective-permute-start.3 = (bf16[256,1024]{1,0:T(8,128)(2,1)}, bf16[256,1024]{1,0:T(8,128)(2,1)S(1)}, u32[]{:S(2)}, u32[]{:S(2)}) collective-permute-start(bf16[256,1024]{1,0:T(8,128)(2,1)} %wo0), channel_id=1, source_target_pairs={{0,1},{1,0},{2,3},{3,2},{4,5},{5,4},{6,7},{7,6},{8,9},{9,8},{10,11... | collective-permute-start | bytes 1572872 | tf_op jit(solution)/shard_map/ppermute | solution.py:1434
  5.2 28.7 %collective-permute-start.5 = (bf16[256,1024]{1,0:T(8,128)(2,1)}, bf16[256,1024]{1,0:T(8,128)(2,1)S(1)}, u32[]{:S(2)}, u32[]{:S(2)}) collective-permute-start(bf16[256,1024]{1,0:T(8,128)(2,1)} %wo0), channel_id=1, source_target_pairs={{0,3},{1,2},{2,1},{3,0},{4,7},{5,6},{6,5},{7,4},{8,11},{9,10},{10,... | collective-permute-start | bytes 1572872 | tf_op jit(solution)/shard_map/ppermute | solution.py:1434
  30.3 21.2 %collective-permute-start.1 = (bf16[4,2,128,256]{3,2,1,0:T(8,128)(2,1)}, bf16[4,2,128,256]{3,2,1,0:T(8,128)(2,1)}, u32[]{:S(2)}, u32[]{:S(2)}) collective-permute-start(bf16[4,2,128,256]{3,2,1,0:T(8,128)(2,1)} %get-tuple-element.76.early0), channel_id=1, source_target_pairs={{0,2},{1,3},{2,0},{3,1},{4,6},{5,7},{6,4},{7,5},{8,10},{9,11},{10,... | collective-permute-start | bytes 1572872 | tf_op jit(solution)/shard_map/ppermute | solution.py:1434
  32.3 19.2 %collective-permute-start = (bf16[4,2,128,256]{3,2,1,0:T(8,128)(2,1)}, bf16[4,2,128,256]{3,2,1,0:T(8,128)(2,1)}, u32[]{:S(2)}, u32[]{:S(2)}) collective-permute-start(bf16[4,2,128,256]{3,2,1,0:T(8,128)(2,1)} %get-tuple-element.76.early0), channel_id=1, source_target_pairs={{0,1},{1,0},{2,3},{3,2},{4,5},{5,4},{6,7},{7,6},{8,9},{9,8},{10,11... | collective-permute-start | bytes 1572872 | tf_op jit(solution)/shard_map/ppermute | solution.py:1434
  33.8 14.9 %copy-start.1 = (bf16[256,1024]{1,0:T(8,128)(2,1)}, bf16[256,1024]{1,0:T(8,128)(2,1)S(1)}, u32[]{:S(2)}) copy-start(bf16[256,1024]{1,0:T(8,128)(2,1)S(1)} %collective-permute-done.4.wo2) | copy-start | bytes 1572868
  33.8 17.6 %collective-permute-start.2 = (bf16[4,1,128,256]{3,2,1,0:T(8,128)(2,1)}, bf16[4,1,128,256]{3,2,1,0:T(8,128)(2,1)S(1)}, u32[]{:S(2)}, u32[]{:S(2)}) collective-permute-start(bf16[4,1,128,256]{3,2,1,0:T(8,128)(2,1)} %get-tuple-element.77), channel_id=1, source_target_pairs={{0,3},{1,2},{2,1},{3,0},{4,7},{5,6},{6,5},{7,4},{8,11},{9,10},{10,... | collective-permute-start | bytes 786440 | tf_op jit(solution)/shard_map/ppermute | solution.py:1434
  33.9 14.9 %copy-start.2 = (bf16[256,1024]{1,0:T(8,128)(2,1)}, bf16[256,1024]{1,0:T(8,128)(2,1)S(1)}, u32[]{:S(2)}) copy-start(bf16[256,1024]{1,0:T(8,128)(2,1)S(1)} %collective-permute-done.3.wo1) | copy-start | bytes 1572868
  33.9 14.9 %copy-start.3 = (bf16[256,1024]{1,0:T(8,128)(2,1)}, bf16[256,1024]{1,0:T(8,128)(2,1)S(1)}, u32[]{:S(2)}) copy-start(bf16[256,1024]{1,0:T(8,128)(2,1)S(1)} %collective-permute-done.5.wo3) | copy-start | bytes 1572868
  51.5 0.7 copy-start.4
  153.4 45.5 %collective-permute-start.6 = (bf16[4,128,1024]{2,1,0:T(8,128)(2,1)}, bf16[4,128,1024]{2,1,0:T(8,128)(2,1)}, u32[]{:S(2)}, u32[]{:S(2)}) collective-permute-start(bf16[4,128,1024]{2,1,0:T(8,128)(2,1)} %get-tuple-element.98), channel_id=1, source_target_pairs={{0,1},{1,0},{2,3},{3,2},{4,5},{5,4},{6,7},{7,6},{8,9},{9,8},{10,11... | collective-permute-start | bytes 3145736 | tf_op jit(solution)/shard_map/ppermute | solution.py:1434
  154.7 44.3 %collective-permute-start.7 = (bf16[4,128,1024]{2,1,0:T(8,128)(2,1)}, bf16[4,128,1024]{2,1,0:T(8,128)(2,1)}, u32[]{:S(2)}, u32[]{:S(2)}) collective-permute-start(bf16[4,128,1024]{2,1,0:T(8,128)(2,1)} %get-tuple-element.99), channel_id=1, source_target_pairs={{0,2},{1,3},{2,0},{3,1},{4,6},{5,7},{6,4},{7,5},{8,10},{9,11},{10,... | collective-permute-start | bytes 3145736 | tf_op jit(solution)/shard_map/ppermute | solution.py:1434
  155.3 49.6 %collective-permute-start.9 = (bf16[2,2,128,1024]{3,2,1,0:T(8,128)(2,1)}, bf16[2,2,128,1024]{3,2,1,0:T(8,128)(2,1)}, u32[]{:S(2)}, u32[]{:S(2)}) collective-permute-start(bf16[2,2,128,1024]{3,2,1,0:T(8,128)(2,1)} %get-tuple-element.103), channel_id=1, source_target_pairs={{0,8},{4,12},{8,0},{12,4},{16,24},{20,28},{24,16},{28,20},{1,9},{5... | collective-permute-start | bytes 3145736 | tf_op jit(solution)/shard_map/ppermute | solution.py:1450
  158.5 49.7 %collective-permute-start.10 = (bf16[2,2,128,1024]{3,2,1,0:T(8,128)(2,1)}, bf16[2,2,128,1024]{3,2,1,0:T(8,128)(2,1)}, u32[]{:S(2)}, u32[]{:S(2)}) collective-permute-start(bf16[2,2,128,1024]{3,2,1,0:T(8,128)(2,1)} %get-tuple-element.105), channel_id=1, source_target_pairs={{0,16},{4,20},{8,24},{12,28},{16,0},{20,4},{24,8},{28,12},{1,17},{... | collective-permute-start | bytes 3145736 | tf_op jit(solution)/shard_map/ppermute | solution.py:1450
  161.6 46.7 %collective-permute-start.8 = (bf16[5,128,1024]{2,1,0:T(8,128)(2,1)}, bf16[5,128,1024]{2,1,0:T(8,128)(2,1)S(1)}, u32[]{:S(2)}, u32[]{:S(2)}) collective-permute-start(bf16[5,128,1024]{2,1,0:T(8,128)(2,1)} %get-tuple-element.100), channel_id=1, source_target_pairs={{0,3},{1,2},{2,1},{3,0},{4,7},{5,6},{6,5},{7,4},{8,11},{9,10},{10,... | collective-permute-start | bytes 3932168 | tf_op jit(solution)/shard_map/ppermute | solution.py:1434
  208.2 1.1 copy-start

commit v4 on v3

--- a/solution.py
+++ b/solution.py
@@ -86,22 +86,31 @@
     cosine, sine = jnp.cos(theta), jnp.sin(theta)
     cos_ref[...] = cosine
     sin_ref[...] = sine
-    hat, _ = norm_rows(tok_ref[...].astype(F32))
-    a1 = (hat * gain_ref[...] + bias_ref[...]).astype(BF16)
-    a1_ref[...] = a1
-    for w_ref, out_ref, out_t_ref, scale in (
-        (wq_ref, None, qt_ref, SCALE),
-        (wk_ref, k_ref, kt_ref, None),
-    ):
-        field = rotate_t(mm(a1, w_ref[...]).T, cosine, sine, 1.0).astype(BF16)
-        if scale is not None:
-            field = field * jnp.asarray(scale, BF16)
-        out_t_ref[...] = field
-        if out_ref is not None:
-            out_ref[...] = field.T
-    values = mm(a1, wv_ref[...]).astype(BF16)
-    v_ref[...] = values
-    vt_ref[...] = values.T
+    parts = 2
+    part = rows // parts
+    spans = [pl.ds(i * part, part) for i in range(parts)]
+    inputs = []
+    for span in spans:
+        hat, _ = norm_rows(tok_ref[span, :].astype(F32))
+        a1 = (hat * gain_ref[...] + bias_ref[...]).astype(BF16)
+        a1_ref[span, :] = a1
+        inputs.append(a1)
+    for i, (span, a1) in enumerate(zip(spans, inputs)):
+        turn = slice(i * part, (i + 1) * part)
+        for w_ref, out_ref, out_t_ref, scale in (
+            (wq_ref, None, qt_ref, SCALE),
+            (wk_ref, k_ref, kt_ref, None),
+        ):
+            field = mm(a1, w_ref[...]).T
+            field = rotate_t(field, cosine[:, turn], sine[:, turn], 1.0).astype(BF16)
+            if scale is not None:
+                field = field * jnp.asarray(scale, BF16)
+            out_t_ref[:, span] = field
+            if out_ref is not None:
+                out_ref[span, :] = field.T
+        values = mm(a1, wv_ref[...]).astype(BF16)
+        v_ref[span, :] = values
+        vt_ref[:, span] = values.T
 
 
 def project(lengths, tokens, gain, bias, wq, wk, wv):
@@ -186,21 +195,25 @@
     window[turn, 0:1], window[turn, 1:2] = window_bounds(len_ref, position)
 
 
-def run_pipeline(count, scores, soften, mix):
-    def two_pairs(turn, _):
-        n = 1 + 2 * turn
-        mix(n - 1, 1)
-        scores(n + 1, 1)
-        soften(n, 0)
-        mix(n, 0)
-        scores(n + 2, 0)
-        soften(n + 1, 1)
+def run_pipeline(count, pairs, inside, scores, soften, mix):
+    def one_turn(n, buf):
+        mask = inside(n)
+        for p in pairs:
+            mix(n - 1, 1 - buf, p)
+            scores(n + 1, 1 - buf, p)
+            soften(n, buf, p, mask)
+
+    def two_turns(turn, _):
+        one_turn(1 + 2 * turn, 0)
+        one_turn(2 + 2 * turn, 1)
         return 0
 
     turns = (count + 1) // 2
-    scores(1, 0)
-    lax.fori_loop(0, turns, two_pairs, 0)
-    mix(2 * turns, 1)
+    for p in pairs:
+        scores(1, 0, p)
+    lax.fori_loop(0, turns, two_turns, 0)
+    for p in pairs:
+        mix(2 * turns, 1, p)
 
 
 def attend_kernel(begin, steps, len_ref, qt_ref, k_hbm, vt_hbm, *rest):
@@ -245,34 +258,34 @@
     for copy in loads:
         copy.wait()
 
-    def scores(n, buf):
+    def inside(n):
+        turn = sched[0, n]
+        return inside_window(window[turn, 0:1], window[turn, 1:2], sched[1, n], rows)
+
+    def scores(n, buf, p):
         turn, keys = sched[0, n], key_rows(sched[1, n], rows)
-        for p in pairs:
-            score_buf[buf, p] = mm(k_ref[keys, feat[p]], diag[turn, p])
-
-    def soften(n, buf):
+        score_buf[buf, p] = mm(k_ref[keys, feat[p]], diag[turn, p])
+
+    def soften(n, buf, p, mask):
         turn = sched[0, n]
-        inside = inside_window(window[turn, 0:1], window[turn, 1:2], sched[1, n], rows)
-        for p in pairs:
-            top, total = stat[turn, p : p + 1], stat[turn, 4 + p : 5 + p]
-            values = jnp.where(inside, score_buf[buf, p], NEG)
-            new_top = jnp.maximum(top, jnp.max(values, axis=0, keepdims=True))
-            prob = jnp.exp(values - new_top)
-            keep = jnp.exp(top - new_top)
-            stat[turn, p : p + 1] = new_top
-            stat[turn, 4 + p : 5 + p] = keep * total + jnp.sum(prob, axis=0, keepdims=True)
-            keep_buf[buf, p : p + 1] = keep
-            prob_buf[buf, p] = prob.astype(BF16)
-
-    def mix(n, buf):
+        top, total = stat[turn, p : p + 1], stat[turn, 4 + p : 5 + p]
+        values = jnp.where(mask, score_buf[buf, p], NEG)
+        new_top = jnp.maximum(top, jnp.max(values, axis=0, keepdims=True))
+        prob = jnp.exp(values - new_top)
+        keep = jnp.exp(top - new_top)
+        stat[turn, p : p + 1] = new_top
+        stat[turn, 4 + p : 5 + p] = keep * total + jnp.sum(prob, axis=0, keepdims=True)
+        keep_buf[buf, p : p + 1] = keep
+        prob_buf[buf, p] = prob.astype(BF16)
+
+    def mix(n, buf, p):
         turn, keys = sched[0, n], key_rows(sched[1, n], rows)
-        for p in pairs:
-            mixed = diagonal_blocks(mm(vt_ref[feat[p], keys], prob_buf[buf, p]))
-            acc[turn, p] = acc[turn, p] * keep_buf[buf, p : p + 1] + mixed
+        mixed = diagonal_blocks(mm(vt_ref[feat[p], keys], prob_buf[buf, p]))
+        acc[turn, p] = acc[turn, p] * keep_buf[buf, p : p + 1] + mixed
 
     prob_buf[1] = jnp.zeros_like(prob_buf[1])
     keep_buf[1] = jnp.ones_like(keep_buf[1])
-    run_pipeline(count, scores, soften, mix)
+    run_pipeline(count, pairs, inside, scores, soften, mix)
 
     def finish(turn, _):
         index = index_of(turn)
@@ -388,31 +401,31 @@
     for copy in loads:
         copy.wait()
 
-    def scores(n, buf):
+    def inside(n):
+        turn = sched[0, n]
+        return inside_window(window[turn, 0:1], window[turn, 1:2], sched[1, n], rows)
+
+    def scores(n, buf, p):
         turn, keys = sched[0, n], key_rows(sched[1, n], rows)
-        for p in pairs:
-            score_buf[buf, p] = mm(k_ref[keys, feat[p]], q_diag[turn, p])
-            prob_grad_buf[buf, p] = mm(v_ref[keys, feat[p]], do_diag[turn, p])
-
-    def soften(n, buf):
+        score_buf[buf, p] = mm(k_ref[keys, feat[p]], q_diag[turn, p])
+        prob_grad_buf[buf, p] = mm(v_ref[keys, feat[p]], do_diag[turn, p])
+
+    def soften(n, buf, p, mask):
         turn = sched[0, n]
-        inside = inside_window(window[turn, 0:1], window[turn, 1:2], sched[1, n], rows)
-        for p in pairs:
-            lse, delta = stat[turn, p : p + 1], stat[turn, 4 + p : 5 + p]
-            prob = jnp.where(inside, jnp.exp(score_buf[buf, p] - lse), 0.0)
-            prob_buf[buf, p] = prob.astype(BF16)
-            score_grad_buf[buf, p] = (prob * (prob_grad_buf[buf, p] - delta)).astype(BF16)
-
-    def mix(n, buf):
+        lse, delta = stat[turn, p : p + 1], stat[turn, 4 + p : 5 + p]
+        prob = jnp.where(mask, jnp.exp(score_buf[buf, p] - lse), 0.0)
+        prob_buf[buf, p] = prob.astype(BF16)
+        score_grad_buf[buf, p] = (prob * (prob_grad_buf[buf, p] - delta)).astype(BF16)
+
+    def mix(n, buf, p):
         turn, keys = sched[0, n], key_rows(sched[1, n], rows)
-        for p in pairs:
-            dv_acc[feat[p], keys] += mm_nt(do_diag[turn, p], prob_buf[buf, p])
-            dk_acc[feat[p], keys] += mm_nt(q_diag[turn, p], score_grad_buf[buf, p])
-            dq_acc[turn, p] += diagonal_blocks(mm(kt_ref[feat[p], keys], score_grad_buf[buf, p]))
+        dv_acc[feat[p], keys] += mm_nt(do_diag[turn, p], prob_buf[buf, p])
+        dk_acc[feat[p], keys] += mm_nt(q_diag[turn, p], score_grad_buf[buf, p])
+        dq_acc[turn, p] += diagonal_blocks(mm(kt_ref[feat[p], keys], score_grad_buf[buf, p]))
 
     prob_buf[1] = jnp.zeros_like(prob_buf[1])
     score_grad_buf[1] = jnp.zeros_like(score_grad_buf[1])
-    run_pipeline(count, scores, soften, mix)
+    run_pipeline(count, pairs, inside, scores, soften, mix)
 
     def finish(turn, _):
         cols = pl.ds(pl.multiple_of(turn * QB, QB), QB)

time: 273 us -> 271 us (level)
  Pallas kernels: 240 us -> 245 us
  waiting for transfers between devices: 12 us -> 7.07 us
    ppermute x2, waiting for transfers between devices: 9.26 us -> 0.01 us  [local_square(): piles[2 * i + 1] = lax.ppermute(piles[2 * i + 1], 'dp', perm)]
    ppermute x9, waiting for transfers between devices: 2.7 us -> 7.07 us  [local_square(): lax.ppermute(a, 'mp', [(i, i ^ shift) for i in range(groups)])]
    pallas_call x1, Pallas kernels: 36 us -> 39.8 us  [attend_back(): pl.pallas_call(attend_back_kernel, in_specs=[SMEM, VMEM] + [ANY] * 3 + [V...]
    ppermute x2, starting transfers between devices: 6.22 us -> 3.39 us  [local_square(): piles[2 * i + 1] = lax.ppermute(piles[2 * i + 1], 'dp', perm)]
  transfers between devices with their start and end apart: 11 -> 11, of which waited for: 3 -> 1; matrix products, arithmetic and copies ran while one was open for 0% -> 0% of each run, Pallas kernels for 28% -> 30%
where the time goes in v4:
time: 271 us; the launch traced here: 270 us
  Pallas kernels  245 us (90%)
  starting transfers between devices  15.1 us (6%)
  waiting for transfers between devices  7.07 us (3%)
    pallas_call x1, Pallas kernels, ffn(): pl.pallas_call(functools.partial(ffn_kernel, packs), in_specs=[SMEM] + [A...  102 us
    pallas_call x1, Pallas kernels, last(): pl.pallas_call(functools.partial(last_kernel, packs), in_specs=[ANY] * 9...  56.7 us
    pallas_call x1, Pallas kernels, attend_back(): pl.pallas_call(attend_back_kernel, in_specs=[SMEM, VMEM] + [ANY] * 3 + [V...  39.8 us
    pallas_call x2, Pallas kernels, attend(): pl.pallas_call(functools.partial(attend_kernel, begin, steps), in_specs=[...  29.8 us
    pallas_call x1, Pallas kernels, project(): pl.pallas_call(qkv_kernel, grid=(rows // block,), in_specs=[SMEM, by_row(...  11.8 us
    ppermute x9, starting transfers between devices, local_square(): lax.ppermute(a, 'mp', [(i, i ^ shift) for i in range(groups)])  11.7 us
    ppermute x9, waiting for transfers between devices, local_square(): lax.ppermute(a, 'mp', [(i, i ^ shift) for i in range(groups)])  7.07 us
  transfers between devices with their start and end apart: 11, of which 1 were waited for; matrix products, arithmetic and copies ran while one was open for 0% of the time, Pallas kernels for 30%

profile of v4, /device:TPU:0, one launch (start us, length us, event | category | flops | bytes accessed | tf_op | source)
XLA Modules:
  0.0 270.1 jit_solution(2466876917195922018)
XLA Ops:
  0.6 3.0 %collective-permute-start.4 = (bf16[256,1024]{1,0:T(8,128)(2,1)}, bf16[256,1024]{1,0:T(8,128)(2,1)S(1)}, u32[]{:S(2)}, u32[]{:S(2)}) collective-permute-start(bf16[256,1024]{1,0:T(8,128)(2,1)} %wo0), channel_id=1, source_target_pairs={{0,2},{1,3},{2,0},{3,1},{4,6},{5,7},{6,4},{7,5},{8,10},{9,11},{10,... | collective-permute-start | bytes 1572872 | tf_op jit(solution)/shard_map/ppermute | solution.py:1447
  3.7 1.5 collective-permute-start.3
  5.2 0.1 collective-permute-start.5
  5.2 11.8 %qkv.1 = (bf16[2560,1024]{1,0:T(8,128)(2,1)}, bf16[2560,256]{1,0:T(8,128)(2,1)}, bf16[2560,256]{1,0:T(8,128)(2,1)}, bf16[256,2560]{1,0:T(8,128)(2,1)}, bf16[256,...) custom-call(s32[1,9]{1,0:T(1,128)} %len_ref.9, ...), custom_call_target="tpu_custom_call" | custom-call | flops 4026531840 | bytes 20971520 | tf_op jit(solution)/shard_map/qkv/pallas_call | solution.py:128
  17.1 13.2 %attend.2 = (bf16[4,2,128,256]{3,2,1,0:T(8,128)(2,1)}, bf16[4,1,128,256]{3,2,1,0:T(8,128)(2,1)}, bf16[256,2560]{1,0:T(8,128)(2,1)}, f32[20,2,256]{2,1,0:T(2,128)}) custom-call(s32[1,9]{1,0:T(1,128)} %len_ref.9, bf16[256,2560]{1,0:T(8,128)(2,1)} %get-tuple-element.78.qt_ref, bf16[2560,256]{1,0:T(8,128)(2,1)} %get-tuple-element.72.k_hbm, ...), custom_call_target="tpu_custom_call" | custom-call | flops 5368709120 | bytes 6553600 | tf_op jit(solution)/shard_map/attend/pallas_call | solution.py:325
  30.3 2.0 collective-permute-start.1
  32.3 1.5 collective-permute-start
  33.8 0.0 collective-permute-done.4.wo2
  33.8 0.1 collective-permute-start.2
  33.8 0.0 collective-permute-done.3.wo1
  33.8 0.0 collective-permute-done.5.wo3
  33.8 16.6 %attend.3 = (bf16[4,3,128,256]{3,2,1,0:T(8,128)(2,1)}, bf16[256,2560]{1,0:T(8,128)(2,1)}, f32[20,2,256]{2,1,0:T(2,128)}) custom-call(s32[1,9]{1,0:T(1,128)} %len_ref.9, bf16[256,2560]{1,0:T(8,128)(2,1)} %get-tuple-element.78.qt_ref, bf16[2560,256]{1,0:T(8,128)(2,1)} %get-tuple-element.72.k_hbm, bf16[256,2560]{1,0:T(8,128)(2,1)} %get-tuple-element.75.vt_hbm, ...), custom_call_target="tpu_custom_call" | custom-call | flops 8053063680 | bytes 6553600 | tf_op jit(solution)/shard_map/attend/pallas_call | solution.py:325
  50.5 0.0 collective-permute-done.2.early3
  50.5 0.0 collective-permute-done.1.early2
  50.5 0.0 collective-permute-done.early1
  50.5 0.7 copy-done.4
  51.2 102.3 %ffn.1 = (f32[5,128,1024]{2,1,0:T(8,128)}, f32[5,128,1024]{2,1,0:T(8,128)}, f32[2,1024]{1,0:T(2,128)}, bf16[4,5,128,256]{3,2,1,0:T(8,128)(2,1)}, bf16[4,512,1024...) custom-call(s32[1,9]{1,0:T(1,128)} %len_ref.9, ...), custom_call_target="tpu_custom_call" | custom-call | flops 53687091200 | bytes 36700160 | tf_op jit(solution)/shard_map/ffn/pallas_call | solution.py:1024
  153.5 0.4 collective-permute-start.6
  153.9 1.7 collective-permute-start.7
  155.6 1.0 collective-permute-start.9
  156.7 2.3 collective-permute-start.10
  159.0 1.5 collective-permute-start.8
  160.5 39.8 %attend_back.1 = (bf16[2560,768]{1,0:T(8,128)(2,1)}, bf16[768,2560]{1,0:T(8,128)(2,1)}) custom-call(s32[1,9]{1,0:T(1,128)} %len_ref.9, bf16[256,2560]{1,0:T(8,128)(2,1)} %get-tuple-element.78.qt_ref, bf16[2560,256]{1,0:T(8,128)(2,1)} %get-tuple-element.72.k_hbm, bf16[256,2560]{1,0:T(8,128)(2,1)} %get-tuple-element.73.kt_hbm, ...), custom_call_target="tpu_custom_call" | custom-call | flops 16777216000 | bytes 18350080 | tf_op jit(solution)/shard_map/attend_back/pallas_call | solution.py:462
  200.2 0.0 collective-permute-done.6.rest_1_
  200.3 7.0 %collective-permute-done.7.rest_2_ = bf16[4,128,1024]{2,1,0:T(8,128)(2,1)} collective-permute-done((bf16[4,128,1024]{2,1,0:T(8,128)(2,1)}, bf16[4,128,1024]{2,1,0:T(8,128)(2,1)}, u32[]{:S(2)}, u32[]{:S(2)}) %collective-permute-start.7) | collective-permute-done | bytes 1048608 | tf_op jit(solution)/shard_map/ppermute | solution.py:1447
  207.3 0.0 collective-permute-done.9.rest_6_
  207.3 0.0 collective-permute-done.10.rest_8_
  207.3 0.0 collective-permute-done.8.rest_3_
  207.3 0.0 copy-start
  207.3 1.0 copy-done
  208.4 56.7 %last.1 = (bf16[5,128,1024]{2,1,0:T(8,128)(2,1)}, bf16[5,128,1024]{2,1,0:T(8,128)(2,1)}, f32[128,256]{1,0:T(8,128)}, f32[128,256]{1,0:T(8,128)}, f32[128,256]{1,...) custom-call(bf16[4,5,128,768]{3,2,1,0:T(8,128)(2,1)} %bitcast.12, ...), custom_call_target="tpu_custom_call" | custom-call | flops 8053063680 | bytes 52428800 | tf_op jit(solution)/shard_map/last/pallas_call | solution.py:1336
  265.1 4.8 %hand_out.1 = (bf16[5,128,1024]{2,1,0:T(8,128)(2,1)}, bf16[5,128,1024]{2,1,0:T(8,128)(2,1)}, f32[128,256]{1,0:T(8,128)}, f32[128,256]{1,0:T(8,128)}, f32[128,256...) custom-call(bf16[5,128,1024]{2,1,0:T(8,128)(2,1)} %get-tuple-element, ...), custom_call_target="tpu_custom_call" | custom-call | tf_op jit(solution)/shard_map/hand_out/pallas_call | solution.py:1427
  (7 shorter events, 0.0 us)
Async XLA Ops:
  0.6 33.1 %collective-permute-start.4 = (bf16[256,1024]{1,0:T(8,128)(2,1)}, bf16[256,1024]{1,0:T(8,128)(2,1)S(1)}, u32[]{:S(2)}, u32[]{:S(2)}) collective-permute-start(bf16[256,1024]{1,0:T(8,128)(2,1)} %wo0), channel_id=1, source_target_pairs={{0,2},{1,3},{2,0},{3,1},{4,6},{5,7},{6,4},{7,5},{8,10},{9,11},{10,... | collective-permute-start | bytes 1572872 | tf_op jit(solution)/shard_map/ppermute | solution.py:1447
  3.7 30.2 %collective-permute-start.3 = (bf16[256,1024]{1,0:T(8,128)(2,1)}, bf16[256,1024]{1,0:T(8,128)(2,1)S(1)}, u32[]{:S(2)}, u32[]{:S(2)}) collective-permute-start(bf16[256,1024]{1,0:T(8,128)(2,1)} %wo0), channel_id=1, source_target_pairs={{0,1},{1,0},{2,3},{3,2},{4,5},{5,4},{6,7},{7,6},{8,9},{9,8},{10,11... | collective-permute-start | bytes 1572872 | tf_op jit(solution)/shard_map/ppermute | solution.py:1447
  5.2 28.7 %collective-permute-start.5 = (bf16[256,1024]{1,0:T(8,128)(2,1)}, bf16[256,1024]{1,0:T(8,128)(2,1)S(1)}, u32[]{:S(2)}, u32[]{:S(2)}) collective-permute-start(bf16[256,1024]{1,0:T(8,128)(2,1)} %wo0), channel_id=1, source_target_pairs={{0,3},{1,2},{2,1},{3,0},{4,7},{5,6},{6,5},{7,4},{8,11},{9,10},{10,... | collective-permute-start | bytes 1572872 | tf_op jit(solution)/shard_map/ppermute | solution.py:1447
  30.3 20.3 %collective-permute-start.1 = (bf16[4,2,128,256]{3,2,1,0:T(8,128)(2,1)}, bf16[4,2,128,256]{3,2,1,0:T(8,128)(2,1)}, u32[]{:S(2)}, u32[]{:S(2)}) collective-permute-start(bf16[4,2,128,256]{3,2,1,0:T(8,128)(2,1)} %get-tuple-element.76.early0), channel_id=1, source_target_pairs={{0,2},{1,3},{2,0},{3,1},{4,6},{5,7},{6,4},{7,5},{8,10},{9,11},{10,... | collective-permute-start | bytes 1572872 | tf_op jit(solution)/shard_map/ppermute | solution.py:1447
  32.3 18.3 %collective-permute-start = (bf16[4,2,128,256]{3,2,1,0:T(8,128)(2,1)}, bf16[4,2,128,256]{3,2,1,0:T(8,128)(2,1)}, u32[]{:S(2)}, u32[]{:S(2)}) collective-permute-start(bf16[4,2,128,256]{3,2,1,0:T(8,128)(2,1)} %get-tuple-element.76.early0), channel_id=1, source_target_pairs={{0,1},{1,0},{2,3},{3,2},{4,5},{5,4},{6,7},{7,6},{8,9},{9,8},{10,11... | collective-permute-start | bytes 1572872 | tf_op jit(solution)/shard_map/ppermute | solution.py:1447
  33.8 16.7 %copy-start.1 = (bf16[256,1024]{1,0:T(8,128)(2,1)}, bf16[256,1024]{1,0:T(8,128)(2,1)S(1)}, u32[]{:S(2)}) copy-start(bf16[256,1024]{1,0:T(8,128)(2,1)S(1)} %collective-permute-done.4.wo2) | copy-start | bytes 1572868
  33.8 16.7 %collective-permute-start.2 = (bf16[4,1,128,256]{3,2,1,0:T(8,128)(2,1)}, bf16[4,1,128,256]{3,2,1,0:T(8,128)(2,1)S(1)}, u32[]{:S(2)}, u32[]{:S(2)}) collective-permute-start(bf16[4,1,128,256]{3,2,1,0:T(8,128)(2,1)} %get-tuple-element.77), channel_id=1, source_target_pairs={{0,3},{1,2},{2,1},{3,0},{4,7},{5,6},{6,5},{7,4},{8,11},{9,10},{10,... | collective-permute-start | bytes 786440 | tf_op jit(solution)/shard_map/ppermute | solution.py:1447
  33.8 16.7 %copy-start.2 = (bf16[256,1024]{1,0:T(8,128)(2,1)}, bf16[256,1024]{1,0:T(8,128)(2,1)S(1)}, u32[]{:S(2)}) copy-start(bf16[256,1024]{1,0:T(8,128)(2,1)S(1)} %collective-permute-done.3.wo1) | copy-start | bytes 1572868
  33.8 16.7 %copy-start.3 = (bf16[256,1024]{1,0:T(8,128)(2,1)}, bf16[256,1024]{1,0:T(8,128)(2,1)S(1)}, u32[]{:S(2)}) copy-start(bf16[256,1024]{1,0:T(8,128)(2,1)S(1)} %collective-permute-done.5.wo3) | copy-start | bytes 1572868
  50.5 0.7 copy-start.4
  153.5 46.8 %collective-permute-start.6 = (bf16[4,128,1024]{2,1,0:T(8,128)(2,1)}, bf16[4,128,1024]{2,1,0:T(8,128)(2,1)}, u32[]{:S(2)}, u32[]{:S(2)}) collective-permute-start(bf16[4,128,1024]{2,1,0:T(8,128)(2,1)} %get-tuple-element.98), channel_id=1, source_target_pairs={{0,1},{1,0},{2,3},{3,2},{4,5},{5,4},{6,7},{7,6},{8,9},{9,8},{10,11... | collective-permute-start | bytes 3145736 | tf_op jit(solution)/shard_map/ppermute | solution.py:1447
  153.9 53.4 %collective-permute-start.7 = (bf16[4,128,1024]{2,1,0:T(8,128)(2,1)}, bf16[4,128,1024]{2,1,0:T(8,128)(2,1)}, u32[]{:S(2)}, u32[]{:S(2)}) collective-permute-start(bf16[4,128,1024]{2,1,0:T(8,128)(2,1)} %get-tuple-element.99), channel_id=1, source_target_pairs={{0,2},{1,3},{2,0},{3,1},{4,6},{5,7},{6,4},{7,5},{8,10},{9,11},{10,... | collective-permute-start | bytes 3145736 | tf_op jit(solution)/shard_map/ppermute | solution.py:1447
  155.6 51.7 %collective-permute-start.9 = (bf16[2,2,128,1024]{3,2,1,0:T(8,128)(2,1)}, bf16[2,2,128,1024]{3,2,1,0:T(8,128)(2,1)}, u32[]{:S(2)}, u32[]{:S(2)}) collective-permute-start(bf16[2,2,128,1024]{3,2,1,0:T(8,128)(2,1)} %get-tuple-element.103), channel_id=1, source_target_pairs={{0,8},{4,12},{8,0},{12,4},{16,24},{20,28},{24,16},{28,20},{1,9},{5... | collective-permute-start | bytes 3145736 | tf_op jit(solution)/shard_map/ppermute | solution.py:1463
  156.7 50.7 %collective-permute-start.10 = (bf16[2,2,128,1024]{3,2,1,0:T(8,128)(2,1)}, bf16[2,2,128,1024]{3,2,1,0:T(8,128)(2,1)}, u32[]{:S(2)}, u32[]{:S(2)}) collective-permute-start(bf16[2,2,128,1024]{3,2,1,0:T(8,128)(2,1)} %get-tuple-element.105), channel_id=1, source_target_pairs={{0,16},{4,20},{8,24},{12,28},{16,0},{20,4},{24,8},{28,12},{1,17},{... | collective-permute-start | bytes 3145736 | tf_op jit(solution)/shard_map/ppermute | solution.py:1463
  159.0 48.3 %collective-permute-start.8 = (bf16[5,128,1024]{2,1,0:T(8,128)(2,1)}, bf16[5,128,1024]{2,1,0:T(8,128)(2,1)S(1)}, u32[]{:S(2)}, u32[]{:S(2)}) collective-permute-start(bf16[5,128,1024]{2,1,0:T(8,128)(2,1)} %get-tuple-element.100), channel_id=1, source_target_pairs={{0,3},{1,2},{2,1},{3,0},{4,7},{5,6},{6,5},{7,4},{8,11},{9,10},{10,... | collective-permute-start | bytes 3932168 | tf_op jit(solution)/shard_map/ppermute | solution.py:1447
  207.3 1.1 copy-start

commit v5 on v4

--- a/solution.py
+++ b/solution.py
@@ -25,6 +25,7 @@
 MESH = pl.DeviceIdType.MESH
 STEPS = 5
 EARLY = 2
+MIDDLE = 2
 TILE = 256
 VMEM_CAP = 62 << 20
 F32 = jnp.float32
@@ -722,6 +723,12 @@
         for copy in pile_copies(kind):
             copy.start()
 
+    def put_middle_rows():
+        return [
+            remote(stage.at[MIDDLE % 2, target], rows_hbm.at[2 + i], sems, 15 + i, 0, target)
+            for i, target in enumerate((x, y, d))
+        ]
+
     def put_rows():
         slot = (steps - 1) % 2
         return [
@@ -876,21 +883,30 @@
             sum_kind(1)
             sum_kind(2)
 
-        def stage_copies(at, final):
+        def stage_copies(at, to_diagonal, to_neighbours):
             slot = lax.rem(at, 2)
-            places = [(me, down0_hbm), (d, down3_hbm)]
-            if not final:
-                places += [(x, down1_hbm), (y, down2_hbm)]
+            places = [(me, down0_hbm.at[at])]
+            if to_diagonal:
+                places.append((d, down3_hbm.at[at - at // 3]))
+            if to_neighbours:
+                places += [(x, down1_hbm.at[at - at // 3]), (y, down2_hbm.at[at - at // 3])]
             return [
-                pltpu.make_async_copy(stage.at[slot, who], out.at[at], stage_sem.at[i, slot])
+                pltpu.make_async_copy(stage.at[slot, who], out, stage_sem.at[i, slot])
                 for i, (who, out) in enumerate(places)
             ]
 
         @pl.when(step < steps)
         def _():
-            @pl.when(step >= 2)
+            @pl.when(step == MIDDLE + 2)
             def _():
-                for copy in stage_copies(step - 2, False):
+                for copy in stage_copies(step - 2, False, False):
+                    copy.wait()
+                for copy in put_middle_rows():
+                    copy.wait_send()
+
+            @pl.when((step >= 2) & (step != MIDDLE + 2))
+            def _():
+                for copy in stage_copies(step - 2, True, True):
                     copy.wait()
 
             def some_output(turn, _):
@@ -904,14 +920,19 @@
 
             lax.fori_loop(0, owners // some, some_output, 0)
 
-            @pl.when(step < steps - 1)
+            @pl.when(step == MIDDLE)
             def _():
-                for copy in stage_copies(step, False):
+                for copy in stage_copies(step, False, False) + put_middle_rows():
+                    copy.start()
+
+            @pl.when((step != MIDDLE) & (step < steps - 1))
+            def _():
+                for copy in stage_copies(step, True, True):
                     copy.start()
 
             @pl.when(step == steps - 1)
             def _():
-                for copy in stage_copies(step, True):
+                for copy in stage_copies(step, True, False):
                     copy.start()
 
             def some_grads(turn, _):
@@ -926,7 +947,7 @@
 
         @pl.when(step == steps)
         def _():
-            for copy in stage_copies(steps - 2, False) + stage_copies(steps - 1, True):
+            for copy in stage_copies(steps - 2, True, True) + stage_copies(steps - 1, True, False):
                 copy.wait()
 
         @pl.when(step >= 2)
@@ -998,6 +1019,8 @@
 
     for copy in put_rows():
         copy.wait()
+    for copy in put_middle_rows():
+        copy.wait_recv()
 
     def finish(step, _):
         for copy in put_do(step) + keep_rows(step):
@@ -1034,7 +1057,7 @@
         ]
         + [
             jax.ShapeDtypeStruct((taken, block, width), BF16)
-            for taken in (steps, steps - 1, steps - 1, steps, 2)
+            for taken in (steps, steps - 2, steps - 2, steps - 1, 5)
         ]
         + [jax.ShapeDtypeStruct((2, 2, width // packs, width), BF16)] * len(PILES),
         scratch_shapes=[
@@ -1073,8 +1096,8 @@
             dma((2, chips)),
             dma((4,)),
             dma((4,)),
-            dma((15, steps)),
-            dma((15, steps)),
+            dma((18, steps)),
+            dma((18, steps)),
         ],
         compiler_params=pltpu.CompilerParams(
             collective_id=0, has_side_effects=True, vmem_limit_bytes=VMEM_CAP
@@ -1119,8 +1142,14 @@
     later = [(grad_t_hbm, grad_t), (a1_hbm, a1)]
     later += [(piles[i], pile.at[i]) for i in range(len(PILES))]
     later += [(h1_hbm, h1)]
-    later += [(downs[i], down.at[i, pl.ds(0, downs[i].shape[0])]) for i in range(4)]
-    later += [(downs[4], down.at[pl.ds(1, 2), steps - 1])]
+    later += [(downs[0], down.at[0])]
+    after = MIDDLE + 1
+    for i in range(1, 4):
+        left = downs[i].shape[0] - MIDDLE
+        later += [(downs[i].at[pl.ds(0, MIDDLE)], down.at[i, pl.ds(0, MIDDLE)])]
+        later += [(downs[i].at[pl.ds(MIDDLE, left)], down.at[i, pl.ds(after, left)])]
+    later += [(downs[4].at[pl.ds(0, 2)], down.at[pl.ds(1, 2), steps - 1])]
+    later += [(downs[4].at[pl.ds(2, 3)], down.at[pl.ds(1, 3), MIDDLE])]
     later = [pltpu.make_async_copy(a, b, load_sem.at[i]) for i, (a, b) in enumerate(later)]
 
     def to_core():
@@ -1373,7 +1402,7 @@
             pltpu.VMEM((owners - 1, 8, share), F32),
             dma((steps,)),
             dma((steps,)),
-            dma((8 + len(piles),)),
+            dma((12 + len(piles),)),
             dma,
             dma,
             dma((chips - 1,)),

time: 271 us -> 276 us (1.018)
  Pallas kernels: 245 us -> 253 us
    pallas_call x1, Pallas kernels: 102 us -> 114 us  [ffn(): pl.pallas_call(functools.partial(ffn_kernel, packs), in_specs=[SMEM] + [A...]
    ppermute x9, waiting for transfers between devices: 7.07 us -> 0.02 us  [local_square(): lax.ppermute(a, 'mp', [(i, i ^ shift) for i in range(groups)])]
    ppermute x2, waiting for transfers between devices: 0.01 us -> 5.87 us  [local_square(): piles[2 * i + 1] = lax.ppermute(piles[2 * i + 1], 'dp', perm)]
    pallas_call x1, Pallas kernels: 56.7 us -> 52.5 us  [last(): pl.pallas_call(functools.partial(last_kernel, packs), in_specs=[ANY] * 9...]
  transfers between devices with their start and end apart: 11 -> 11, of which waited for: 1 -> 2; matrix products, arithmetic and copies ran while one was open for 0% -> 0% of each run, Pallas kernels for 30% -> 30%
where the time goes in v5:
time: 276 us
  Pallas kernels  253 us (92%)
  starting transfers between devices  16.1 us (6%)
  waiting for transfers between devices  5.89 us (2%)
    pallas_call x1, Pallas kernels, ffn(): pl.pallas_call(functools.partial(ffn_kernel, packs), in_specs=[SMEM] + [A...  114 us
    pallas_call x1, Pallas kernels, last(): pl.pallas_call(functools.partial(last_kernel, packs), in_specs=[ANY] * 9...  52.5 us
    pallas_call x1, Pallas kernels, attend_back(): pl.pallas_call(attend_back_kernel, in_specs=[SMEM, VMEM] + [ANY] * 3 + [V...  40.1 us
    pallas_call x2, Pallas kernels, attend(): pl.pallas_call(functools.partial(attend_kernel, begin, steps), in_specs=[...  30 us
    pallas_call x1, Pallas kernels, project(): pl.pallas_call(qkv_kernel, grid=(rows // block,), in_specs=[SMEM, by_row(...  11.8 us
    ppermute x9, starting transfers between devices, local_square(): lax.ppermute(a, 'mp', [(i, i ^ shift) for i in range(groups)])  11.7 us
    ppermute x2, waiting for transfers between devices, local_square(): piles[2 * i + 1] = lax.ppermute(piles[2 * i + 1], 'dp', perm)  5.87 us
  transfers between devices with their start and end apart: 11, of which 2 were waited for; matrix products, arithmetic and copies ran while one was open for 0% of the time, Pallas kernels for 30%

profile of v5, /device:TPU:0, one launch (start us, length us, event | category | flops | bytes accessed | tf_op | source)
XLA Modules:
  0.0 276.4 jit_solution(16380116865726532102)
XLA Ops:
  0.6 3.0 %collective-permute-start.4 = (bf16[256,1024]{1,0:T(8,128)(2,1)}, bf16[256,1024]{1,0:T(8,128)(2,1)S(1)}, u32[]{:S(2)}, u32[]{:S(2)}) collective-permute-start(bf16[256,1024]{1,0:T(8,128)(2,1)} %wo0), channel_id=1, source_target_pairs={{0,2},{1,3},{2,0},{3,1},{4,6},{5,7},{6,4},{7,5},{8,10},{9,11},{10,... | collective-permute-start | bytes 1572872 | tf_op jit(solution)/shard_map/ppermute | solution.py:1476
  3.7 1.5 collective-permute-start.3
  5.2 0.1 collective-permute-start.5
  5.2 11.8 %qkv.1 = (bf16[2560,1024]{1,0:T(8,128)(2,1)}, bf16[2560,256]{1,0:T(8,128)(2,1)}, bf16[2560,256]{1,0:T(8,128)(2,1)}, bf16[256,2560]{1,0:T(8,128)(2,1)}, bf16[256,...) custom-call(s32[1,9]{1,0:T(1,128)} %len_ref.9, ...), custom_call_target="tpu_custom_call" | custom-call | flops 4026531840 | bytes 20971520 | tf_op jit(solution)/shard_map/qkv/pallas_call | solution.py:129
  17.0 13.2 %attend.2 = (bf16[4,2,128,256]{3,2,1,0:T(8,128)(2,1)}, bf16[4,1,128,256]{3,2,1,0:T(8,128)(2,1)}, bf16[256,2560]{1,0:T(8,128)(2,1)}, f32[20,2,256]{2,1,0:T(2,128)}) custom-call(s32[1,9]{1,0:T(1,128)} %len_ref.9, bf16[256,2560]{1,0:T(8,128)(2,1)} %get-tuple-element.78.qt_ref, bf16[2560,256]{1,0:T(8,128)(2,1)} %get-tuple-element.72.k_hbm, ...), custom_call_target="tpu_custom_call" | custom-call | flops 5368709120 | bytes 6553600 | tf_op jit(solution)/shard_map/attend/pallas_call | solution.py:326
  30.3 2.0 collective-permute-start.1
  32.3 1.5 collective-permute-start
  33.8 0.0 collective-permute-done.4.wo2
  33.8 0.1 collective-permute-start.2
  33.8 0.0 collective-permute-done.3.wo1
  33.8 0.0 collective-permute-done.5.wo3
  33.9 16.7 %attend.3 = (bf16[4,3,128,256]{3,2,1,0:T(8,128)(2,1)}, bf16[256,2560]{1,0:T(8,128)(2,1)}, f32[20,2,256]{2,1,0:T(2,128)}) custom-call(s32[1,9]{1,0:T(1,128)} %len_ref.9, bf16[256,2560]{1,0:T(8,128)(2,1)} %get-tuple-element.78.qt_ref, bf16[2560,256]{1,0:T(8,128)(2,1)} %get-tuple-element.72.k_hbm, bf16[256,2560]{1,0:T(8,128)(2,1)} %get-tuple-element.75.vt_hbm, ...), custom_call_target="tpu_custom_call" | custom-call | flops 8053063680 | bytes 6553600 | tf_op jit(solution)/shard_map/attend/pallas_call | solution.py:326
  50.6 0.0 collective-permute-done.2.early3
  50.6 0.0 collective-permute-done.1.early2
  50.7 0.0 collective-permute-done.early1
  50.7 0.7 copy-done.5
  51.3 113.5 %ffn.1 = (f32[5,128,1024]{2,1,0:T(8,128)}, f32[5,128,1024]{2,1,0:T(8,128)}, f32[2,1024]{1,0:T(2,128)}, bf16[4,5,128,256]{3,2,1,0:T(8,128)(2,1)}, bf16[4,512,1024...) custom-call(s32[1,9]{1,0:T(1,128)} %len_ref.9, ...), custom_call_target="tpu_custom_call" | custom-call | flops 53687091200 | bytes 36700160 | tf_op jit(solution)/shard_map/ffn/pallas_call | solution.py:1047
  164.9 0.2 collective-permute-start.6
  165.1 1.7 collective-permute-start.7
  166.9 1.6 collective-permute-start.8
  168.4 2.9 %collective-permute-start.9 = (bf16[2,2,128,1024]{3,2,1,0:T(8,128)(2,1)}, bf16[2,2,128,1024]{3,2,1,0:T(8,128)(2,1)}, u32[]{:S(2)}, u32[]{:S(2)}) collective-permute-start(bf16[2,2,128,1024]{3,2,1,0:T(8,128)(2,1)} %get-tuple-element.103), channel_id=1, source_target_pairs={{0,8},{4,12},{8,0},{12,4},{16,24},{20,28},{24,16},{28,20},{1,9},{5... | collective-permute-start | bytes 3145736 | tf_op jit(solution)/shard_map/ppermute | solution.py:1492
  171.3 1.6 collective-permute-start.10
  172.9 40.1 %attend_back.1 = (bf16[2560,768]{1,0:T(8,128)(2,1)}, bf16[768,2560]{1,0:T(8,128)(2,1)}) custom-call(s32[1,9]{1,0:T(1,128)} %len_ref.9, bf16[256,2560]{1,0:T(8,128)(2,1)} %get-tuple-element.78.qt_ref, bf16[2560,256]{1,0:T(8,128)(2,1)} %get-tuple-element.72.k_hbm, bf16[256,2560]{1,0:T(8,128)(2,1)} %get-tuple-element.73.kt_hbm, ...), custom_call_target="tpu_custom_call" | custom-call | flops 16777216000 | bytes 18350080 | tf_op jit(solution)/shard_map/attend_back/pallas_call | solution.py:463
  213.0 0.0 collective-permute-done.6.rest_1_
  213.0 0.0 copy-start.1
  213.0 0.0 collective-permute-done.7.rest_2_
  213.0 0.0 collective-permute-done.8.rest_3_
  213.0 0.0 copy-start
  213.0 2.2 collective-permute-done.9.rest_6_
  215.2 3.7 %collective-permute-done.10.rest_8_ = bf16[2,2,128,1024]{3,2,1,0:T(8,128)(2,1)} collective-permute-done((bf16[2,2,128,1024]{3,2,1,0:T(8,128)(2,1)}, bf16[2,2,128,1024]{3,2,1,0:T(8,128)(2,1)}, u32[]{:S(2)}, u32[]{:S(2)}) %collective-permute-start.10) | collective-permute-done | bytes 1048608 | tf_op jit(solution)/shard_map/ppermute | solution.py:1492
  218.9 52.5 %last.1 = (bf16[5,128,1024]{2,1,0:T(8,128)(2,1)}, bf16[5,128,1024]{2,1,0:T(8,128)(2,1)}, f32[128,256]{1,0:T(8,128)}, f32[128,256]{1,0:T(8,128)}, f32[128,256]{1,...) custom-call(bf16[4,5,128,768]{3,2,1,0:T(8,128)(2,1)} %bitcast.12, ...), custom_call_target="tpu_custom_call" | custom-call | flops 8053063680 | bytes 52428800 | tf_op jit(solution)/shard_map/last/pallas_call | solution.py:1365
  271.4 4.8 %hand_out.1 = (bf16[5,128,1024]{2,1,0:T(8,128)(2,1)}, bf16[5,128,1024]{2,1,0:T(8,128)(2,1)}, f32[128,256]{1,0:T(8,128)}, f32[128,256]{1,0:T(8,128)}, f32[128,256...) custom-call(bf16[5,128,1024]{2,1,0:T(8,128)(2,1)} %get-tuple-element, ...), custom_call_target="tpu_custom_call" | custom-call | tf_op jit(solution)/shard_map/hand_out/pallas_call | solution.py:1456
  (9 shorter events, 0.0 us)
Async XLA Ops:
  0.6 33.1 %collective-permute-start.4 = (bf16[256,1024]{1,0:T(8,128)(2,1)}, bf16[256,1024]{1,0:T(8,128)(2,1)S(1)}, u32[]{:S(2)}, u32[]{:S(2)}) collective-permute-start(bf16[256,1024]{1,0:T(8,128)(2,1)} %wo0), channel_id=1, source_target_pairs={{0,2},{1,3},{2,0},{3,1},{4,6},{5,7},{6,4},{7,5},{8,10},{9,11},{10,... | collective-permute-start | bytes 1572872 | tf_op jit(solution)/shard_map/ppermute | solution.py:1476
  3.7 30.2 %collective-permute-start.3 = (bf16[256,1024]{1,0:T(8,128)(2,1)}, bf16[256,1024]{1,0:T(8,128)(2,1)S(1)}, u32[]{:S(2)}, u32[]{:S(2)}) collective-permute-start(bf16[256,1024]{1,0:T(8,128)(2,1)} %wo0), channel_id=1, source_target_pairs={{0,1},{1,0},{2,3},{3,2},{4,5},{5,4},{6,7},{7,6},{8,9},{9,8},{10,11... | collective-permute-start | bytes 1572872 | tf_op jit(solution)/shard_map/ppermute | solution.py:1476
  5.2 28.7 %collective-permute-start.5 = (bf16[256,1024]{1,0:T(8,128)(2,1)}, bf16[256,1024]{1,0:T(8,128)(2,1)S(1)}, u32[]{:S(2)}, u32[]{:S(2)}) collective-permute-start(bf16[256,1024]{1,0:T(8,128)(2,1)} %wo0), channel_id=1, source_target_pairs={{0,3},{1,2},{2,1},{3,0},{4,7},{5,6},{6,5},{7,4},{8,11},{9,10},{10,... | collective-permute-start | bytes 1572872 | tf_op jit(solution)/shard_map/ppermute | solution.py:1476
  30.3 20.4 %collective-permute-start.1 = (bf16[4,2,128,256]{3,2,1,0:T(8,128)(2,1)}, bf16[4,2,128,256]{3,2,1,0:T(8,128)(2,1)}, u32[]{:S(2)}, u32[]{:S(2)}) collective-permute-start(bf16[4,2,128,256]{3,2,1,0:T(8,128)(2,1)} %get-tuple-element.76.early0), channel_id=1, source_target_pairs={{0,2},{1,3},{2,0},{3,1},{4,6},{5,7},{6,4},{7,5},{8,10},{9,11},{10,... | collective-permute-start | bytes 1572872 | tf_op jit(solution)/shard_map/ppermute | solution.py:1476
  32.3 18.4 %collective-permute-start = (bf16[4,2,128,256]{3,2,1,0:T(8,128)(2,1)}, bf16[4,2,128,256]{3,2,1,0:T(8,128)(2,1)}, u32[]{:S(2)}, u32[]{:S(2)}) collective-permute-start(bf16[4,2,128,256]{3,2,1,0:T(8,128)(2,1)} %get-tuple-element.76.early0), channel_id=1, source_target_pairs={{0,1},{1,0},{2,3},{3,2},{4,5},{5,4},{6,7},{7,6},{8,9},{9,8},{10,11... | collective-permute-start | bytes 1572872 | tf_op jit(solution)/shard_map/ppermute | solution.py:1476
  33.8 16.8 %copy-start.2 = (bf16[256,1024]{1,0:T(8,128)(2,1)}, bf16[256,1024]{1,0:T(8,128)(2,1)S(1)}, u32[]{:S(2)}) copy-start(bf16[256,1024]{1,0:T(8,128)(2,1)S(1)} %collective-permute-done.4.wo2) | copy-start | bytes 1572868
  33.8 16.8 %collective-permute-start.2 = (bf16[4,1,128,256]{3,2,1,0:T(8,128)(2,1)}, bf16[4,1,128,256]{3,2,1,0:T(8,128)(2,1)S(1)}, u32[]{:S(2)}, u32[]{:S(2)}) collective-permute-start(bf16[4,1,128,256]{3,2,1,0:T(8,128)(2,1)} %get-tuple-element.77), channel_id=1, source_target_pairs={{0,3},{1,2},{2,1},{3,0},{4,7},{5,6},{6,5},{7,4},{8,11},{9,10},{10,... | collective-permute-start | bytes 786440 | tf_op jit(solution)/shard_map/ppermute | solution.py:1476
  33.8 16.8 %copy-start.3 = (bf16[256,1024]{1,0:T(8,128)(2,1)}, bf16[256,1024]{1,0:T(8,128)(2,1)S(1)}, u32[]{:S(2)}) copy-start(bf16[256,1024]{1,0:T(8,128)(2,1)S(1)} %collective-permute-done.3.wo1) | copy-start | bytes 1572868
  33.8 16.8 %copy-start.4 = (bf16[256,1024]{1,0:T(8,128)(2,1)}, bf16[256,1024]{1,0:T(8,128)(2,1)S(1)}, u32[]{:S(2)}) copy-start(bf16[256,1024]{1,0:T(8,128)(2,1)S(1)} %collective-permute-done.5.wo3) | copy-start | bytes 1572868
  50.6 0.7 copy-start.5
  164.9 48.1 %collective-permute-start.6 = (bf16[3,128,1024]{2,1,0:T(8,128)(2,1)}, bf16[3,128,1024]{2,1,0:T(8,128)(2,1)S(1)}, u32[]{:S(2)}, u32[]{:S(2)}) collective-permute-start(bf16[3,128,1024]{2,1,0:T(8,128)(2,1)} %get-tuple-element.98), channel_id=1, source_target_pairs={{0,1},{1,0},{2,3},{3,2},{4,5},{5,4},{6,7},{7,6},{8,9},{9,8},{10,11... | collective-permute-start | bytes 2359304 | tf_op jit(solution)/shard_map/ppermute | solution.py:1476
  165.1 47.9 %collective-permute-start.7 = (bf16[3,128,1024]{2,1,0:T(8,128)(2,1)}, bf16[3,128,1024]{2,1,0:T(8,128)(2,1)}, u32[]{:S(2)}, u32[]{:S(2)}) collective-permute-start(bf16[3,128,1024]{2,1,0:T(8,128)(2,1)} %get-tuple-element.99), channel_id=1, source_target_pairs={{0,2},{1,3},{2,0},{3,1},{4,6},{5,7},{6,4},{7,5},{8,10},{9,11},{10,... | collective-permute-start | bytes 2359304 | tf_op jit(solution)/shard_map/ppermute | solution.py:1476
  166.9 46.1 %collective-permute-start.8 = (bf16[4,128,1024]{2,1,0:T(8,128)(2,1)}, bf16[4,128,1024]{2,1,0:T(8,128)(2,1)S(1)}, u32[]{:S(2)}, u32[]{:S(2)}) collective-permute-start(bf16[4,128,1024]{2,1,0:T(8,128)(2,1)} %get-tuple-element.100), channel_id=1, source_target_pairs={{0,3},{1,2},{2,1},{3,0},{4,7},{5,6},{6,5},{7,4},{8,11},{9,10},{10,... | collective-permute-start | bytes 3145736 | tf_op jit(solution)/shard_map/ppermute | solution.py:1476
  168.4 46.7 %collective-permute-start.9 = (bf16[2,2,128,1024]{3,2,1,0:T(8,128)(2,1)}, bf16[2,2,128,1024]{3,2,1,0:T(8,128)(2,1)}, u32[]{:S(2)}, u32[]{:S(2)}) collective-permute-start(bf16[2,2,128,1024]{3,2,1,0:T(8,128)(2,1)} %get-tuple-element.103), channel_id=1, source_target_pairs={{0,8},{4,12},{8,0},{12,4},{16,24},{20,28},{24,16},{28,20},{1,9},{5... | collective-permute-start | bytes 3145736 | tf_op jit(solution)/shard_map/ppermute | solution.py:1492
  171.3 47.6 %collective-permute-start.10 = (bf16[2,2,128,1024]{3,2,1,0:T(8,128)(2,1)}, bf16[2,2,128,1024]{3,2,1,0:T(8,128)(2,1)}, u32[]{:S(2)}, u32[]{:S(2)}) collective-permute-start(bf16[2,2,128,1024]{3,2,1,0:T(8,128)(2,1)} %get-tuple-element.105), channel_id=1, source_target_pairs={{0,16},{4,20},{8,24},{12,28},{16,0},{20,4},{24,8},{28,12},{1,17},{... | collective-permute-start | bytes 3145736 | tf_op jit(solution)/shard_map/ppermute | solution.py:1492
  213.0 5.9 %copy-start.1 = (bf16[3,128,1024]{2,1,0:T(8,128)(2,1)}, bf16[3,128,1024]{2,1,0:T(8,128)(2,1)S(1)}, u32[]{:S(2)}) copy-start(bf16[3,128,1024]{2,1,0:T(8,128)(2,1)S(1)} %collective-permute-done.6.rest_1_) | copy-start | bytes 2359300
  213.0 5.9 %copy-start = (bf16[4,128,1024]{2,1,0:T(8,128)(2,1)}, bf16[4,128,1024]{2,1,0:T(8,128)(2,1)S(1)}, u32[]{:S(2)}) copy-start(bf16[4,128,1024]{2,1,0:T(8,128)(2,1)S(1)} %collective-permute-done.8.rest_3_) | copy-start | bytes 3145732
